TPU v7x, 32 devices: a whole 2x2x4 slice. The times are simulated.
32 devices in a mesh: wide: 8 (over z, y), narrow: 4 (over x, core).
Axes of the slice: x: 2, y: 2, z: 4, core: 2. Of those that a mesh axis runs over, the one named last changes fastest.
Arguments:
- tokens: bfloat16 [16, 256, 2048], P('wide', 'narrow'), may hold values from -6 to 6
- caption: bfloat16 [16, 128, 4096], P('wide', None, 'narrow'), may hold values from -6 to 6
- token_mask: int32 [16, 256], P('wide', 'narrow'), may hold values 0 or 1
- cotangent: bfloat16 [16, 256, 2048], P('wide', 'narrow'), may hold values from -6 to 6
- gain_self: bfloat16 [2048], replicated, may hold values from 0.5 to 1.5
- gain_cross: bfloat16 [2048], replicated, may hold values from 0.5 to 1.5
- gain_feed: bfloat16 [2048], replicated, may hold values from 0.5 to 1.5
- text_proj: bfloat16 [4096, 2048], P('narrow'), may hold values from -0.09375 to 0.09375
- query_self: bfloat16 [2048, 2048], P(None, 'narrow'), may hold values from -0.25 to 0.25
- key_self: bfloat16 [2048, 2048], P(None, 'narrow'), may hold values from -0.125 to 0.125
- value_self: bfloat16 [2048, 2048], P(None, 'narrow'), may hold values from -0.125 to 0.125
- out_self: bfloat16 [2048, 2048], P('narrow'), may hold values from -0.625 to 0.625
- query_cross: bfloat16 [2048, 2048], P(None, 'narrow'), may hold values from -0.25 to 0.25
- key_cross: bfloat16 [2048, 2048], P(None, 'narrow'), may hold values from -0.125 to 0.125
- value_cross: bfloat16 [2048, 2048], P(None, 'narrow'), may hold values from -0.125 to 0.125
- out_cross: bfloat16 [2048, 2048], P('narrow'), may hold values from -0.625 to 0.625
- up_proj: bfloat16 [2048, 8192], P(None, 'narrow'), may hold values from -0.125 to 0.125
- down_proj: bfloat16 [8192, 2048], P('narrow'), may hold values from -0.09375 to 0.09375
Outputs:
- layer_out: bfloat16 [16, 256, 2048], P('wide', 'narrow')
- grad_tokens: bfloat16 [16, 256, 2048], P('wide', 'narrow')
- grad_caption: bfloat16 [16, 128, 4096], P('wide', None, 'narrow')
- grad_gain_self: float32 [2048], replicated
- grad_gain_cross: float32 [2048], replicated
- grad_gain_feed: float32 [2048], replicated
- grad_text: float32 [4096, 2048], P('narrow', 'wide')
- grad_query_self: float32 [2048, 2048], P('wide', 'narrow')
- grad_key_self: float32 [2048, 2048], P('wide', 'narrow')
- grad_value_self: float32 [2048, 2048], P('wide', 'narrow')
- grad_out_self: float32 [2048, 2048], P('narrow', 'wide')
- grad_query_cross: float32 [2048, 2048], P('wide', 'narrow')
- grad_key_cross: float32 [2048, 2048], P('wide', 'narrow')
- grad_value_cross: float32 [2048, 2048], P('wide', 'narrow')
- grad_out_cross: float32 [2048, 2048], P('narrow', 'wide')
- grad_up: float32 [2048, 8192], P('wide', 'narrow')
- grad_down: float32 [8192, 2048], P('narrow', 'wide')
All inputs are finite; a program needn't handle non-finite values. No bound on the sum of `token_mask` on one device may be relied on, other than what follows from the above.
Results may differ from a plain program's by a relative error of at most 0.03.
The roundings to bfloat16 on the way count: a program that leaves them out, or rounds other values in their place, can miss the bound.
Values may be sent and summed in bfloat16 or wider, within the bound.
A program may use at most 640 MiB of HBM per device.

v0:
```python
import math

import jax
import jax.numpy as jnp
from jax import lax
from jax.sharding import PartitionSpec as P

HEAD = 128


def normalize(rows):
    centre = jnp.mean(rows, axis=-1, keepdims=True)
    centred = rows - centre
    variance = jnp.mean(centred * centred, axis=-1, keepdims=True)
    inv_std = lax.rsqrt(variance + 1e-05)
    return (centred * inv_std, inv_std)


def norm_back(d_normed, normed, inv_std):
    inner = d_normed - jnp.mean(d_normed, axis=-1, keepdims=True)
    inner = inner - normed * jnp.mean(d_normed * normed, axis=-1, keepdims=True)
    return inv_std * inner


def contract(left, right):
    return lax.dot_general(
        left, right, (((0,), (0,)), ((), ())), preferred_element_type=jnp.float32
    )


def against(left, right):
    return lax.dot_general(
        left, right, (((1,), (1,)), ((), ())), preferred_element_type=jnp.float32
    )


def times_weight(left, right):
    return jnp.dot(left, right, preferred_element_type=jnp.float32)


def split_heads(matrix):
    return matrix.reshape(matrix.shape[0], matrix.shape[1] // HEAD, HEAD)


def head_scores(query, keys):
    scores = jnp.einsum(
        "qhe,khe->hqk", split_heads(query), split_heads(keys), preferred_element_type=jnp.float32
    )
    return scores * (1.0 / math.sqrt(HEAD))


def attend(query, keys, values):
    scores = head_scores(query, keys)
    peak = jnp.max(scores, axis=-1, keepdims=True)
    powers = jnp.exp(scores - peak)
    summed = jnp.sum(powers, axis=-1, keepdims=True)
    low_probs = (powers / summed).astype(jnp.bfloat16)
    attended = jnp.einsum(
        "hqk,khe->qhe", low_probs, split_heads(values), preferred_element_type=jnp.float32
    )
    return (
        attended.reshape(query.shape[0], query.shape[1]).astype(jnp.bfloat16),
        peak + jnp.log(summed),
    )


def attend_back(query, keys, values, log_total, d_attended):
    probs = jnp.exp(head_scores(query, keys) - log_total)
    low_probs = probs.astype(jnp.bfloat16)
    d_heads = split_heads(d_attended)
    d_probs = jnp.einsum(
        "qhe,khe->hqk", d_heads, split_heads(values), preferred_element_type=jnp.float32
    )
    d_values = jnp.einsum("hqk,qhe->khe", low_probs, d_heads, preferred_element_type=jnp.float32)
    weighted = jnp.sum(probs * d_probs, axis=-1, keepdims=True)
    d_scores = (probs * (d_probs - weighted)).astype(jnp.bfloat16)
    scale = 1.0 / math.sqrt(HEAD)
    d_query = (
        jnp.einsum("hqk,khe->qhe", d_scores, split_heads(keys), preferred_element_type=jnp.float32)
        * scale
    )
    d_keys = (
        jnp.einsum("hqk,qhe->khe", d_scores, split_heads(query), preferred_element_type=jnp.float32)
        * scale
    )
    d_query = d_query.reshape(query.shape[0], query.shape[1]).astype(jnp.bfloat16)
    d_keys = d_keys.reshape(keys.shape[0], keys.shape[1]).astype(jnp.bfloat16)
    d_values = d_values.reshape(values.shape[0], values.shape[1]).astype(jnp.bfloat16)
    return (d_query, d_keys, d_values)


def group_rows(piece):
    return lax.all_gather(piece, "narrow", axis=0, tiled=True)


def own_rows(term, count_own):
    return lax.psum_scatter(
        term(jnp.int32(0), count_own * lax.axis_size("narrow")),
        "narrow",
        scatter_dimension=0,
        tiled=True,
    )


def feed_rows(piece):
    return lax.all_gather(piece, "narrow", axis=0, tiled=True)


def feed_back(term, count_own):
    return lax.psum_scatter(
        term(jnp.int32(0), lax.axis_size("narrow") * count_own).astype(jnp.bfloat16),
        "narrow",
        scatter_dimension=0,
        tiled=True,
    ).astype(jnp.float32)


def text_total(partial_value):
    return lax.psum(partial_value, "narrow")


def local(
    tokens,
    caption,
    token_mask,
    cotangent,
    gain_self,
    gain_cross,
    gain_feed,
    text_proj,
    query_self,
    key_self,
    value_self,
    out_self,
    query_cross,
    key_cross,
    value_cross,
    out_cross,
    up_proj,
    down_proj,
):
    own_count = tokens.shape[1]
    gain_one = gain_self.astype(jnp.float32)
    gain_two = gain_cross.astype(jnp.float32)
    gain_three = gain_feed.astype(jnp.float32)

    def forward_backward(totals, data):
        rows, words, marks, grads_in = data
        resid_in = rows.astype(jnp.float32)
        normed_self, inv_self = normalize(resid_in)
        hidden_self = (normed_self * gain_one).astype(jnp.bfloat16)
        image_self = group_rows(hidden_self)
        query_sa = times_weight(image_self, query_self).astype(jnp.bfloat16)
        keys_sa = times_weight(image_self, key_self).astype(jnp.bfloat16)
        values_sa = times_weight(image_self, value_self).astype(jnp.bfloat16)
        attended_sa, total_sa = attend(query_sa, keys_sa, values_sa)
        branch_sa = own_rows(lambda start, count: times_weight(attended_sa, out_self), own_count)
        resid_mid = resid_in + branch_sa
        context = text_total(times_weight(words, text_proj)).astype(jnp.bfloat16)
        normed_cross, inv_cross = normalize(resid_mid)
        hidden_cross = (normed_cross * gain_two).astype(jnp.bfloat16)
        image_cross = group_rows(hidden_cross)
        query_ca = times_weight(image_cross, query_cross).astype(jnp.bfloat16)
        keys_ca = times_weight(context, key_cross).astype(jnp.bfloat16)
        values_ca = times_weight(context, value_cross).astype(jnp.bfloat16)
        attended_ca, total_ca = attend(query_ca, keys_ca, values_ca)
        branch_ca = own_rows(lambda start, count: times_weight(attended_ca, out_cross), own_count)
        resid_late = resid_mid + branch_ca
        normed_feed, inv_feed = normalize(resid_late)
        hidden_feed = (normed_feed * gain_three).astype(jnp.bfloat16)
        d_result = grads_in.astype(jnp.float32) * marks[:, None].astype(jnp.float32)
        d_low = d_result.astype(jnp.bfloat16)
        image_feed = feed_rows(hidden_feed)
        pre_act = times_weight(image_feed, up_proj)
        gelu_out, gelu_pull = jax.vjp(jax.nn.gelu, pre_act)
        activ = gelu_out.astype(jnp.bfloat16)
        branch_feed = feed_back(lambda start, count: times_weight(activ, down_proj), own_count)
        resid_out = resid_late + branch_feed
        d_image = feed_rows(d_low)
        d_pre = gelu_pull(against(d_image, down_proj))[0].astype(jnp.bfloat16)
        part_down = contract(activ, d_image)
        part_up = contract(image_feed, d_pre)
        d_hidden_feed = feed_back(lambda start, count: against(d_pre, up_proj), own_count)
        part_gain_feed = jnp.sum(d_hidden_feed * normed_feed, axis=0)
        d_late = d_result + norm_back(d_hidden_feed * gain_three, normed_feed, inv_feed)
        d_late_low = d_late.astype(jnp.bfloat16)
        d_image_cross = group_rows(d_late_low)
        part_out_cross = contract(attended_ca, d_image_cross)
        d_attended_ca = against(d_image_cross, out_cross).astype(jnp.bfloat16)
        d_query_ca, d_keys_ca, d_values_ca = attend_back(
            query_ca, keys_ca, values_ca, total_ca, d_attended_ca
        )
        part_query_cross = contract(image_cross, d_query_ca)
        part_key_cross = contract(context, d_keys_ca)
        part_value_cross = contract(context, d_values_ca)
        d_hidden_cross = own_rows(lambda start, count: against(d_query_ca, query_cross), own_count)
        d_context = text_total(against(d_keys_ca, key_cross) + against(d_values_ca, value_cross))
        d_context = d_context.astype(jnp.bfloat16)
        part_text = contract(words, d_context)
        d_words = against(d_context, text_proj).astype(jnp.bfloat16)
        part_gain_cross = jnp.sum(d_hidden_cross * normed_cross, axis=0)
        d_mid = d_late + norm_back(d_hidden_cross * gain_two, normed_cross, inv_cross)
        d_mid_low = d_mid.astype(jnp.bfloat16)
        d_image_self = group_rows(d_mid_low)
        part_out_self = contract(attended_sa, d_image_self)
        d_attended_sa = against(d_image_self, out_self).astype(jnp.bfloat16)
        d_query_sa, d_keys_sa, d_values_sa = attend_back(
            query_sa, keys_sa, values_sa, total_sa, d_attended_sa
        )
        part_query_self = contract(image_self, d_query_sa)
        part_key_self = contract(image_self, d_keys_sa)
        part_value_self = contract(image_self, d_values_sa)

        def self_term(start, count):
            total = against(d_query_sa, query_self)
            total = total + against(d_keys_sa, key_self)
            return total + against(d_values_sa, value_self)

        d_hidden_self = own_rows(self_term, own_count)
        part_gain_self = jnp.sum(d_hidden_self * normed_self, axis=0)
        d_input = d_mid + norm_back(d_hidden_self * gain_one, normed_self, inv_self)
        parts = (
            part_gain_self,
            part_gain_cross,
            part_gain_feed,
            part_text,
            part_query_self,
            part_key_self,
            part_value_self,
            part_out_self,
            part_query_cross,
            part_key_cross,
            part_value_cross,
            part_out_cross,
            part_up,
            part_down,
        )
        updated = tuple((total + part for total, part in zip(totals, parts)))
        return (updated, (resid_out.astype(jnp.bfloat16), d_input.astype(jnp.bfloat16), d_words))

    zeros = tuple(
        (
            jnp.zeros(weight.shape, jnp.float32)
            for weight in (
                gain_self,
                gain_cross,
                gain_feed,
                text_proj,
                query_self,
                key_self,
                value_self,
                out_self,
                query_cross,
                key_cross,
                value_cross,
                out_cross,
                up_proj,
                down_proj,
            )
        )
    )
    data = (tokens, caption, token_mask, cotangent)
    totals, outputs = lax.scan(forward_backward, zeros, data)
    summed = (
        lax.psum_scatter(
            totals[3].astype(jnp.bfloat16), "wide", scatter_dimension=1, tiled=True
        ).astype(jnp.float32),
        lax.psum_scatter(
            totals[4].astype(jnp.bfloat16), "wide", scatter_dimension=0, tiled=True
        ).astype(jnp.float32),
        lax.psum_scatter(
            totals[5].astype(jnp.bfloat16), "wide", scatter_dimension=0, tiled=True
        ).astype(jnp.float32),
        lax.psum_scatter(
            totals[6].astype(jnp.bfloat16), "wide", scatter_dimension=0, tiled=True
        ).astype(jnp.float32),
        lax.psum_scatter(
            totals[7].astype(jnp.bfloat16), "wide", scatter_dimension=1, tiled=True
        ).astype(jnp.float32),
        lax.psum_scatter(
            totals[8].astype(jnp.bfloat16), "wide", scatter_dimension=0, tiled=True
        ).astype(jnp.float32),
        lax.psum_scatter(
            totals[9].astype(jnp.bfloat16), "wide", scatter_dimension=0, tiled=True
        ).astype(jnp.float32),
        lax.psum_scatter(
            totals[10].astype(jnp.bfloat16), "wide", scatter_dimension=0, tiled=True
        ).astype(jnp.float32),
        lax.psum_scatter(
            totals[11].astype(jnp.bfloat16), "wide", scatter_dimension=1, tiled=True
        ).astype(jnp.float32),
        lax.psum_scatter(
            totals[12].astype(jnp.bfloat16), "wide", scatter_dimension=0, tiled=True
        ).astype(jnp.float32),
        lax.psum_scatter(
            totals[13].astype(jnp.bfloat16), "wide", scatter_dimension=1, tiled=True
        ).astype(jnp.float32),
    )
    gains_done = lax.psum((totals[0], totals[1], totals[2]), ("wide", "narrow"))
    return (
        outputs[0],
        outputs[1],
        outputs[2],
        gains_done[0],
        gains_done[1],
        gains_done[2],
        summed[0],
        summed[1],
        summed[2],
        summed[3],
        summed[4],
        summed[5],
        summed[6],
        summed[7],
        summed[8],
        summed[9],
        summed[10],
    )


def solution(mesh):
    in_specs = (
        P("wide", "narrow", None),
        P("wide", None, "narrow"),
        P("wide", "narrow"),
        P("wide", "narrow", None),
        P(),
        P(),
        P(),
        P("narrow", None),
        P(None, "narrow"),
        P(None, "narrow"),
        P(None, "narrow"),
        P("narrow", None),
        P(None, "narrow"),
        P(None, "narrow"),
        P(None, "narrow"),
        P("narrow", None),
        P(None, "narrow"),
        P("narrow", None),
    )
    out_specs = (
        P("wide", "narrow", None),
        P("wide", "narrow", None),
        P("wide", None, "narrow"),
        P(),
        P(),
        P(),
        P("narrow", "wide"),
        P("wide", "narrow"),
        P("wide", "narrow"),
        P("wide", "narrow"),
        P("narrow", "wide"),
        P("wide", "narrow"),
        P("wide", "narrow"),
        P("wide", "narrow"),
        P("narrow", "wide"),
        P("wide", "narrow"),
        P("narrow", "wide"),
    )
    return jax.shard_map(local, mesh=mesh, in_specs=in_specs, out_specs=out_specs, check_vma=False)
```

profile of v0, /device:TPU:0, one launch (start us, length us, event | category | flops | bytes accessed | tf_op | source)
XLA Modules:
  0.0 1780.0 jit_solution(13403800361869481657)
XLA Ops:
  10.3 801.6 %while.45 = (s32[]{:T(128)}, f32[2048]{0:T(1024)}, f32[2048]{0:T(1024)}, f32[2048]{0:T(1024)}, f32[1024,2048]{1,0:T(8,128)}, /*index=5*/f32[2048,512]{1,0:T(8,12...) while((s32[]{:T(128)}, f32[2048]{0:T(1024)}, ...), condition=%wide.region_30.31_spmd.clone, body=%wide.region_0.30_spmd.clone.sunk | while | flops 26455246848 | bytes 800258496 | solution.py:263
  14.8 19.5 %all-gather.7.cloned.1.call-done = bf16[256,2048]{1,0:T(8,128)(2,1)} async-done(((bf16[64,2048]{1,0:T(8,128)(2,1)}), bf16[256,2048]{1,0:T(8,128)(2,1)}) %all-gather.7.cloned.1.call-update) | async-done | bytes 1048592 | tf_op jit(solution)/shard_map/while/body/eval_jaxpr/all_gather | solution.py:93
  51.0 26.6 %reduce-scatter.40.cloned.1.call-done = f32[64,2048]{1,0:T(8,128)} async-done(((f32[256,2048]{1,0:T(8,128)}), f32[64,2048]{1,0:T(8,128)}) %reduce-scatter.40.cloned.1.call-update) | async-done | bytes 524304 | tf_op jit(solution)/shard_map/while/body/eval_jaxpr/reduce_scatter | solution.py:97
  80.0 32.0 %all-reduce.3 = bf16[128,2048]{1,0:T(8,128)(2,1)S(1)} all-reduce(f32[128,2048]{1,0:T(8,128)} %fusion.374), channel_id=1, replica_groups=mesh['wide'=8,'narrow'=4] {'narrow'}, use_global_device_ids=true, to_apply=%region_6.6 | all-reduce | flops 262144 | bytes 1572864 | tf_op jit(solution)/shard_map/while/body/eval_jaxpr/psum | solution.py:119
  124.8 29.2 %reduce-scatter.42.cloned.1.call-done = f32[64,2048]{1,0:T(8,128)} async-done(((f32[256,2048]{1,0:T(8,128)}), f32[64,2048]{1,0:T(8,128)}) %reduce-scatter.42.cloned.1.call-update) | async-done | bytes 524304 | tf_op jit(solution)/shard_map/while/body/eval_jaxpr/reduce_scatter | solution.py:97
  208.5 25.0 %reduce-scatter.44.cloned.1.call-done = bf16[64,2048]{1,0:T(8,128)(2,1)} async-done(((bf16[256,2048]{1,0:T(8,128)(2,1)}), bf16[64,2048]{1,0:T(8,128)(2,1)}) %reduce-scatter.44.cloned.1.call-update) | async-done | bytes 262160 | tf_op jit(solution)/shard_map/while/body/eval_jaxpr/reduce_scatter | solution.py:110
  289.4 27.7 %reduce-scatter.46.cloned.1.call-done = f32[64,2048]{1,0:T(8,128)} async-done(((f32[256,2048]{1,0:T(8,128)}), f32[64,2048]{1,0:T(8,128)}) %reduce-scatter.46.cloned.1.call-update) | async-done | bytes 524304 | tf_op jit(solution)/shard_map/while/body/eval_jaxpr/reduce_scatter | solution.py:97
  327.7 30.0 %all-reduce.4 = bf16[128,2048]{1,0:T(8,128)(2,1)S(1)} all-reduce(f32[128,2048]{1,0:T(8,128)} %convolution_add_fusion.8), channel_id=1, replica_groups=mesh['wide'=8,'narrow'=4] {'narrow'}, use_global_device_ids=true, to_apply=%region_26.26 | all-reduce | flops 262144 | bytes 1572864 | tf_op jit(solution)/shard_map/while/body/eval_jaxpr/psum | solution.py:119
  446.8 26.6 %reduce-scatter.40.cloned.1.call-done = f32[64,2048]{1,0:T(8,128)} async-done(((f32[256,2048]{1,0:T(8,128)}), f32[64,2048]{1,0:T(8,128)}) %reduce-scatter.40.cloned.1.call-update) | async-done | bytes 524304 | tf_op jit(solution)/shard_map/while/body/eval_jaxpr/reduce_scatter | solution.py:97
  475.8 32.1 %all-reduce.3 = bf16[128,2048]{1,0:T(8,128)(2,1)S(1)} all-reduce(f32[128,2048]{1,0:T(8,128)} %fusion.374), channel_id=1, replica_groups=mesh['wide'=8,'narrow'=4] {'narrow'}, use_global_device_ids=true, to_apply=%region_6.6 | all-reduce | flops 262144 | bytes 1572864 | tf_op jit(solution)/shard_map/while/body/eval_jaxpr/psum | solution.py:119
  520.7 29.1 %reduce-scatter.42.cloned.1.call-done = f32[64,2048]{1,0:T(8,128)} async-done(((f32[256,2048]{1,0:T(8,128)}), f32[64,2048]{1,0:T(8,128)}) %reduce-scatter.42.cloned.1.call-update) | async-done | bytes 524304 | tf_op jit(solution)/shard_map/while/body/eval_jaxpr/reduce_scatter | solution.py:97
  604.3 25.0 %reduce-scatter.44.cloned.1.call-done = bf16[64,2048]{1,0:T(8,128)(2,1)} async-done(((bf16[256,2048]{1,0:T(8,128)(2,1)}), bf16[64,2048]{1,0:T(8,128)(2,1)}) %reduce-scatter.44.cloned.1.call-update) | async-done | bytes 262160 | tf_op jit(solution)/shard_map/while/body/eval_jaxpr/reduce_scatter | solution.py:110
  725.8 27.6 %all-reduce.4 = bf16[128,2048]{1,0:T(8,128)(2,1)S(1)} all-reduce(f32[128,2048]{1,0:T(8,128)} %convolution_add_fusion.8), channel_id=1, replica_groups=mesh['wide'=8,'narrow'=4] {'narrow'}, use_global_device_ids=true, to_apply=%region_26.26 | all-reduce | flops 262144 | bytes 1572864 | tf_op jit(solution)/shard_map/while/body/eval_jaxpr/psum | solution.py:119
  868.7 41.2 %all-reduce = (f32[2048]{0:T(1024)}, f32[2048]{0:T(1024)}, f32[2048]{0:T(1024)}) all-reduce(f32[2048]{0:T(1024)S(1)} %copy-done.69, f32[2048]{0:T(1024)S(1)} %copy-done.66, f32[2048]{0:T(1024)S(1)} %copy-done.63), channel_id=1, replica_groups=mesh['wide'=8,'narrow'=4] {'wide','narrow'}, use_global_device_ids=true, to_apply=%region_31.32 | all-reduce | flops 6144 | bytes 49152 | tf_op jit(solution)/shard_map/psum | solution.py:299
  911.8 44.3 %reduce-scatter.22.cloned.1.call-done = bf16[256,512]{1,0:T(8,128)(2,1)} async-done(((bf16[2048,512]{1,0:T(8,128)(2,1)}), bf16[256,512]{1,0:T(8,128)(2,1)}) %reduce-scatter.22.cloned.1.call-update) | async-done | bytes 262160 | tf_op jit(solution)/shard_map/reduce_scatter | solution.py:271
  957.9 68.3 %reduce-scatter.24.cloned.1.call-done = bf16[256,512]{1,0:T(8,128)(2,1)} async-done(((bf16[2048,512]{1,0:T(8,128)(2,1)}), bf16[256,512]{1,0:T(8,128)(2,1)}) %reduce-scatter.24.cloned.1.call-update) | async-done | bytes 262160 | tf_op jit(solution)/shard_map/reduce_scatter | solution.py:274
  1028.0 68.9 %reduce-scatter.26.cloned.1.call-done = bf16[512,256]{1,0:T(8,128)(2,1)} async-done(((bf16[512,2048]{1,0:T(8,128)(2,1)}), bf16[512,256]{1,0:T(8,128)(2,1)}) %reduce-scatter.26.cloned.1.call-update) | async-done | bytes 262160 | tf_op jit(solution)/shard_map/reduce_scatter | solution.py:277
  1098.6 68.4 %reduce-scatter.28.cloned.1.call-done = bf16[256,512]{1,0:T(8,128)(2,1)} async-done(((bf16[2048,512]{1,0:T(8,128)(2,1)}), bf16[256,512]{1,0:T(8,128)(2,1)}) %reduce-scatter.28.cloned.1.call-update) | async-done | bytes 262160 | tf_op jit(solution)/shard_map/reduce_scatter | solution.py:280
  1168.9 68.4 %reduce-scatter.30.cloned.1.call-done = bf16[256,512]{1,0:T(8,128)(2,1)} async-done(((bf16[2048,512]{1,0:T(8,128)(2,1)}), bf16[256,512]{1,0:T(8,128)(2,1)}) %reduce-scatter.30.cloned.1.call-update) | async-done | bytes 262160 | tf_op jit(solution)/shard_map/reduce_scatter | solution.py:283
  1239.1 68.2 %reduce-scatter.32.cloned.1.call-done = bf16[256,512]{1,0:T(8,128)(2,1)} async-done(((bf16[2048,512]{1,0:T(8,128)(2,1)}), bf16[256,512]{1,0:T(8,128)(2,1)}) %reduce-scatter.32.cloned.1.call-update) | async-done | bytes 262160 | tf_op jit(solution)/shard_map/reduce_scatter | solution.py:286
  1309.1 69.0 %reduce-scatter.34.cloned.1.call-done = bf16[512,256]{1,0:T(8,128)(2,1)} async-done(((bf16[512,2048]{1,0:T(8,128)(2,1)}), bf16[512,256]{1,0:T(8,128)(2,1)}) %reduce-scatter.34.cloned.1.call-update) | async-done | bytes 262160 | tf_op jit(solution)/shard_map/reduce_scatter | solution.py:289
  1379.9 88.8 %reduce-scatter.18.cloned.1.call-done = bf16[1024,256]{1,0:T(8,128)(2,1)} async-done(((bf16[1024,2048]{1,0:T(8,128)(2,1)}), bf16[1024,256]{1,0:T(8,128)(2,1)}) %reduce-scatter.18.cloned.1.call-update) | async-done | bytes 524304 | tf_op jit(solution)/shard_map/reduce_scatter | solution.py:265
  1470.7 148.7 %reduce-scatter.36.cloned.1.call-done = bf16[256,2048]{1,0:T(8,128)(2,1)} async-done(((bf16[2048,2048]{1,0:T(8,128)(2,1)}), bf16[256,2048]{1,0:T(8,128)(2,1)}) %reduce-scatter.36.cloned.1.call-update) | async-done | bytes 1048592 | tf_op jit(solution)/shard_map/reduce_scatter | solution.py:292
  1622.2 147.3 %reduce-scatter.38.cloned.1.call-done = bf16[2048,256]{1,0:T(8,128)(2,1)} async-done(((bf16[2048,2048]{1,0:T(8,128)(2,1)}), bf16[2048,256]{1,0:T(8,128)(2,1)}) %reduce-scatter.38.cloned.1.call-update) | async-done | bytes 1048592 | tf_op jit(solution)/shard_map/reduce_scatter | solution.py:295
  (643 shorter events, 544.0 us)
Async XLA Ops:
  46.0 70.3 %all-gather.11.cloned.1.call-start = ((), (), s32[]{:S(2)}) async-start(), calls=%async_computation.31 | async-start | bytes 1310720 | tf_op jit(solution)/shard_map/while/body/eval_jaxpr/all_gather | solution.py:93
  79.9 74.1 %reduce-scatter.42.cloned.1.call-start = ((), (), s32[]{:S(2)}) async-start(), calls=%async_computation.32 | async-start | bytes 2621440 | tf_op jit(solution)/shard_map/while/body/eval_jaxpr/reduce_scatter | solution.py:97
  124.8 66.9 %all-gather.13.cloned.1.call-start = ((), (), s32[]{:S(2)}) async-start(), calls=%async_computation.33 | async-start | bytes 1310720 | tf_op jit(solution)/shard_map/while/body/eval_jaxpr/all_gather | solution.py:106
  156.3 77.2 %reduce-scatter.44.cloned.1.call-start = ((), (), s32[]{:S(2)}) async-start(), calls=%async_computation.34 | async-start | bytes 1310720 | tf_op jit(solution)/shard_map/while/body/eval_jaxpr/reduce_scatter | solution.py:110
  245.2 71.9 %reduce-scatter.46.cloned.1.call-start = ((), (), s32[]{:S(2)}) async-start(), calls=%async_computation.36 | async-start | bytes 2621440 | tf_op jit(solution)/shard_map/while/body/eval_jaxpr/reduce_scatter | solution.py:97
  264.1 93.6 %all-gather.17.cloned.1.call-start = ((), (), s32[]{:S(2)}) async-start(), calls=%async_computation.37 | async-start | bytes 1310720 | tf_op jit(solution)/shard_map/while/body/eval_jaxpr/all_gather | solution.py:93
  321.2 83.4 %reduce-scatter.48.cloned.1.call-start = ((), (), s32[]{:S(2)}) async-start(), calls=%async_computation.38 | async-start | bytes 2621440 | tf_op jit(solution)/shard_map/while/body/eval_jaxpr/reduce_scatter | solution.py:97
  441.8 70.3 %all-gather.11.cloned.1.call-start = ((), (), s32[]{:S(2)}) async-start(), calls=%async_computation.31 | async-start | bytes 1310720 | tf_op jit(solution)/shard_map/while/body/eval_jaxpr/all_gather | solution.py:93
  475.7 74.0 %reduce-scatter.42.cloned.1.call-start = ((), (), s32[]{:S(2)}) async-start(), calls=%async_computation.32 | async-start | bytes 2621440 | tf_op jit(solution)/shard_map/while/body/eval_jaxpr/reduce_scatter | solution.py:97
  552.1 77.2 %reduce-scatter.44.cloned.1.call-start = ((), (), s32[]{:S(2)}) async-start(), calls=%async_computation.34 | async-start | bytes 1310720 | tf_op jit(solution)/shard_map/while/body/eval_jaxpr/reduce_scatter | solution.py:110
  641.0 72.0 %reduce-scatter.46.cloned.1.call-start = ((), (), s32[]{:S(2)}) async-start(), calls=%async_computation.36 | async-start | bytes 2621440 | tf_op jit(solution)/shard_map/while/body/eval_jaxpr/reduce_scatter | solution.py:97
  659.8 93.5 %all-gather.17.cloned.1.call-start = ((), (), s32[]{:S(2)}) async-start(), calls=%async_computation.37 | async-start | bytes 1310720 | tf_op jit(solution)/shard_map/while/body/eval_jaxpr/all_gather | solution.py:93
  717.2 86.1 %reduce-scatter.48.cloned.1.call-start = ((), (), s32[]{:S(2)}) async-start(), calls=%async_computation.38 | async-start | bytes 2621440 | tf_op jit(solution)/shard_map/while/body/eval_jaxpr/reduce_scatter | solution.py:97
  811.9 98.1 %reduce-scatter.20.cloned.1.call-start = ((), (), s32[]{:S(2)}) async-start(), calls=%async_computation.18 | async-start | bytes 2359296 | tf_op jit(solution)/shard_map/reduce_scatter | solution.py:268
  815.7 140.4 %reduce-scatter.22.cloned.1.call-start = ((), (), s32[]{:S(2)}) async-start(), calls=%async_computation.19 | async-start | bytes 2359296 | tf_op jit(solution)/shard_map/reduce_scatter | solution.py:271
  819.6 206.6 %reduce-scatter.24.cloned.1.call-start = ((), (), s32[]{:S(2)}) async-start(), calls=%async_computation.20 | async-start | bytes 2359296 | tf_op jit(solution)/shard_map/reduce_scatter | solution.py:274
  823.5 273.3 %reduce-scatter.26.cloned.1.call-start = ((), (), s32[]{:S(2)}) async-start(), calls=%async_computation.21 | async-start | bytes 2359296 | tf_op jit(solution)/shard_map/reduce_scatter | solution.py:277
  827.6 339.4 %reduce-scatter.28.cloned.1.call-start = ((), (), s32[]{:S(2)}) async-start(), calls=%async_computation.22 | async-start | bytes 2359296 | tf_op jit(solution)/shard_map/reduce_scatter | solution.py:280
  831.5 405.8 %reduce-scatter.30.cloned.1.call-start = ((), (), s32[]{:S(2)}) async-start(), calls=%async_computation.23 | async-start | bytes 2359296 | tf_op jit(solution)/shard_map/reduce_scatter | solution.py:283
  835.4 471.9 %reduce-scatter.32.cloned.1.call-start = ((), (), s32[]{:S(2)}) async-start(), calls=%async_computation.24 | async-start | bytes 2359296 | tf_op jit(solution)/shard_map/reduce_scatter | solution.py:286
  839.3 538.8 %reduce-scatter.34.cloned.1.call-start = ((), (), s32[]{:S(2)}) async-start(), calls=%async_computation.25 | async-start | bytes 2359296 | tf_op jit(solution)/shard_map/reduce_scatter | solution.py:289
  843.3 625.4 %reduce-scatter.18.cloned.1.call-start = ((), (), s32[]{:S(2)}) async-start(), calls=%async_computation.17 | async-start | bytes 4718592 | tf_op jit(solution)/shard_map/reduce_scatter | solution.py:265
  849.4 770.0 %reduce-scatter.36.cloned.1.call-start = ((), (), s32[]{:S(2)}) async-start(), calls=%async_computation.26 | async-start | bytes 9437184 | tf_op jit(solution)/shard_map/reduce_scatter | solution.py:292
  858.8 910.7 %reduce-scatter.38.cloned.1.call-start = ((), (), s32[]{:S(2)}) async-start(), calls=%async_computation.27 | async-start | bytes 9437184 | tf_op jit(solution)/shard_map/reduce_scatter | solution.py:295
  (178 other events, 1893.5 us)
Sparse Core Ops, SparseCore 0:
  14.9 19.4 all-gather.6
  46.1 31.4 reduce-scatter.39
  80.1 21.0 all-gather.10
  123.1 30.9 reduce-scatter.41
  156.1 16.7 all-gather.8
  174.9 16.7 all-gather.12
  208.6 24.8 reduce-scatter.43
  237.7 16.7 all-gather.14
  257.6 24.8 reduce-scatter.49
  285.6 31.4 reduce-scatter.45
  321.4 20.5 all-gather.16
  369.8 31.4 reduce-scatter.47
  412.9 17.1 all-gather.6
  441.9 31.4 reduce-scatter.39
  475.9 21.0 all-gather.10
  518.9 30.8 reduce-scatter.41
  551.8 16.7 all-gather.8
  570.7 16.7 all-gather.12
  604.4 24.8 reduce-scatter.43
  633.5 16.7 all-gather.14
  653.3 24.8 reduce-scatter.49
  681.5 31.4 reduce-scatter.45
  717.3 18.3 all-gather.16
  765.5 32.3 reduce-scatter.47
Sparse Core Ops, SparseCore 1:
  816.4 69.2 reduce-scatter.19
  889.6 66.4 reduce-scatter.21
  959.5 66.6 reduce-scatter.23
  1029.7 67.1 reduce-scatter.25
  1100.4 66.6 reduce-scatter.27
  1170.6 66.6 reduce-scatter.29
  1240.6 66.6 reduce-scatter.31
  1310.7 67.3 reduce-scatter.33
  1381.6 87.0 reduce-scatter.17
  1472.7 146.6 reduce-scatter.35
  1622.9 146.5 reduce-scatter.37
where the time goes:
time: 1780 us
  waiting for transfers between devices  1160 us (65%)
  matrix products  242 us (14%)
  blocking collectives  163 us (9%)
  other arithmetic  129 us (7%)
  local copies, waits for them, and re-layouts  61.2 us (3%)
    reduce_scatter x8, waiting for transfers between devices, own_rows(): lax.psum_scatter(term(jnp.int32(0), count_own * lax.axis_size('narrow')),...  159 us
    reduce_scatter x1, waiting for transfers between devices, local(): lax.psum_scatter(totals[12].astype(jnp.bfloat16), 'wide', scatter_dimensi...  149 us
    reduce_scatter x1, waiting for transfers between devices, local(): lax.psum_scatter(totals[13].astype(jnp.bfloat16), 'wide', scatter_dimensi...  147 us
    psum x4, blocking collectives, text_total(): return lax.psum(partial_value, 'narrow')  122 us
    reduce_scatter x1, waiting for transfers between devices, local(): lax.psum_scatter(totals[3].astype(jnp.bfloat16), 'wide', scatter_dimensio...  88.8 us
    dot_general x22, matrix products, contract(): lax.dot_general(left, right, (((0,), (0,)), ((), ())), preferred_element_...  81.7 us
    dot_general x22, matrix products, times_weight(): return jnp.dot(left, right, preferred_element_type=jnp.float32)  74.4 us
    dot_general x22, matrix products, against(): lax.dot_general(left, right, (((1,), (1,)), ((), ())), preferred_element_...  70.4 us
  transfers between devices with their start and end apart: 35, of which 26 were waited for; matrix products, arithmetic and copies ran while one was open for 14% of the time, Pallas kernels for 0%

commit v1 on v0

v1 whole, which is shorter than its diff:
```python
import math

import jax
import jax.numpy as jnp
from jax import lax
from jax.experimental import pallas as pl
from jax.experimental.pallas import tpu as pltpu
from jax.sharding import PartitionSpec as P

HEAD = 128
MESH = pl.DeviceIdType.MESH

def normalize(rows):
    centre = jnp.mean(rows, axis=-1, keepdims=True)
    centred = rows - centre
    variance = jnp.mean(centred * centred, axis=-1, keepdims=True)
    inv_std = lax.rsqrt(variance + 1e-05)
    return (centred * inv_std, inv_std)


def norm_back(d_normed, normed, inv_std):
    inner = d_normed - jnp.mean(d_normed, axis=-1, keepdims=True)
    inner = inner - normed * jnp.mean(d_normed * normed, axis=-1, keepdims=True)
    return inv_std * inner


def times_weight(left, right):
    return jnp.dot(left, right, preferred_element_type=jnp.float32)


def split_heads(matrix):
    return matrix.reshape(matrix.shape[0], matrix.shape[1], matrix.shape[2] // HEAD, HEAD)


def join_heads(heads):
    return heads.reshape(heads.shape[0], heads.shape[1], heads.shape[2] * HEAD)


def head_scores(query, keys):
    scores = jnp.einsum(
        "bqhe,bkhe->bhqk", split_heads(query), split_heads(keys), preferred_element_type=jnp.float32
    )
    return scores * (1.0 / math.sqrt(HEAD))


def attend(query, keys, values):
    scores = head_scores(query, keys)
    peak = jnp.max(scores, axis=-1, keepdims=True)
    powers = jnp.exp(scores - peak)
    summed = jnp.sum(powers, axis=-1, keepdims=True)
    low_probs = (powers / summed).astype(jnp.bfloat16)
    attended = jnp.einsum(
        "bhqk,bkhe->bqhe", low_probs, split_heads(values), preferred_element_type=jnp.float32
    )
    return join_heads(attended).astype(jnp.bfloat16), peak + jnp.log(summed)


def attend_back(query, keys, values, log_total, d_attended):
    probs = jnp.exp(head_scores(query, keys) - log_total)
    low_probs = probs.astype(jnp.bfloat16)
    d_heads = split_heads(d_attended)
    d_probs = jnp.einsum(
        "bqhe,bkhe->bhqk", d_heads, split_heads(values), preferred_element_type=jnp.float32
    )
    d_values = jnp.einsum("bhqk,bqhe->bkhe", low_probs, d_heads, preferred_element_type=jnp.float32)
    weighted = jnp.sum(probs * d_probs, axis=-1, keepdims=True)
    d_scores = (probs * (d_probs - weighted)).astype(jnp.bfloat16)
    scale = 1.0 / math.sqrt(HEAD)
    d_query = (
        jnp.einsum("bhqk,bkhe->bqhe", d_scores, split_heads(keys), preferred_element_type=jnp.float32)
        * scale
    )
    d_keys = (
        jnp.einsum("bhqk,bqhe->bkhe", d_scores, split_heads(query), preferred_element_type=jnp.float32)
        * scale
    )
    return tuple(join_heads(d).astype(jnp.bfloat16) for d in (d_query, d_keys, d_values))


def contract(left, right):
    return lax.dot_general(
        left, right, (((0, 1), (0, 1)), ((), ())), preferred_element_type=jnp.float32
    ).astype(jnp.bfloat16)


def against(left, right):
    return lax.dot_general(
        left, right, (((2,), (1,)), ((), ())), preferred_element_type=jnp.float32
    )


def group_rows(piece):
    return lax.all_gather(piece, "narrow", axis=1, tiled=True)


def own_rows(partial):
    return lax.psum_scatter(partial, "narrow", scatter_dimension=1, tiled=True)


def feed_back(partial):
    return own_rows(partial.astype(jnp.bfloat16)).astype(jnp.float32)


def text_total(partial):
    return lax.psum(partial, "narrow")


def wide_sum(arrays, dims, wide, order=None, z_first=3, ahead=2):
    Z = wide // 2
    units = []
    shapes = []
    for a, (arr, dim) in enumerate(zip(arrays, dims)):
        if dim == 0:
            blk = arr.shape[0] // wide
            n = arr.shape[1] // 512
            shapes.append((blk, arr.shape[1]))
        else:
            blk = arr.shape[1] // wide
            n = arr.shape[0] // 512
            shapes.append((arr.shape[0], blk))
        for c in range(n):
            units.append((a, dim, c, blk))
    if order is not None:
        units = [units[i] for i in order]
    blk = units[0][3]
    shp = [(blk, 512), (512, blk)]
    U = len(units)
    zset = set(int((k + 0.5) * U / z_first) for k in range(z_first)) if z_first else set()
    yf = [u for k, u in enumerate(units) if k not in zset]
    zf = [u for k, u in enumerate(units) if k in zset]
    cnt = {}
    def slot(key):
        cnt[key] = cnt.get(key, 0) + 1
        return cnt[key] - 1
    yslots = [slot(("y", u[1])) for u in yf]
    zslots = [slot(("z", u[1])) for u in zf]
    ny = [max(1, cnt.get(("y", d), 0)) for d in (0, 1)]
    nz = [max(1, cnt.get(("z", d), 0)) for d in (0, 1)]
    OWN = 3

    def kernel(*refs):
        ins = refs[: len(arrays)]
        outs = refs[len(arrays): 2 * len(arrays)]
        (S0, S1, R0, R1, L0, L1, O0, O1, T0, T1, ZR0, ZR1, ZL0, ZL1, YB0, YB1, F0, F1,
         ysend, yrecv, own_sem, rsend, rrecv, lsend, lrecv,
         tsem, zrsend, zrrecv, zlsend, zlrecv, ybsend, ybrecv, out_sem) = refs[2 * len(arrays):]
        S, R, L, O, T, ZR, ZL, YB, F = ((S0, S1), (R0, R1), (L0, L1), (O0, O1), (T0, T1), (ZR0, ZR1), (ZL0, ZL1), (YB0, YB1), (F0, F1))
        me = lax.axis_index("wide")
        z = me // 2
        y = me % 2
        yp = {"wide": z * 2 + (1 - y)}
        zr = {"wide": jnp.minimum(z + 1, Z - 1) * 2 + y}
        zl = {"wide": jnp.maximum(z - 1, 0) * 2 + y}
        has_r = z < Z - 1
        has_l = z > 0
        bar = pltpu.get_barrier_semaphore()
        pl.semaphore_signal(bar, inc=1, device_id=yp, device_id_type=MESH)
        @pl.when(has_r)
        def _():
            pl.semaphore_signal(bar, inc=1, device_id=zr, device_id_type=MESH)
        @pl.when(has_l)
        def _():
            pl.semaphore_signal(bar, inc=1, device_id=zl, device_id_type=MESH)
        pl.semaphore_wait(bar, 1 + has_r.astype(jnp.int32) + has_l.astype(jnp.int32))

        def block(u, w):
            a, dim, c, b = u
            start = pl.multiple_of(w * b, b)
            if dim == 0:
                return ins[a].at[pl.ds(start, b), pl.ds(c * 512, 512)]
            return ins[a].at[pl.ds(c * 512, 512), pl.ds(start, b)]

        def outblock(u):
            a, dim, c, b = u
            if dim == 0:
                return outs[a].at[:, pl.ds(c * 512, 512)]
            return outs[a].at[pl.ds(c * 512, 512), :]

        def addto(dst, src):
            rows = dst.shape[0]
            step = min(rows, 64)
            def body(i, _):
                s = pl.ds(pl.multiple_of(i * step, step), step)
                dst[s, :] = dst[s, :] + src[s, :]
                return 0
            lax.fori_loop(0, rows // step, body, 0)

        def rc(src, dst, ss, rs, dev):
            return pltpu.make_async_remote_copy(src_ref=src, dst_ref=dst, send_sem=ss, recv_sem=rs, device_id=dev, device_id_type=MESH)

        def ycopy(i, k):
            u, s = yf[i], yslots[i]
            return rc(block(u, k * 2 + (1 - y)), S[u[1]].at[s, k], ysend.at[i, k], yrecv.at[i, k], yp)
        def ocopy(i, k):
            u = yf[i]
            return pltpu.make_async_copy(block(u, k * 2 + y), O[u[1]].at[i % OWN, k], own_sem.at[i % OWN, k])
        korder = [0, Z - 1] + list(range(1, Z - 1))
        def ystart(i):
            for k in korder:
                ycopy(i, k).start()
        def ostart(i):
            for k in korder:
                ocopy(i, k).start()
        def yadd(i):
            u, s = yf[i], yslots[i]
            for k in korder:
                ycopy(i, k).wait_recv()
                ocopy(i, k).wait()
                addto(S[u[1]].at[s, k], O[u[1]].at[i % OWN, k])

        def rcopy(i, t):
            u, s = yf[i], yslots[i]
            d = Z - t + z
            return rc(S[u[1]].at[s, jnp.clip(d, 0, Z - 1)], R[u[1]].at[s, t - 1], rsend.at[i, t - 1], rrecv.at[i, t - 1], zr)
        def lcopy(i, t):
            u, s = yf[i], yslots[i]
            d = t - Z + z
            return rc(S[u[1]].at[s, jnp.clip(d, 0, Z - 1)], L[u[1]].at[s, t - 1], lsend.at[i, t - 1], lrecv.at[i, t - 1], zl)
        def chain(i, t):
            u, s = yf[i], yslots[i]
            kd = u[1]
            @pl.when(has_r & (t >= z + 1))
            def _():
                if t > 1:
                    @pl.when(has_l & (t - 1 >= z))
                    def _():
                        rcopy(i, t - 1).wait_recv()
                        addto(S[kd].at[s, jnp.clip(Z - t + z, 0, Z - 1)], R[kd].at[s, t - 2])
                rcopy(i, t).start()
            zb = Z - 1 - z
            @pl.when(has_l & (t >= zb + 1))
            def _():
                if t > 1:
                    @pl.when(has_r & (t - 1 >= zb))
                    def _():
                        lcopy(i, t - 1).wait_recv()
                        addto(S[kd].at[s, jnp.clip(t - Z + z, 0, Z - 1)], L[kd].at[s, t - 2])
                lcopy(i, t).start()
        nfin = [0]
        def emit(u, get):
            f = nfin[0]
            nfin[0] += 1
            q = f % 2
            if f >= 2:
                pu = emitted[f - 2]
                pltpu.make_async_copy(F[pu[1]].at[q], outblock(pu), out_sem.at[q]).wait()
            get(F[u[1]].at[q])
            pltpu.make_async_copy(F[u[1]].at[q], outblock(u), out_sem.at[q]).start()
            emitted.append(u)
        emitted = []
        def final(i):
            u, s = yf[i], yslots[i]
            kd = u[1]
            @pl.when(has_l)
            def _():
                rcopy(i, Z - 1).wait_recv()
                addto(S[kd].at[s, z], R[kd].at[s, Z - 2])
            @pl.when(has_r)
            def _():
                lcopy(i, Z - 1).wait_recv()
                addto(S[kd].at[s, z], L[kd].at[s, Z - 2])
            def get(dst):
                dst[...] = S[kd][s, z]
            emit(u, get)

        def tcopy(j, w):
            u, s = zf[j], zslots[j]
            return pltpu.make_async_copy(block(u, w), T[u[1]].at[s, w // 2, w % 2], tsem.at[j, w])
        def zrcopy(j, t):
            u, s = zf[j], zslots[j]
            d = Z - t + z
            return rc(T[u[1]].at[s, jnp.clip(d, 0, Z - 1)], ZR[u[1]].at[s, t - 1], zrsend.at[j, t - 1], zrrecv.at[j, t - 1], zr)
        def zlcopy(j, t):
            u, s = zf[j], zslots[j]
            d = t - Z + z
            return rc(T[u[1]].at[s, jnp.clip(d, 0, Z - 1)], ZL[u[1]].at[s, t - 1], zlsend.at[j, t - 1], zlrecv.at[j, t - 1], zl)
        def zchain(j, t):
            u, s = zf[j], zslots[j]
            kd = u[1]
            if t == 1:
                for w in range(wide):
                    tcopy(j, w).wait()
            @pl.when(has_r & (t >= z + 1))
            def _():
                if t > 1:
                    @pl.when(has_l & (t - 1 >= z))
                    def _():
                        zrcopy(j, t - 1).wait_recv()
                        for q in range(2):
                            addto(T[kd].at[s, jnp.clip(Z - t + z, 0, Z - 1), q], ZR[kd].at[s, t - 2, q])
                zrcopy(j, t).start()
            zb = Z - 1 - z
            @pl.when(has_l & (t >= zb + 1))
            def _():
                if t > 1:
                    @pl.when(has_r & (t - 1 >= zb))
                    def _():
                        zlcopy(j, t - 1).wait_recv()
                        for q in range(2):
                            addto(T[kd].at[s, jnp.clip(t - Z + z, 0, Z - 1), q], ZL[kd].at[s, t - 2, q])
                zlcopy(j, t).start()
        def ybcopy(j):
            u, s = zf[j], zslots[j]
            return rc(T[u[1]].at[s, z, 1 - y], YB[u[1]].at[s], ybsend.at[j], ybrecv.at[j], yp)
        def zfold(j):
            u, s = zf[j], zslots[j]
            kd = u[1]
            @pl.when(has_l)
            def _():
                zrcopy(j, Z - 1).wait_recv()
                for q in range(2):
                    addto(T[kd].at[s, z, q], ZR[kd].at[s, Z - 2, q])
            @pl.when(has_r)
            def _():
                zlcopy(j, Z - 1).wait_recv()
                for q in range(2):
                    addto(T[kd].at[s, z, q], ZL[kd].at[s, Z - 2, q])
            ybcopy(j).start()
        def zfinal(j):
            u, s = zf[j], zslots[j]
            kd = u[1]
            ybcopy(j).wait_recv()
            def get(dst):
                dst[...] = T[kd][s, z, y] + YB[kd][s]
            emit(u, get)

        NY, NZ = len(yf), len(zf)
        for i in range(min(ahead, NY)):
            ystart(i)
        for j in range(NZ):
            for w in range(wide):
                tcopy(j, w).start()
        for i in range(min(2, NY)):
            ostart(i)
        gap = max(2, NY // max(NZ, 1))
        zev = {}
        for j in range(NZ):
            b = j * gap
            for t in range(1, Z):
                zev.setdefault(b + 1 * (t - 1), []).append(("c", j, t))
            zev.setdefault(b + (Z - 1), []).append(("f", j, 0))
            zev.setdefault(b + (Z - 1) + 1, []).append(("e", j, 0))
        last = max([NY + Z] + [k + 1 for k in zev])
        for k in range(last):
            for ev in zev.get(k, []):
                if ev[0] == "c":
                    zchain(ev[1], ev[2])
                elif ev[0] == "f":
                    zfold(ev[1])
                else:
                    zfinal(ev[1])
            if k < NY:
                if k + ahead < NY:
                    ystart(k + ahead)
                if k + 2 < NY:
                    ostart(k + 2)
                yadd(k)
            for t in range(1, Z):
                i = k - (t - 1)
                if 0 <= i < NY:
                    chain(i, t)
            i = k - (Z - 1)
            if 0 <= i < NY:
                final(i)
        nf = nfin[0]
        for f in range(max(0, nf - 2), nf):
            u = emitted[f]
            pltpu.make_async_copy(F[u[1]].at[f % 2], outblock(u), out_sem.at[f % 2]).wait()
        for i in range(NY):
            for k in range(Z):
                ycopy(i, k).wait_send()
            for t in range(1, Z):
                @pl.when(has_r & (t >= z + 1))
                def _():
                    rcopy(i, t).wait_send()
                @pl.when(has_l & (t >= Z - z))
                def _():
                    lcopy(i, t).wait_send()
        for j in range(NZ):
            for t in range(1, Z):
                @pl.when(has_r & (t >= z + 1))
                def _():
                    zrcopy(j, t).wait_send()
                @pl.when(has_l & (t >= Z - z))
                def _():
                    zlcopy(j, t).wait_send()
            ybcopy(j).wait_send()

    bf = jnp.bfloat16
    V = pltpu.VMEM
    DS = pltpu.SemaphoreType.DMA
    sc = []
    for d in (0, 1): sc.append(V((ny[d], Z) + shp[d], bf))
    for _ in range(2):
        for d in (0, 1): sc.append(V((ny[d], Z - 1) + shp[d], bf))
    for d in (0, 1): sc.append(V((OWN, Z) + shp[d], bf))
    for d in (0, 1): sc.append(V((nz[d], Z, 2) + shp[d], bf))
    for _ in range(2):
        for d in (0, 1): sc.append(V((nz[d], Z - 1, 2) + shp[d], bf))
    for d in (0, 1): sc.append(V((nz[d],) + shp[d], bf))
    for d in (0, 1): sc.append(V((2,) + shp[d], bf))
    NY, NZ = len(yf), max(1, len(zf))
    sc += [DS((NY, Z)), DS((NY, Z)), DS((OWN, Z))] + [DS((NY, Z - 1))] * 4
    sc += [DS((NZ, wide))] + [DS((NZ, Z - 1))] * 4 + [DS((NZ,)), DS((NZ,)), DS((2,))]
    return pl.pallas_call(
        kernel,
        out_shape=[jax.ShapeDtypeStruct(s, bf) for s in shapes],
        in_specs=[pl.BlockSpec(memory_space=pl.ANY)] * len(arrays),
        out_specs=[pl.BlockSpec(memory_space=pl.ANY)] * len(arrays),
        scratch_shapes=sc,
        compiler_params=pltpu.CompilerParams(collective_id=0, has_side_effects=True, vmem_limit_bytes=63 * 1024 * 1024),
        name="wide_sum",
    )(*arrays)


def local(
    tokens,
    caption,
    token_mask,
    cotangent,
    gain_self,
    gain_cross,
    gain_feed,
    text_proj,
    query_self,
    key_self,
    value_self,
    out_self,
    query_cross,
    key_cross,
    value_cross,
    out_cross,
    up_proj,
    down_proj,
):
    gain_one = gain_self.astype(jnp.float32)
    gain_two = gain_cross.astype(jnp.float32)
    gain_three = gain_feed.astype(jnp.float32)
    low = jnp.bfloat16

    resid_in = tokens.astype(jnp.float32)
    normed_self, inv_self = normalize(resid_in)
    image_self = group_rows((normed_self * gain_one).astype(low))
    query_sa = times_weight(image_self, query_self).astype(low)
    keys_sa = times_weight(image_self, key_self).astype(low)
    values_sa = times_weight(image_self, value_self).astype(low)
    attended_sa, total_sa = attend(query_sa, keys_sa, values_sa)
    resid_mid = resid_in + own_rows(times_weight(attended_sa, out_self))
    context = text_total(times_weight(caption, text_proj)).astype(low)
    keys_ca = times_weight(context, key_cross).astype(low)
    values_ca = times_weight(context, value_cross).astype(low)
    normed_cross, inv_cross = normalize(resid_mid)
    image_cross = group_rows((normed_cross * gain_two).astype(low))
    query_ca = times_weight(image_cross, query_cross).astype(low)
    attended_ca, total_ca = attend(query_ca, keys_ca, values_ca)
    resid_late = resid_mid + own_rows(times_weight(attended_ca, out_cross))
    normed_feed, inv_feed = normalize(resid_late)
    d_result = cotangent.astype(jnp.float32) * token_mask[:, :, None].astype(jnp.float32)
    d_image = group_rows(d_result.astype(low))
    image_feed = group_rows((normed_feed * gain_three).astype(low))
    pre_act = times_weight(image_feed, up_proj)
    gelu_out, gelu_pull = jax.vjp(jax.nn.gelu, pre_act)
    activ = gelu_out.astype(low)
    resid_out = resid_late + feed_back(times_weight(activ, down_proj))
    d_pre = gelu_pull(against(d_image, down_proj))[0].astype(low)
    part_down = contract(activ, d_image)
    part_up = contract(image_feed, d_pre)
    d_hidden_feed = feed_back(against(d_pre, up_proj))
    part_gain_feed = jnp.sum(d_hidden_feed * normed_feed, axis=(0, 1))
    d_late = d_result + norm_back(d_hidden_feed * gain_three, normed_feed, inv_feed)
    d_image_cross = group_rows(d_late.astype(low))
    part_out_cross = contract(attended_ca, d_image_cross)
    d_attended_ca = against(d_image_cross, out_cross).astype(low)
    d_query_ca, d_keys_ca, d_values_ca = attend_back(
        query_ca, keys_ca, values_ca, total_ca, d_attended_ca
    )
    part_query_cross = contract(image_cross, d_query_ca)
    part_key_cross = contract(context, d_keys_ca)
    part_value_cross = contract(context, d_values_ca)
    d_hidden_cross = own_rows(against(d_query_ca, query_cross))
    d_context = text_total(against(d_keys_ca, key_cross) + against(d_values_ca, value_cross))
    d_context = d_context.astype(low)
    part_text = contract(caption, d_context)
    d_words = against(d_context, text_proj).astype(low)
    part_gain_cross = jnp.sum(d_hidden_cross * normed_cross, axis=(0, 1))
    d_mid = d_late + norm_back(d_hidden_cross * gain_two, normed_cross, inv_cross)
    d_image_self = group_rows(d_mid.astype(low))
    part_out_self = contract(attended_sa, d_image_self)
    d_attended_sa = against(d_image_self, out_self).astype(low)
    d_query_sa, d_keys_sa, d_values_sa = attend_back(
        query_sa, keys_sa, values_sa, total_sa, d_attended_sa
    )
    part_query_self = contract(image_self, d_query_sa)
    part_key_self = contract(image_self, d_keys_sa)
    part_value_self = contract(image_self, d_values_sa)
    d_hidden_self = own_rows(
        against(d_query_sa, query_self)
        + against(d_keys_sa, key_self)
        + against(d_values_sa, value_self)
    )
    part_gain_self = jnp.sum(d_hidden_self * normed_self, axis=(0, 1))
    d_input = d_mid + norm_back(d_hidden_self * gain_one, normed_self, inv_self)
    parts = (
        part_text,
        part_query_self,
        part_key_self,
        part_value_self,
        part_out_self,
        part_query_cross,
        part_key_cross,
        part_value_cross,
        part_out_cross,
        part_up,
        part_down,
    )
    dims = (1, 0, 0, 0, 1, 0, 0, 0, 1, 0, 1)
    wide = lax.axis_size("wide")
    if wide % 2 == 0 and 4 <= wide <= 8:
        summed = wide_sum(parts, dims, wide)
    else:
        summed = [
            lax.psum_scatter(part, "wide", scatter_dimension=dim, tiled=True)
            for part, dim in zip(parts, dims)
        ]
    gains = lax.psum((part_gain_self, part_gain_cross, part_gain_feed), ("wide", "narrow"))
    return (
        resid_out.astype(low),
        d_input.astype(low),
        d_words,
        *gains,
        *[part.astype(jnp.float32) for part in summed],
    )


def solution(mesh):
    in_specs = (
        P("wide", "narrow", None),
        P("wide", None, "narrow"),
        P("wide", "narrow"),
        P("wide", "narrow", None),
        P(),
        P(),
        P(),
        P("narrow", None),
        P(None, "narrow"),
        P(None, "narrow"),
        P(None, "narrow"),
        P("narrow", None),
        P(None, "narrow"),
        P(None, "narrow"),
        P(None, "narrow"),
        P("narrow", None),
        P(None, "narrow"),
        P("narrow", None),
    )
    out_specs = (
        P("wide", "narrow", None),
        P("wide", "narrow", None),
        P("wide", None, "narrow"),
        P(),
        P(),
        P(),
        P("narrow", "wide"),
        P("wide", "narrow"),
        P("wide", "narrow"),
        P("wide", "narrow"),
        P("narrow", "wide"),
        P("wide", "narrow"),
        P("wide", "narrow"),
        P("wide", "narrow"),
        P("narrow", "wide"),
        P("wide", "narrow"),
        P("narrow", "wide"),
    )
    return jax.shard_map(local, mesh=mesh, in_specs=in_specs, out_specs=out_specs, check_vma=False)
```

time: 1780 us -> 1060 us (0.60)
  waiting for transfers between devices: 1160 us -> 283 us
  Pallas kernels: 0 us -> 396 us
  matrix products: 242 us -> 148 us
  other arithmetic: 129 us -> 40 us
  local copies, waits for them, and re-layouts: 61.2 us -> 24.7 us
    reduce_scatter x23 -> x6, waiting for transfers between devices: 1050 us -> 186 us  [own_rows(): return lax.psum_scatter(partial, 'narrow', scatter_dimension=1, tiled=True)]
    pallas_call x0 -> x1, Pallas kernels: none -> 396 us  [wide_sum(): pl.pallas_call(kernel, out_shape=[jax.ShapeDtypeStruct(s, bf) for s in sh...]
    dot_general x68 -> x34, matrix products: 168 us -> 95.5 us  [the longest x11 45.2 us: contract(): lax.dot_general(left, right, (((0, 1), (0, 1)), ((), ())), preferred_elem...]
    convert_element_type x36 -> x19, other arithmetic: 94.8 us -> 26 us  [the longest x11 13 us: local(): part.astype(jnp.float32)]
    while x328 -> x0, local copies, waits for them, and re-layouts: 57.1 us -> none
    dot_general x22 -> x11, matrix products: 74.4 us -> 52.1 us  [times_weight(): return jnp.dot(left, right, preferred_element_type=jnp.float32)]
    psum x5 -> x3, blocking collectives: 163 us -> 147 us  [the longest x2 104 us: text_total(): return lax.psum(partial, 'narrow')]
    all_gather x12 -> x6, waiting for transfers between devices: 108 us -> 96 us  [group_rows(): return lax.all_gather(piece, 'narrow', axis=1, tiled=True)]
  transfers between devices with their start and end apart: 35 -> 12, of which waited for: 26 -> 10; matrix products, arithmetic and copies ran while one was open for 14% -> 9% of each run, Pallas kernels for 0% -> 38%
where the time goes in v1:
time: 1060 us; the launch traced here: 1050 us
  Pallas kernels  396 us (37%)
  waiting for transfers between devices  283 us (27%)
  matrix products  148 us (14%)
  blocking collectives  147 us (14%)
  other arithmetic  40 us (4%)
  local copies, waits for them, and re-layouts  24.7 us (2%)
  between operations  15.3 us (1%)
    pallas_call x1, Pallas kernels, wide_sum(): pl.pallas_call(kernel, out_shape=[jax.ShapeDtypeStruct(s, bf) for s in sh...  396 us
    reduce_scatter x6, waiting for transfers between devices, own_rows(): return lax.psum_scatter(partial, 'narrow', scatter_dimension=1, tiled=True)  186 us
    psum x2, blocking collectives, text_total(): return lax.psum(partial, 'narrow')  104 us
    all_gather x6, waiting for transfers between devices, group_rows(): return lax.all_gather(piece, 'narrow', axis=1, tiled=True)  96 us
    dot_general x11, matrix products, times_weight(): return jnp.dot(left, right, preferred_element_type=jnp.float32)  52.1 us
    dot_general x11, matrix products, contract(): lax.dot_general(left, right, (((0, 1), (0, 1)), ((), ())), preferred_elem...  45.2 us
    psum x1, blocking collectives, local(): lax.psum((part_gain_self, part_gain_cross, part_gain_feed), ('wide', 'nar...  43 us
    dot_general x11, matrix products, against(): lax.dot_general(left, right, (((2,), (1,)), ((), ())), preferred_element_...  42.5 us
  transfers between devices with their start and end apart: 12, of which 10 were waited for; matrix products, arithmetic and copies ran while one was open for 9% of the time, Pallas kernels for 38%

profile of v1, /device:TPU:0, one launch (start us, length us, event | category | flops | bytes accessed | tf_op | source)
XLA Modules:
  0.0 1054.6 jit_solution(14579058047893765839)
XLA Ops:
  13.4 25.4 %all-gather.7.cloned.1.call-done = bf16[2,256,2048]{2,1,0:T(8,128)(2,1)} async-done(((bf16[2,64,2048]{2,1,0:T(8,128)(2,1)}), bf16[2,256,2048]{2,1,0:T(8,128)(2,1)}) %all-gather.7.cloned.1.call-update) | async-done | bytes 2097168 | tf_op jit(solution)/shard_map/all_gather | solution.py:93
  59.6 44.0 %reduce-scatter.7.cloned.1.call-done = f32[2,64,2048]{2,1,0:T(8,128)} async-done(((f32[2,256,2048]{2,1,0:T(8,128)}), f32[2,64,2048]{2,1,0:T(8,128)}) %reduce-scatter.7.cloned.1.call-update) | async-done | bytes 1048592 | tf_op jit(solution)/shard_map/reduce_scatter | solution.py:97
  107.1 4.8 fusion.17
  111.8 52.1 %all-reduce.3 = bf16[2,128,2048]{2,1,0:T(8,128)(2,1)} all-reduce(f32[2,128,2048]{2,1,0:T(8,128)} %fusion.17), channel_id=1, replica_groups=mesh['wide'=8,'narrow'=4] {'narrow'}, use_global_device_ids=true, to_apply=%region_5.0 | all-reduce | flops 524288 | bytes 3145728 | tf_op jit(solution)/shard_map/psum | solution.py:105
  182.5 45.2 %reduce-scatter.9.cloned.1.call-done = f32[2,64,2048]{2,1,0:T(8,128)} async-done(((f32[2,256,2048]{2,1,0:T(8,128)}), f32[2,64,2048]{2,1,0:T(8,128)}) %reduce-scatter.9.cloned.1.call-update) | async-done | bytes 1048592 | tf_op jit(solution)/shard_map/reduce_scatter | solution.py:97
  232.8 21.4 %all-gather.11.cloned.1.call-done = bf16[2,256,2048]{2,1,0:T(8,128)(2,1)} async-done(((bf16[2,64,2048]{2,1,0:T(8,128)(2,1)}), bf16[2,256,2048]{2,1,0:T(8,128)(2,1)}) %all-gather.11.cloned.1.call-update) | async-done | bytes 2097168 | tf_op jit(solution)/shard_map/all_gather | solution.py:93
  254.2 10.5 fusion.6
  264.7 14.1 %all-gather.13.cloned.1.call-done = bf16[2,256,2048]{2,1,0:T(8,128)(2,1)} async-done(((bf16[2,64,2048]{2,1,0:T(8,128)(2,1)}), bf16[2,256,2048]{2,1,0:T(8,128)(2,1)}) %all-gather.13.cloned.1.call-update) | async-done | bytes 2097168 | tf_op jit(solution)/shard_map/all_gather | solution.py:93
  278.8 11.8 %fusion.14 = bf16[2,256,2048]{2,1,0:T(8,128)(2,1)S(1)} fusion(f32[2,256,2048]{2,1,0:T(8,128)} %fusion.6, bf16[2,256,2048]{2,1,0:T(8,128)(2,1)} %all-gather.13.cloned.1.call-done, bf16[2048,2048]{1,0:T(8,128)(2,1)} %param.35), kind=kOutput, calls=%fused_computation.19 | convolution fusion | flops 4315938816 | bytes 16777216 | tf_op jit(solution)/shard_map/dot_general | solution.py:87
  291.9 9.3 fusion.20
  301.8 31.1 %reduce-scatter.13.cloned.1.call-done = bf16[2,64,2048]{2,1,0:T(8,128)(2,1)} async-done(((bf16[2,256,2048]{2,1,0:T(8,128)(2,1)}), bf16[2,64,2048]{2,1,0:T(8,128)(2,1)}) %reduce-scatter.13.cloned.1.call-update) | async-done | bytes 524304 | tf_op jit(solution)/shard_map/reduce_scatter | solution.py:97
  337.2 22.7 %all-gather.15.cloned.1.call-done = bf16[2,256,2048]{2,1,0:T(8,128)(2,1)} async-done(((bf16[2,64,2048]{2,1,0:T(8,128)(2,1)}), bf16[2,256,2048]{2,1,0:T(8,128)(2,1)}) %all-gather.15.cloned.1.call-update) | async-done | bytes 2097168 | tf_op jit(solution)/shard_map/all_gather | solution.py:93
  359.9 4.3 fusion.80
  373.6 10.8 %fusion.23 = bf16[2,256,2048]{2,1,0:T(8,128)(2,1)} fusion(bf16[2048,2048]{1,0:T(8,128)(2,1)} %param.35, f32[2,256,2048]{2,1,0:T(8,128)} %fusion.6), kind=kOutput, calls=%fused_computation.36 | convolution fusion | flops 4305453056 | bytes 14680064 | tf_op jit(solution)/shard_map/dot_general | solution.py:28
  384.5 33.7 %reduce-scatter.15.cloned.1.call-done = f32[2,64,2048]{2,1,0:T(8,128)} async-done(((f32[2,256,2048]{2,1,0:T(8,128)}), f32[2,64,2048]{2,1,0:T(8,128)}) %reduce-scatter.15.cloned.1.call-update) | async-done | bytes 1048592 | tf_op jit(solution)/shard_map/reduce_scatter | solution.py:97
  420.2 32.4 %reduce-scatter.11.cloned.1.call-done = bf16[2,64,2048]{2,1,0:T(8,128)(2,1)} async-done(((bf16[2,256,2048]{2,1,0:T(8,128)(2,1)}), bf16[2,64,2048]{2,1,0:T(8,128)(2,1)}) %reduce-scatter.11.cloned.1.call-update) | async-done | bytes 524304 | tf_op jit(solution)/shard_map/reduce_scatter | solution.py:97
  452.6 4.4 fusion.142
  457.3 10.1 bitcast_convert_fusion.1.refs_9_
  467.3 12.4 %all-gather.17.cloned.1.call-done = bf16[2,256,2048]{2,1,0:T(8,128)(2,1)} async-done(((bf16[2,64,2048]{2,1,0:T(8,128)(2,1)}), bf16[2,256,2048]{2,1,0:T(8,128)(2,1)}) %all-gather.17.cloned.1.call-update) | async-done | bytes 2097168 | tf_op jit(solution)/shard_map/all_gather | solution.py:93
  497.8 10.5 bitcast_convert_fusion.refs_10_
  522.8 52.3 %all-reduce.4 = bf16[2,128,2048]{2,1,0:T(8,128)(2,1)} all-reduce(f32[2,128,2048]{2,1,0:T(8,128)S(1)} %convolution_add_fusion), channel_id=1, replica_groups=mesh['wide'=8,'narrow'=4] {'narrow'}, use_global_device_ids=true, to_apply=%region_25.0 | all-reduce | flops 524288 | bytes 3145728 | tf_op jit(solution)/shard_map/psum | solution.py:105
  575.1 4.7 fusion.19.refs_0_
  592.6 395.5 %wide_sum.1 = (bf16[1024,256]{1,0:T(8,128)(2,1)}, bf16[256,512]{1,0:T(8,128)(2,1)}, bf16[256,512]{1,0:T(8,128)(2,1)}, bf16[256,512]{1,0:T(8,128)(2,1)}, bf16[512...) custom-call(bf16[1024,2048]{1,0:T(8,128)(2,1)} %fusion.19.refs_0_, ...), custom_call_target="tpu_custom_call" | custom-call | tf_op jit(solution)/shard_map/wide_sum/pallas_call | solution.py:405
  1003.0 43.0 %all-reduce = (f32[2048]{0:T(1024)}, f32[2048]{0:T(1024)}, f32[2048]{0:T(1024)}) all-reduce(f32[2048]{0:T(1024)S(1)} %get-tuple-element.43, f32[2048]{0:T(1024)S(1)} %get-tuple-element.39, f32[2048]{0:T(1024)S(1)} %get-tuple-element.41), channel_id=1, replica_groups=mesh['wide'=8,'narrow'=4] {'wide','narrow'}, use_global_device_ids=true, to_apply=%region_27.0 | all-reduce | flops 6144 | bytes 49152 | tf_op jit(solution)/shard_map/psum | solution.py:525
  (257 shorter events, 132.8 us)
Async XLA Ops:
  7.2 99.9 %copy-start = (bf16[2,128,1024]{2,1,0:T(8,128)(2,1)S(1)}, bf16[2,128,1024]{2,1,0:T(8,128)(2,1)}, u32[]{:S(2)}) copy-start(bf16[2,128,1024]{2,1,0:T(8,128)(2,1)} %param.19) | copy-start | bytes 1572868
  7.2 31.6 %all-gather.7.cloned.1.call-start = ((), (), s32[]{:S(2)}) async-start(), calls=%async_computation.6 | async-start | bytes 2621440 | tf_op jit(solution)/shard_map/all_gather | solution.py:93
  13.3 31.0 %copy-start.27 = (bf16[2048,512]{1,0:T(8,128)(2,1)S(1)}, bf16[2048,512]{1,0:T(8,128)(2,1)}, u32[]{:S(2)}) copy-start(bf16[2048,512]{1,0:T(8,128)(2,1)} %param.26) | copy-start | bytes 6291460
  13.3 90.2 %reduce-scatter.7.cloned.1.call-start = ((), (), s32[]{:S(2)}) async-start(), calls=%async_computation.7 | async-start | bytes 5242880 | tf_op jit(solution)/shard_map/reduce_scatter | solution.py:97
  44.3 5.9 copy-start.17
  58.9 44.7 %copy-start.7 = (bf16[2,64,2048]{2,1,0:T(8,128)(2,1)S(1)}, bf16[2,64,2048]{2,1,0:T(8,128)(2,1)}, u32[]{:S(2)}) copy-start(bf16[2,64,2048]{2,1,0:T(8,128)(2,1)} %param.18) | copy-start | bytes 1572868
  58.9 111.2 %all-gather.9.cloned.1.call-start = ((), (), s32[]{:S(2)}) async-start(), calls=%async_computation.8 | async-start | bytes 2621440 | tf_op jit(solution)/shard_map/all_gather | solution.py:93
  107.0 120.7 %reduce-scatter.9.cloned.1.call-start = ((), (), s32[]{:S(2)}) async-start(), calls=%async_computation.9 | async-start | bytes 5242880 | tf_op jit(solution)/shard_map/reduce_scatter | solution.py:97
  181.8 72.4 %all-gather.11.cloned.1.call-start = ((), (), s32[]{:S(2)}) async-start(), calls=%async_computation.10 | async-start | bytes 2621440 | tf_op jit(solution)/shard_map/all_gather | solution.py:93
  231.4 47.4 %all-gather.13.cloned.1.call-start = ((), (), s32[]{:S(2)}) async-start(), calls=%async_computation.12 | async-start | bytes 2621440 | tf_op jit(solution)/shard_map/all_gather | solution.py:93
  232.5 100.4 %reduce-scatter.13.cloned.1.call-start = ((), (), s32[]{:S(2)}) async-start(), calls=%async_computation.13 | async-start | bytes 2621440 | tf_op jit(solution)/shard_map/reduce_scatter | solution.py:97
  301.3 58.7 %all-gather.15.cloned.1.call-start = ((), (), s32[]{:S(2)}) async-start(), calls=%async_computation.14 | async-start | bytes 2621440 | tf_op jit(solution)/shard_map/all_gather | solution.py:93
  337.2 81.0 %reduce-scatter.15.cloned.1.call-start = ((), (), s32[]{:S(2)}) async-start(), calls=%async_computation.15 | async-start | bytes 5242880 | tf_op jit(solution)/shard_map/reduce_scatter | solution.py:97
  373.6 79.0 %reduce-scatter.11.cloned.1.call-start = ((), (), s32[]{:S(2)}) async-start(), calls=%async_computation.11 | async-start | bytes 2621440 | tf_op jit(solution)/shard_map/reduce_scatter | solution.py:97
  384.5 95.3 %all-gather.17.cloned.1.call-start = ((), (), s32[]{:S(2)}) async-start(), calls=%async_computation.16 | async-start | bytes 2621440 | tf_op jit(solution)/shard_map/all_gather | solution.py:93
  457.0 544.2 %reduce-scatter.17.cloned.1.call-start = ((), (), s32[]{:S(2)}) async-start(), calls=%async_computation.17 | async-start | bytes 5242880 | tf_op jit(solution)/shard_map/reduce_scatter | solution.py:97
  486.3 6.3 copy-start.37
  497.8 10.5 copy-start.13
  497.8 10.5 copy-start.15
  497.8 10.8 %copy-start.6 = (f32[2,4,256,128]{2,3,1,0:T(8,128)S(1)}, f32[2,4,256,128]{2,3,1,0:T(8,128)}, u32[]{:S(2)}) copy-start(f32[2,4,256,128]{2,3,1,0:T(8,128)} %copy-done.4) | copy-start | bytes 3145732
  497.8 10.8 %copy-start.16 = (bf16[2,256,512]{1,2,0:T(8,128)(2,1)S(1)}, bf16[2,256,512]{1,2,0:T(8,128)(2,1)}, u32[]{:S(2)}) copy-start(bf16[2,256,512]{1,2,0:T(8,128)(2,1)} %copy.110) | copy-start | bytes 1572868
  988.1 6.6 copy-start.50
  999.7 46.3 %copy-start.22 = (f32[2,64,2048]{2,1,0:T(8,128)S(1)}, f32[2,64,2048]{2,1,0:T(8,128)}, u32[]{:S(2)}) copy-start(f32[2,64,2048]{2,1,0:T(8,128)} %get-tuple-element.52) | copy-start | bytes 3145732
  1001.2 44.8 %copy-start.20 = (f32[2,64,2048]{2,1,0:T(8,128)S(1)}, f32[2,64,2048]{2,1,0:T(8,128)}, u32[]{:S(2)}) copy-start(f32[2,64,2048]{2,1,0:T(8,128)} %reduce-scatter.17.cloned.1.call-done) | copy-start | bytes 3145732
  (59 other events, 122.7 us)
Sparse Core Ops, SparseCore 0:
  13.4 25.2 all-gather.6
  59.0 44.4 reduce-scatter.6
  107.1 33.6 all-gather.8
  181.9 45.7 reduce-scatter.8
  231.6 22.5 all-gather.10
  256.2 22.5 all-gather.12
  301.4 31.4 reduce-scatter.12
  337.3 22.5 all-gather.14
  373.7 44.4 reduce-scatter.14
  421.2 31.4 reduce-scatter.10
  457.1 22.5 all-gather.16
  496.3 55.9 reduce-scatter.16

commit v2 on v1

--- a/solution.py
+++ b/solution.py
@@ -9,20 +9,6 @@
 
 HEAD = 128
 MESH = pl.DeviceIdType.MESH
-
-def normalize(rows):
-    centre = jnp.mean(rows, axis=-1, keepdims=True)
-    centred = rows - centre
-    variance = jnp.mean(centred * centred, axis=-1, keepdims=True)
-    inv_std = lax.rsqrt(variance + 1e-05)
-    return (centred * inv_std, inv_std)
-
-
-def norm_back(d_normed, normed, inv_std):
-    inner = d_normed - jnp.mean(d_normed, axis=-1, keepdims=True)
-    inner = inner - normed * jnp.mean(d_normed * normed, axis=-1, keepdims=True)
-    return inv_std * inner
-
 
 def times_weight(left, right):
     return jnp.dot(left, right, preferred_element_type=jnp.float32)
@@ -102,7 +88,343 @@
 
 
 def text_total(partial):
-    return lax.psum(partial, "narrow")
+    own = lax.psum_scatter(partial, "narrow", scatter_dimension=1, tiled=True)
+    return lax.all_gather(own.astype(jnp.bfloat16), "narrow", axis=1, tiled=True)
+
+
+VM = pl.BlockSpec(memory_space=pltpu.VMEM)
+HB = pl.BlockSpec(memory_space=pl.ANY)
+SLAB = 16
+
+
+def norm_rows(rows):
+    centre = jnp.mean(rows, axis=-1, keepdims=True)
+    centred = rows - centre
+    variance = jnp.mean(centred * centred, axis=-1, keepdims=True)
+    inv_std = lax.rsqrt(variance + 1e-05)
+    return centred * inv_std, inv_std
+
+
+def each_slab(count, step):
+    def body(i, carry):
+        step(pl.ds(pl.multiple_of(i * SLAB, SLAB), SLAB))
+        return carry
+
+    lax.fori_loop(0, count // SLAB, body, 0)
+
+
+class Narrow:
+    def __init__(self):
+        self.me = lax.axis_index("narrow")
+        self.x = self.me // 2
+        self.c = self.me % 2
+        self.core_at = self.x * 2 + 1 - self.c
+        self.chip_at = (1 - self.x) * 2 + self.c
+        self.far_at = (1 - self.x) * 2 + 1 - self.c
+        self.core = {"narrow": self.core_at}
+        self.chip = {"narrow": self.chip_at}
+
+    def meet(self):
+        barrier = pltpu.get_barrier_semaphore()
+        for peer in (self.core, self.chip):
+            pl.semaphore_signal(barrier, inc=1, device_id=peer, device_id_type=MESH)
+        pl.semaphore_wait(barrier, 2)
+
+
+def send(src, dst, sems, index, peer):
+    return pltpu.make_async_remote_copy(
+        src_ref=src,
+        dst_ref=dst,
+        send_sem=sems.at[(0,) + index],
+        recv_sem=sems.at[(1,) + index],
+        device_id=peer,
+        device_id_type=MESH,
+    )
+
+
+class Gather:
+    def __init__(self, net, held, full, sems, local_sems):
+        self.net, self.held, self.full, self.sems, self.local = net, held, full, sems, local_sems
+        self.own = held.shape[1]
+
+    def place(self, b, who):
+        return self.full.at[b, pl.ds(pl.multiple_of(who * self.own, self.own), self.own), :]
+
+    def to_core(self, b):
+        return send(self.held.at[b], self.place(b, self.net.me), self.sems, (b, 0), self.net.core)
+
+    def to_chip(self, b):
+        return send(self.held.at[b], self.place(b, self.net.me), self.sems, (b, 1), self.net.chip)
+
+    def onward(self, b):
+        block = self.place(b, self.net.chip_at)
+        return send(block, block, self.sems, (b, 2), self.net.core)
+
+    def keep(self, b):
+        return pltpu.make_async_copy(self.held.at[b], self.place(b, self.net.me), self.local.at[b])
+
+    def start(self, b):
+        self.to_chip(b).start()
+        self.to_core(b).start()
+        self.keep(b).start()
+
+    def forward(self, b):
+        self.to_chip(b).wait_recv()
+        self.onward(b).start()
+
+    def finish(self, b):
+        self.to_core(b).wait_recv()
+        self.onward(b).wait_recv()
+        self.to_core(b).wait_send()
+        self.to_chip(b).wait_send()
+        self.onward(b).wait_send()
+        self.keep(b).wait()
+
+
+class Scatter:
+    def __init__(self, net, part, landed, outgoing, arrived, sems):
+        self.net, self.part, self.landed = net, part, landed
+        self.outgoing, self.arrived, self.sems = outgoing, arrived, sems
+        self.own = part.shape[1] // 4
+
+    def rows(self, b, who):
+        return self.part.at[b, pl.ds(pl.multiple_of(who * self.own, self.own), self.own), :]
+
+    def core_copy(self, b, k):
+        who = self.net.far_at if k == 0 else self.net.core_at
+        return send(self.rows(b, who), self.landed.at[b, k], self.sems, (b, k), self.net.core)
+
+    def chip_copy(self, b):
+        return send(self.outgoing.at[b], self.arrived.at[b], self.sems, (b, 2), self.net.chip)
+
+    def start(self, b):
+        self.core_copy(b, 0).start()
+        self.core_copy(b, 1).start()
+
+    def cross(self, b):
+        self.core_copy(b, 0).wait_recv()
+        mine = self.rows(b, self.net.chip_at)
+
+        def step(s):
+            total = mine[s, :] + self.landed[b, 0, s, :]
+            self.outgoing[b, s, :] = total.astype(self.outgoing.dtype)
+
+        each_slab(self.own, step)
+        self.chip_copy(b).start()
+
+    def ready(self, b):
+        self.core_copy(b, 1).wait_recv()
+        self.chip_copy(b).wait_recv()
+
+    def total(self, b, s):
+        near = self.rows(b, self.net.me)[s, :] + self.landed[b, 1, s, :]
+        return near + self.arrived[b, s, :].astype(jnp.float32)
+
+    def finish(self, b):
+        self.core_copy(b, 0).wait_send()
+        self.core_copy(b, 1).wait_send()
+        self.chip_copy(b).wait_send()
+
+
+def scatter_scratch(images, own, width):
+    return [
+        pltpu.VMEM((images, 4 * own, width), jnp.float32),
+        pltpu.VMEM((images, 2, own, width), jnp.float32),
+        pltpu.VMEM((images, own, width), jnp.bfloat16),
+        pltpu.VMEM((images, own, width), jnp.bfloat16),
+        pltpu.SemaphoreType.DMA((2, images, 3)),
+    ]
+
+
+def gather_scratch(images, own, width):
+    return [
+        pltpu.VMEM((images, own, width), jnp.bfloat16),
+        pltpu.SemaphoreType.DMA((2, images, 3)),
+        pltpu.SemaphoreType.DMA((images,)),
+    ]
+
+
+def partial_rows(part, b, lefts, rights, transposed, tile=512):
+    width = part.shape[2]
+
+    def body(i, carry):
+        cols = pl.ds(pl.multiple_of(i * tile, tile), tile)
+        total = None
+        for left, right in zip(lefts, rights):
+            if transposed:
+                term = lax.dot_general(
+                    left[b], right[cols, :], (((1,), (1,)), ((), ())),
+                    preferred_element_type=jnp.float32,
+                )
+            else:
+                term = jnp.dot(left[b], right[:, cols], preferred_element_type=jnp.float32)
+            total = term if total is None else total + term
+        part[b, :, cols] = total
+        return carry
+
+    lax.fori_loop(0, width // tile, body, 0)
+
+
+def params(number, limit):
+    return pltpu.CompilerParams(
+        collective_id=number, has_side_effects=True, vmem_limit_bytes=limit * 1024 * 1024
+    )
+
+
+def open_rows(tokens, gain, number):
+    images, own, width = tokens.shape
+
+    def kernel(rows, gain_ref, full, held, sems, local):
+        net = Narrow()
+        net.meet()
+        gather = Gather(net, held, full, sems, local)
+        for b in range(images):
+            def step(s, b=b):
+                normed, _ = norm_rows(rows[b, s, :].astype(jnp.float32))
+                held[b, s, :] = (normed * gain_ref[...]).astype(jnp.bfloat16)
+            each_slab(own, step)
+            gather.start(b)
+        for b in range(images):
+            gather.forward(b)
+        for b in range(images):
+            gather.finish(b)
+
+    return pl.pallas_call(
+        kernel,
+        out_shape=jax.ShapeDtypeStruct((images, 4 * own, width), jnp.bfloat16),
+        in_specs=[VM, VM],
+        out_specs=HB,
+        scratch_shapes=gather_scratch(images, own, width),
+        compiler_params=params(number, 16),
+        name="open_rows",
+    )(tokens, gain)
+
+
+def forward_rows(lefts, rights, resid, gain, number):
+    images, own, width = resid.shape
+    count = len(lefts)
+
+    def kernel(*refs):
+        left_refs, right_refs = refs[:count], refs[count : 2 * count]
+        resid_ref, gain_ref, out, full = refs[2 * count : 2 * count + 4]
+        rest = refs[2 * count + 4 :]
+        net = Narrow()
+        scatter = Scatter(net, *rest[:5])
+        held, sems, local = rest[5:]
+        gather = Gather(net, held, full, sems, local)
+        net.meet()
+        for b in range(images):
+            partial_rows(scatter.part, b, left_refs, right_refs, False)
+            scatter.start(b)
+        for b in range(images):
+            scatter.cross(b)
+        for b in range(images):
+            scatter.ready(b)
+
+            def step(s, b=b):
+                rows = resid_ref[b, s, :].astype(jnp.float32) + scatter.total(b, s)
+                out[b, s, :] = rows
+                normed, _ = norm_rows(rows)
+                held[b, s, :] = (normed * gain_ref[...]).astype(jnp.bfloat16)
+
+            each_slab(own, step)
+            gather.start(b)
+        for b in range(images):
+            gather.forward(b)
+        for b in range(images):
+            scatter.finish(b)
+            gather.finish(b)
+
+    return pl.pallas_call(
+        kernel,
+        out_shape=[
+            jax.ShapeDtypeStruct((images, own, width), jnp.float32),
+            jax.ShapeDtypeStruct((images, 4 * own, width), jnp.bfloat16),
+        ],
+        in_specs=[VM] * (2 * count + 2),
+        out_specs=[VM, HB],
+        scratch_shapes=scatter_scratch(images, own, width) + gather_scratch(images, own, width),
+        compiler_params=params(number, 40),
+        name="forward_rows",
+    )(*lefts, *rights, resid, gain)
+
+
+def backward_rows(lefts, rights, above, rows_in, gain, number, masks=None, gathered=True):
+    images, own, width = rows_in.shape
+    count = len(lefts)
+    extra = [] if masks is None else [masks]
+
+    def kernel(*refs):
+        left_refs, right_refs = refs[:count], refs[count : 2 * count]
+        above_ref, rows_ref, gain_ref = refs[2 * count : 2 * count + 3]
+        refs = refs[2 * count + 3 :]
+        mask_ref = None
+        if masks is not None:
+            mask_ref, refs = refs[0], refs[1:]
+        out, gain_out = refs[:2]
+        refs = refs[2:]
+        if gathered:
+            full, refs = refs[0], refs[1:]
+        net = Narrow()
+        scatter = Scatter(net, *refs[:5])
+        if gathered:
+            held, sems, local = refs[5:]
+            gather = Gather(net, held, full, sems, local)
+        net.meet()
+        for b in range(images):
+            partial_rows(scatter.part, b, left_refs, right_refs, True)
+            scatter.start(b)
+        gain_out[...] = jnp.zeros_like(gain_out)
+        for b in range(images):
+            scatter.cross(b)
+        for b in range(images):
+            scatter.ready(b)
+
+            def step(s, b=b):
+                d_hidden = scatter.total(b, s)
+                normed, inv_std = norm_rows(rows_ref[b, s, :].astype(jnp.float32))
+                gain_out[...] += jnp.sum(d_hidden * normed, axis=0, keepdims=True)
+                top = above_ref[b, s, :].astype(jnp.float32)
+                if mask_ref is not None:
+                    top = top * mask_ref[b, s, :]
+                scaled = d_hidden * gain_ref[...]
+                inner = scaled - jnp.mean(scaled, axis=-1, keepdims=True)
+                inner = inner - normed * jnp.mean(scaled * normed, axis=-1, keepdims=True)
+                d_rows = top + inv_std * inner
+                out[b, s, :] = d_rows.astype(out.dtype)
+                if gathered:
+                    held[b, s, :] = d_rows.astype(jnp.bfloat16)
+
+            each_slab(own, step)
+            if gathered:
+                gather.start(b)
+        if gathered:
+            for b in range(images):
+                gather.forward(b)
+        for b in range(images):
+            scatter.finish(b)
+            if gathered:
+                gather.finish(b)
+
+    out_shape = [
+        jax.ShapeDtypeStruct((images, own, width), jnp.float32 if gathered else jnp.bfloat16),
+        jax.ShapeDtypeStruct((1, width), jnp.float32),
+    ]
+    out_specs = [VM, VM]
+    scratch = scatter_scratch(images, own, width)
+    if gathered:
+        out_shape.append(jax.ShapeDtypeStruct((images, 4 * own, width), jnp.bfloat16))
+        out_specs.append(HB)
+        scratch += gather_scratch(images, own, width)
+    return pl.pallas_call(
+        kernel,
+        out_shape=out_shape,
+        in_specs=[VM] * (2 * count + 3 + len(extra)),
+        out_specs=out_specs,
+        scratch_shapes=scratch,
+        compiler_params=params(number, 48),
+        name="backward_rows",
+    )(*lefts, *rights, above, rows_in, gain, *extra)
 
 
 def wide_sum(arrays, dims, wide, order=None, z_first=3, ahead=2):
@@ -433,31 +755,25 @@
     up_proj,
     down_proj,
 ):
-    gain_one = gain_self.astype(jnp.float32)
-    gain_two = gain_cross.astype(jnp.float32)
-    gain_three = gain_feed.astype(jnp.float32)
+    gain_one = gain_self.astype(jnp.float32)[None]
+    gain_two = gain_cross.astype(jnp.float32)[None]
+    gain_three = gain_feed.astype(jnp.float32)[None]
     low = jnp.bfloat16
 
-    resid_in = tokens.astype(jnp.float32)
-    normed_self, inv_self = normalize(resid_in)
-    image_self = group_rows((normed_self * gain_one).astype(low))
+    image_self = open_rows(tokens, gain_one, 1)
     query_sa = times_weight(image_self, query_self).astype(low)
     keys_sa = times_weight(image_self, key_self).astype(low)
     values_sa = times_weight(image_self, value_self).astype(low)
     attended_sa, total_sa = attend(query_sa, keys_sa, values_sa)
-    resid_mid = resid_in + own_rows(times_weight(attended_sa, out_self))
+    resid_mid, image_cross = forward_rows([attended_sa], [out_self], tokens, gain_two, 2)
     context = text_total(times_weight(caption, text_proj)).astype(low)
     keys_ca = times_weight(context, key_cross).astype(low)
     values_ca = times_weight(context, value_cross).astype(low)
-    normed_cross, inv_cross = normalize(resid_mid)
-    image_cross = group_rows((normed_cross * gain_two).astype(low))
     query_ca = times_weight(image_cross, query_cross).astype(low)
     attended_ca, total_ca = attend(query_ca, keys_ca, values_ca)
-    resid_late = resid_mid + own_rows(times_weight(attended_ca, out_cross))
-    normed_feed, inv_feed = normalize(resid_late)
-    d_result = cotangent.astype(jnp.float32) * token_mask[:, :, None].astype(jnp.float32)
-    d_image = group_rows(d_result.astype(low))
-    image_feed = group_rows((normed_feed * gain_three).astype(low))
+    resid_late, image_feed = forward_rows([attended_ca], [out_cross], resid_mid, gain_three, 3)
+    marks = token_mask[:, :, None].astype(jnp.float32)
+    d_image = group_rows((cotangent.astype(jnp.float32) * marks).astype(low))
     pre_act = times_weight(image_feed, up_proj)
     gelu_out, gelu_pull = jax.vjp(jax.nn.gelu, pre_act)
     activ = gelu_out.astype(low)
@@ -465,10 +781,9 @@
     d_pre = gelu_pull(against(d_image, down_proj))[0].astype(low)
     part_down = contract(activ, d_image)
     part_up = contract(image_feed, d_pre)
-    d_hidden_feed = feed_back(against(d_pre, up_proj))
-    part_gain_feed = jnp.sum(d_hidden_feed * normed_feed, axis=(0, 1))
-    d_late = d_result + norm_back(d_hidden_feed * gain_three, normed_feed, inv_feed)
-    d_image_cross = group_rows(d_late.astype(low))
+    d_late, part_gain_feed, d_image_cross = backward_rows(
+        [d_pre], [up_proj], cotangent, resid_late, gain_three, 4, masks=marks
+    )
     part_out_cross = contract(attended_ca, d_image_cross)
     d_attended_ca = against(d_image_cross, out_cross).astype(low)
     d_query_ca, d_keys_ca, d_values_ca = attend_back(
@@ -477,14 +792,13 @@
     part_query_cross = contract(image_cross, d_query_ca)
     part_key_cross = contract(context, d_keys_ca)
     part_value_cross = contract(context, d_values_ca)
-    d_hidden_cross = own_rows(against(d_query_ca, query_cross))
+    d_mid, part_gain_cross, d_image_self = backward_rows(
+        [d_query_ca], [query_cross], d_late, resid_mid, gain_two, 5
+    )
     d_context = text_total(against(d_keys_ca, key_cross) + against(d_values_ca, value_cross))
     d_context = d_context.astype(low)
     part_text = contract(caption, d_context)
     d_words = against(d_context, text_proj).astype(low)
-    part_gain_cross = jnp.sum(d_hidden_cross * normed_cross, axis=(0, 1))
-    d_mid = d_late + norm_back(d_hidden_cross * gain_two, normed_cross, inv_cross)
-    d_image_self = group_rows(d_mid.astype(low))
     part_out_self = contract(attended_sa, d_image_self)
     d_attended_sa = against(d_image_self, out_self).astype(low)
     d_query_sa, d_keys_sa, d_values_sa = attend_back(
@@ -493,13 +807,15 @@
     part_query_self = contract(image_self, d_query_sa)
     part_key_self = contract(image_self, d_keys_sa)
     part_value_self = contract(image_self, d_values_sa)
-    d_hidden_self = own_rows(
-        against(d_query_sa, query_self)
-        + against(d_keys_sa, key_self)
-        + against(d_values_sa, value_self)
-    )
-    part_gain_self = jnp.sum(d_hidden_self * normed_self, axis=(0, 1))
-    d_input = d_mid + norm_back(d_hidden_self * gain_one, normed_self, inv_self)
+    d_input, part_gain_self = backward_rows(
+        [d_query_sa, d_keys_sa, d_values_sa],
+        [query_self, key_self, value_self],
+        d_mid,
+        tokens,
+        gain_one,
+        6,
+        gathered=False,
+    )
     parts = (
         part_text,
         part_query_self,
@@ -522,10 +838,10 @@
             lax.psum_scatter(part, "wide", scatter_dimension=dim, tiled=True)
             for part, dim in zip(parts, dims)
         ]
-    gains = lax.psum((part_gain_self, part_gain_cross, part_gain_feed), ("wide", "narrow"))
+    gains = lax.psum((part_gain_self[0], part_gain_cross[0], part_gain_feed[0]), ("wide", "narrow"))
     return (
         resid_out.astype(low),
-        d_input.astype(low),
+        d_input,
         d_words,
         *gains,
         *[part.astype(jnp.float32) for part in summed],

time: 1060 us -> 863 us (0.81)
  waiting for transfers between devices: 283 us -> 40.1 us
  Pallas kernels: 396 us -> 582 us
  blocking collectives: 147 us -> 40.2 us
  matrix products: 148 us -> 121 us
  other arithmetic: 40 us -> 20.7 us
    pallas_call x0 -> x6, Pallas kernels: none -> 187 us  [the longest x3 103 us: backward_rows(): pl.pallas_call(kernel, out_shape=out_shape, in_specs=[VM] * (2 * count +...]
    reduce_scatter x6 -> x1, waiting for transfers between devices: 186 us -> 0.01 us  [own_rows(): return lax.psum_scatter(partial, 'narrow', scatter_dimension=1, tiled=True)]
    psum x3 -> x1, blocking collectives: 147 us -> 40.2 us  [local(): lax.psum((part_gain_self[0], part_gain_cross[0], part_gain_feed[0]), ('wi...]
    all_gather x6 -> x1, waiting for transfers between devices: 96 us -> 0.01 us  [group_rows(): return lax.all_gather(piece, 'narrow', axis=1, tiled=True)]
    reduce_scatter x0 -> x2, waiting for transfers between devices: none -> 34.3 us  [text_total(): own = lax.psum_scatter(partial, 'narrow', scatter_dimension=1, tiled=True)]
    dot_general x11 -> x6, matrix products: 42.5 us -> 21.6 us  [against(): lax.dot_general(left, right, (((2,), (1,)), ((), ())), preferred_element_...]
    reduce_sum x9 -> x0, other arithmetic: 11.9 us -> none  [the longest x3 4.4 us: normalize(): centre = jnp.mean(rows, axis=-1, keepdims=True)]
    dot_general x11 -> x9, matrix products: 52.1 us -> 41.2 us  [times_weight(): return jnp.dot(left, right, preferred_element_type=jnp.float32)]
  transfers between devices with their start and end apart: 12 -> 6, of which waited for: 10 -> 2; matrix products, arithmetic and copies ran while one was open for 9% -> 12% of each run, Pallas kernels for 38% -> 18%
where the time goes in v2:
time: 863 us; the launch traced here: 854 us
  Pallas kernels  582 us (67%)
  matrix products  121 us (14%)
  blocking collectives  40.2 us (5%)
  waiting for transfers between devices  40.1 us (5%)
  local copies, waits for them, and re-layouts  34.8 us (4%)
  other arithmetic  20.7 us (2%)
  between operations  15.1 us (2%)
    pallas_call x1, Pallas kernels, wide_sum(): pl.pallas_call(kernel, out_shape=[jax.ShapeDtypeStruct(s, bf) for s in sh...  395 us
    pallas_call x3, Pallas kernels, backward_rows(): pl.pallas_call(kernel, out_shape=out_shape, in_specs=[VM] * (2 * count +...  103 us
    pallas_call x2, Pallas kernels, forward_rows(): pl.pallas_call(kernel, out_shape=[jax.ShapeDtypeStruct((images, own, widt...  62.3 us
    dot_general x11, matrix products, contract(): lax.dot_general(left, right, (((0, 1), (0, 1)), ((), ())), preferred_elem...  42.4 us
    dot_general x9, matrix products, times_weight(): return jnp.dot(left, right, preferred_element_type=jnp.float32)  41.2 us
    psum x1, blocking collectives, local(): lax.psum((part_gain_self[0], part_gain_cross[0], part_gain_feed[0]), ('wi...  40.2 us
    reduce_scatter x2, waiting for transfers between devices, text_total(): own = lax.psum_scatter(partial, 'narrow', scatter_dimension=1, tiled=True)  34.3 us
    unnamed x151, local copies, waits for them, and re-layouts  24.9 us
  transfers between devices with their start and end apart: 6, of which 2 were waited for; matrix products, arithmetic and copies ran while one was open for 12% of the time, Pallas kernels for 18%

profile of v2, /device:TPU:0, one launch (start us, length us, event | category | flops | bytes accessed | tf_op | source)
XLA Modules:
  0.0 853.8 jit_solution(2952879247851109401)
XLA Ops:
  8.2 4.8 fusion.15
  13.1 34.2 %reduce-scatter.4.cloned.1.call-done = f32[2,32,2048]{2,1,0:T(8,128)} async-done(((f32[2,128,2048]{2,1,0:T(8,128)}), f32[2,32,2048]{2,1,0:T(8,128)}) %reduce-scatter.4.cloned.1.call-update) | async-done | bytes 524304 | tf_op jit(solution)/shard_map/reduce_scatter | solution.py:91
  50.4 21.4 %open_rows.1 = bf16[2,256,2048]{2,1,0:T(8,128)(2,1)S(1)} custom-call(bf16[2,64,2048]{2,1,0:T(8,128)(2,1)S(1)} %copy-done.1, f32[1,2048]{1,0:T(1,128)S(1)} %bitcast.208), custom_call_target="tpu_custom_call" | custom-call | tf_op jit(solution)/shard_map/open_rows/pallas_call | solution.py:292
  71.9 3.6 fusion.68
  77.0 4.5 fusion.49
  87.2 31.9 %forward_rows.2 = (f32[2,64,2048]{2,1,0:T(8,128)S(1)}, bf16[2,256,2048]{2,1,0:T(8,128)(2,1)S(1)}) custom-call(bf16[2,256,512]{2,1,0:T(8,128)(2,1)S(1)} %copy.100.refs_0_, bf16[512,2048]{1,0:T(8,128)(2,1)S(1)} %copy-done.9, bf16[2,64,2048]{2,1,0:T(8,128)(2,1)S(1)} %copy-done.1, f32[1,2048]{1,0:T(1,128)S(1)} %bitcast.206), custom_call_target="tpu_custom_call" | custom-call | tf_op jit(solution)/shard_map/forward_rows/pallas_call | solution.py:338
  123.8 2.8 fusion.75
  134.4 30.4 %forward_rows.3 = (f32[2,64,2048]{2,1,0:T(8,128)S(1)}, bf16[2,256,2048]{2,1,0:T(8,128)(2,1)}) custom-call(bf16[2,256,512]{2,1,0:T(8,128)(2,1)S(1)} %copy.101.refs_0_, bf16[512,2048]{1,0:T(8,128)(2,1)S(1)} %copy-done.5, f32[2,64,2048]{2,1,0:T(8,128)S(1)} %get-tuple-element.41.refs_2_.refs_3_, f32[1,2048]{1,0:T(1,128)S(1)} %bitcast.210), custom_call_target="tpu_custom_call" | custom-call | tf_op jit(solution)/shard_map/forward_rows/pallas_call | solution.py:338
  165.8 10.5 %fusion.4 = f32[2,256,2048]{2,1,0:T(8,128)} fusion(bf16[2,256,2048]{2,1,0:T(8,128)(2,1)} %get-tuple-element.43, bf16[2048,2048]{1,0:T(8,128)(2,1)} %refs_1_.6), kind=kOutput, calls=%fused_computation.7 | convolution fusion | flops 4294967296 | bytes 14680064 | tf_op jit(solution)/shard_map/dot_general | solution.py:14
  176.3 13.3 %fusion.12.refs_0_ = bf16[2,256,2048]{2,1,0:T(8,128)(2,1)} fusion(f32[2,256,2048]{2,1,0:T(8,128)} %fusion.4, bf16[2,256,2048]{2,1,0:T(8,128)(2,1)} %all-gather.6.cloned.1.call-done, bf16[2048,2048]{1,0:T(8,128)(2,1)} %param.35), kind=kOutput, calls=%fused_computation.17 | convolution fusion | flops 4315938816 | bytes 16777216 | tf_op jit(solution)/shard_map/dot_general | solution.py:73
  189.5 37.0 %backward_rows.3 = (f32[2,64,2048]{2,1,0:T(8,128)S(1)}, f32[1,2048]{1,0:T(1,128)S(1)}, bf16[2,256,2048]{2,1,0:T(8,128)(2,1)S(1)}) custom-call(bf16[2,256,2048]{2,1,0:T(8,128)(2,1)} %fusion.12.refs_0_, bf16[2048,2048]{1,0:T(8,128)(2,1)} %refs_1_.6, bf16[2,64,2048]{2,1,0:T(8,128)(2,1)S(1)} %copy-done.13, f32[2,64,2048]{2,1,0:T(8,128)S(1)} %copy-done.3, ...), custom_call_target="tpu_custom_call" | custom-call | tf_op jit(solution)/shard_map/backward_rows/pallas_call | solution.py:419
  246.2 43.3 %backward_rows.4 = (f32[2,64,2048]{2,1,0:T(8,128)S(1)}, f32[1,2048]{1,0:T(1,128)S(1)}, bf16[2,256,2048]{2,1,0:T(8,128)(2,1)S(1)}) custom-call(bf16[2,256,512]{2,1,0:T(8,128)(2,1)S(1)} %copy.102.refs_0_, bf16[2048,512]{1,0:T(8,128)(2,1)} %refs_1_.7, f32[2,64,2048]{2,1,0:T(8,128)S(1)} %copy-done.15, f32[2,64,2048]{2,1,0:T(8,128)S(1)} %get-tuple-element.41.refs_2_.refs_3_, ...), custom_call_target="tpu_custom_call" | custom-call | tf_op jit(solution)/shard_map/backward_rows/pallas_call | solution.py:419
  308.3 22.9 %backward_rows.5 = (bf16[2,64,2048]{2,1,0:T(8,128)(2,1)S(1)}, f32[1,2048]{1,0:T(1,128)S(1)}) custom-call(bf16[2,256,512]{2,1,0:T(8,128)(2,1)S(1)} %copy.103.refs_0_, bf16[2,256,512]{2,1,0:T(8,128)(2,1)S(1)} %copy.104.refs_1_, bf16[2,256,512]{2,1,0:T(8,128)(2,1)S(1)} %copy.105.refs_2_, bf16[2048,512]{1,0:T(8,128)(2,1)S(1)} %copy-done.11, ...), custom_call_target="tpu_custom_call" | custom-call | tf_op jit(solution)/shard_map/backward_rows/pallas_call | solution.py:419
  332.0 9.5 %fusion.18 = bf16[2,256,2048]{2,1,0:T(8,128)(2,1)} fusion(bf16[2048,2048]{1,0:T(8,128)(2,1)} %param.35, f32[2,256,2048]{2,1,0:T(8,128)S(1)} %copy-done.73), kind=kOutput, calls=%fused_computation.32 | convolution fusion | flops 4305453056 | bytes 14680064 | tf_op jit(solution)/shard_map/dot_general | solution.py:14
  341.6 40.2 %all-reduce = (f32[2048]{0:T(1024)}, f32[2048]{0:T(1024)}, f32[2048]{0:T(1024)}) all-reduce(f32[2048]{0:T(1024)S(1)} %bitcast.214, f32[2048]{0:T(1024)S(1)} %bitcast.213, f32[2048]{0:T(1024)S(1)} %bitcast.212), channel_id=1, replica_groups=mesh['wide'=8,'narrow'=4] {'wide','narrow'}, use_global_device_ids=true, to_apply=%region_9.0 | all-reduce | flops 6144 | bytes 49152 | tf_op jit(solution)/shard_map/psum | solution.py:841
  388.6 2.8 bitcast_convert_fusion.6.refs_5_
  394.0 2.6 bitcast_convert_fusion.10.refs_1_
  396.7 2.6 bitcast_convert_fusion.9.refs_2_
  399.3 2.6 bitcast_convert_fusion.8.refs_3_
  402.9 7.6 bitcast_convert_fusion.refs_10_
  412.3 10.2 %bitcast_convert_fusion.1.refs_9_ = bf16[2048,2048]{1,0:T(8,128)(2,1)} fusion(bf16[2,256,2048]{2,1,0:T(8,128)(2,1)} %get-tuple-element.43, bf16[2,256,2048]{2,1,0:T(8,128)(2,1)} %fusion.12.refs_0_), kind=kOutput, calls=%fused_computation.1 | convolution fusion | flops 4299161600 | bytes 12582912 | tf_op jit(solution)/shard_map/dot_general | solution.py:67
  424.4 5.8 all-gather.8.cloned.1.call-done
  430.2 4.5 fusion.17.refs_0_
  434.7 395.0 %wide_sum.1 = (bf16[1024,256]{1,0:T(8,128)(2,1)}, bf16[256,512]{1,0:T(8,128)(2,1)}, bf16[256,512]{1,0:T(8,128)(2,1)}, bf16[256,512]{1,0:T(8,128)(2,1)}, bf16[512...) custom-call(bf16[1024,2048]{1,0:T(8,128)(2,1)} %fusion.17.refs_0_, ...), custom_call_target="tpu_custom_call" | custom-call | tf_op jit(solution)/shard_map/wide_sum/pallas_call | solution.py:727
  (229 shorter events, 94.8 us)
Async XLA Ops:
  7.2 40.1 %reduce-scatter.4.cloned.1.call-start = ((), (), s32[]{:S(2)}) async-start(), calls=%async_computation.3 | async-start | bytes 2621440 | tf_op jit(solution)/shard_map/reduce_scatter | solution.py:91
  13.0 36.2 %copy-start.71 = (s32[2,64]{1,0:T(2,128)S(1)}, s32[2,64]{1,0:T(2,128)}, u32[]{:S(2)}) copy-start(s32[2,64]{1,0:T(2,128)} %param.20) | copy-start | bytes 1540
  13.0 36.2 %copy-start.12 = (bf16[2,64,2048]{2,1,0:T(8,128)(2,1)S(1)}, bf16[2,64,2048]{2,1,0:T(8,128)(2,1)}, u32[]{:S(2)}) copy-start(bf16[2,64,2048]{2,1,0:T(8,128)(2,1)} %refs_2_.3) | copy-start | bytes 1572868
  13.0 37.3 %copy-start.68 = (bf16[2048]{0:T(1024)(128)(2,1)S(1)}, bf16[2048]{0:T(1024)(128)(2,1)}, u32[]{:S(2)}) copy-start(bf16[2048]{0:T(1024)(128)(2,1)} %param.22) | copy-start | bytes 12292
  13.0 37.3 %copy-start.69 = (bf16[2048]{0:T(1024)(128)(2,1)S(1)}, bf16[2048]{0:T(1024)(128)(2,1)}, u32[]{:S(2)}) copy-start(bf16[2048]{0:T(1024)(128)(2,1)} %param.23) | copy-start | bytes 12292
  13.0 37.3 %copy-start.70 = (bf16[2048]{0:T(1024)(128)(2,1)S(1)}, bf16[2048]{0:T(1024)(128)(2,1)}, u32[]{:S(2)}) copy-start(bf16[2048]{0:T(1024)(128)(2,1)} %param.24) | copy-start | bytes 12292
  13.0 37.4 %copy-start.1 = (bf16[2,64,2048]{2,1,0:T(8,128)(2,1)S(1)}, bf16[2,64,2048]{2,1,0:T(8,128)(2,1)}, u32[]{:S(2)}) copy-start(bf16[2,64,2048]{2,1,0:T(8,128)(2,1)} %refs_7_.1) | copy-start | bytes 1572868
  13.1 110.8 %all-gather.4.cloned.1.call-start = ((), (), s32[]{:S(2)}) async-start(), calls=%async_computation.4 | async-start | bytes 1310720 | tf_op jit(solution)/shard_map/all_gather | solution.py:92
  49.1 127.1 %all-gather.6.cloned.1.call-start = ((), (), s32[]{:S(2)}) async-start(), calls=%async_computation.6 | async-start | bytes 2621440 | tf_op jit(solution)/shard_map/all_gather | solution.py:79
  50.2 360.3 %reduce-scatter.8.cloned.1.call-start = ((), (), s32[]{:S(2)}) async-start(), calls=%async_computation.7 | async-start | bytes 2621440 | tf_op jit(solution)/shard_map/reduce_scatter | solution.py:91
  75.6 8.3 copy-start.56
  77.0 5.9 copy-start.36
  87.2 33.3 %copy-start.47 = (bf16[2048,512]{1,0:T(8,128)(2,1)S(1)}, bf16[2048,512]{1,0:T(8,128)(2,1)}, u32[]{:S(2)}) copy-start(bf16[2048,512]{1,0:T(8,128)(2,1)} %refs_1_.7) | copy-start | bytes 6291460
  176.2 13.3 %copy-start.13 = (bf16[2,64,2048]{2,1,0:T(8,128)(2,1)S(1)}, bf16[2,64,2048]{2,1,0:T(8,128)(2,1)}, u32[]{:S(2)}) copy-start(bf16[2,64,2048]{2,1,0:T(8,128)(2,1)} %refs_2_.3) | copy-start | bytes 1572868
  176.3 13.3 %copy-start.3 = (f32[2,64,2048]{2,1,0:T(8,128)S(1)}, f32[2,64,2048]{2,1,0:T(8,128)}, u32[]{:S(2)}) copy-start(f32[2,64,2048]{2,1,0:T(8,128)} %copy-done.2) | copy-start | bytes 3145732
  189.5 39.4 %copy-start.6 = (bf16[512,2048]{1,0:T(8,128)(2,1)S(1)}, bf16[512,2048]{1,0:T(8,128)(2,1)}, u32[]{:S(2)}) copy-start(bf16[512,2048]{1,0:T(8,128)(2,1)} %refs_1_.5) | copy-start | bytes 6291460
  241.6 180.8 %reduce-scatter.6.cloned.1.call-start = ((), (), s32[]{:S(2)}) async-start(), calls=%async_computation.5 | async-start | bytes 2621440 | tf_op jit(solution)/shard_map/reduce_scatter | solution.py:83
  246.2 45.6 %copy-start.10 = (bf16[512,2048]{1,0:T(8,128)(2,1)S(1)}, bf16[512,2048]{1,0:T(8,128)(2,1)}, u32[]{:S(2)}) copy-start(bf16[512,2048]{1,0:T(8,128)(2,1)} %refs_1_.4) | copy-start | bytes 6291460
  308.3 23.7 %copy-start.73 = (f32[2,256,2048]{2,1,0:T(8,128)S(1)}, f32[2,256,2048]{2,1,0:T(8,128)}, u32[]{:S(2)}) copy-start(f32[2,256,2048]{2,1,0:T(8,128)} %fusion.4) | copy-start | bytes 12582916
  341.5 40.3 %copy-start.40 = (bf16[2,128,2048]{2,1,0:T(8,128)(2,1)S(1)}, bf16[2,128,2048]{2,1,0:T(8,128)(2,1)}, u32[]{:S(2)}) copy-start(bf16[2,128,2048]{2,1,0:T(8,128)(2,1)} %all-gather.4.cloned.1.call-done) | copy-start | bytes 3145732
  341.5 40.3 %copy-start.44 = (bf16[2,4,128,128]{3,2,1,0:T(8,128)(2,1)S(1)}, bf16[2,4,128,128]{3,2,1,0:T(8,128)(2,1)}, u32[]{:S(2)}) copy-start(bf16[2,4,128,128]{3,2,1,0:T(8,128)(2,1)} %copy-done.43) | copy-start | bytes 786436
  341.5 88.7 %all-gather.8.cloned.1.call-start = ((), (), s32[]{:S(2)}) async-start(), calls=%async_computation.8 | async-start | bytes 1310720 | tf_op jit(solution)/shard_map/all_gather | solution.py:92
  412.3 10.2 %copy-start.4 = (f32[2,64,2048]{2,1,0:T(8,128)S(1)}, f32[2,64,2048]{2,1,0:T(8,128)}, u32[]{:S(2)}) copy-start(f32[2,64,2048]{2,1,0:T(8,128)} %copy-done.2) | copy-start | bytes 3145732
  829.8 6.6 copy-start.63
  (57 other events, 129.6 us)
Sparse Core Ops, SparseCore 0:
  13.2 34.1 reduce-scatter.3
  49.6 21.8 all-gather.3
  73.7 25.1 all-gather.5
  241.8 42.8 reduce-scatter.7
  341.6 31.5 reduce-scatter.5
  412.4 17.7 all-gather.7

commit v3 on v1

v3 whole, which is shorter than its diff:
```python
import math
import types

import jax
import jax.numpy as jnp
from jax import lax
from jax.experimental import pallas as pl
from jax.experimental.pallas import tpu as pltpu
from jax.sharding import PartitionSpec as P

HEAD = 128
MESH = pl.DeviceIdType.MESH
WIDE, NARROW = "wide", "narrow"
LOW, F32 = jnp.bfloat16, jnp.float32
LAST, FIRST = (((1,), (1,)), ((), ())), (((0,), (0,)), ((), ()))

def normalize(rows):
    centre = jnp.mean(rows, axis=-1, keepdims=True)
    centred = rows - centre
    variance = jnp.mean(centred * centred, axis=-1, keepdims=True)
    inv_std = lax.rsqrt(variance + 1e-05)
    return (centred * inv_std, inv_std)


def norm_back(d_normed, normed, inv_std):
    inner = d_normed - jnp.mean(d_normed, axis=-1, keepdims=True)
    inner = inner - normed * jnp.mean(d_normed * normed, axis=-1, keepdims=True)
    return inv_std * inner


def times_weight(left, right):
    return jnp.dot(left, right, preferred_element_type=jnp.float32)


def split_heads(matrix):
    return matrix.reshape(matrix.shape[0], matrix.shape[1], matrix.shape[2] // HEAD, HEAD)


def join_heads(heads):
    return heads.reshape(heads.shape[0], heads.shape[1], heads.shape[2] * HEAD)


def head_scores(query, keys):
    scores = jnp.einsum(
        "bqhe,bkhe->bhqk", split_heads(query), split_heads(keys), preferred_element_type=jnp.float32
    )
    return scores * (1.0 / math.sqrt(HEAD))


def attend(query, keys, values):
    scores = head_scores(query, keys)
    peak = jnp.max(scores, axis=-1, keepdims=True)
    powers = jnp.exp(scores - peak)
    summed = jnp.sum(powers, axis=-1, keepdims=True)
    low_probs = (powers / summed).astype(jnp.bfloat16)
    attended = jnp.einsum(
        "bhqk,bkhe->bqhe", low_probs, split_heads(values), preferred_element_type=jnp.float32
    )
    return join_heads(attended).astype(jnp.bfloat16), peak + jnp.log(summed)


def attend_back(query, keys, values, log_total, d_attended):
    probs = jnp.exp(head_scores(query, keys) - log_total)
    low_probs = probs.astype(jnp.bfloat16)
    d_heads = split_heads(d_attended)
    d_probs = jnp.einsum(
        "bqhe,bkhe->bhqk", d_heads, split_heads(values), preferred_element_type=jnp.float32
    )
    d_values = jnp.einsum("bhqk,bqhe->bkhe", low_probs, d_heads, preferred_element_type=jnp.float32)
    weighted = jnp.sum(probs * d_probs, axis=-1, keepdims=True)
    d_scores = (probs * (d_probs - weighted)).astype(jnp.bfloat16)
    scale = 1.0 / math.sqrt(HEAD)
    d_query = (
        jnp.einsum("bhqk,bkhe->bqhe", d_scores, split_heads(keys), preferred_element_type=jnp.float32)
        * scale
    )
    d_keys = (
        jnp.einsum("bhqk,bqhe->bkhe", d_scores, split_heads(query), preferred_element_type=jnp.float32)
        * scale
    )
    return tuple(join_heads(d).astype(jnp.bfloat16) for d in (d_query, d_keys, d_values))


def contract(left, right):
    return lax.dot_general(
        left, right, (((0, 1), (0, 1)), ((), ())), preferred_element_type=jnp.float32
    ).astype(jnp.bfloat16)


def against(left, right):
    return lax.dot_general(
        left, right, (((2,), (1,)), ((), ())), preferred_element_type=jnp.float32
    )


def group_rows(piece):
    return lax.all_gather(piece, NARROW, axis=1, tiled=True)


def own_rows(partial):
    return lax.psum_scatter(partial, NARROW, scatter_dimension=1, tiled=True)


def feed_back(partial):
    return own_rows(partial.astype(jnp.bfloat16)).astype(jnp.float32)


def text_total(partial):
    return lax.psum(partial, NARROW)


def by_collectives(
    tokens,
    caption,
    token_mask,
    cotangent,
    gain_self,
    gain_cross,
    gain_feed,
    text_proj,
    query_self,
    key_self,
    value_self,
    out_self,
    query_cross,
    key_cross,
    value_cross,
    out_cross,
    up_proj,
    down_proj,
):
    gain_one = gain_self.astype(jnp.float32)
    gain_two = gain_cross.astype(jnp.float32)
    gain_three = gain_feed.astype(jnp.float32)
    low = jnp.bfloat16

    resid_in = tokens.astype(jnp.float32)
    normed_self, inv_self = normalize(resid_in)
    image_self = group_rows((normed_self * gain_one).astype(low))
    query_sa = times_weight(image_self, query_self).astype(low)
    keys_sa = times_weight(image_self, key_self).astype(low)
    values_sa = times_weight(image_self, value_self).astype(low)
    attended_sa, total_sa = attend(query_sa, keys_sa, values_sa)
    resid_mid = resid_in + own_rows(times_weight(attended_sa, out_self))
    context = text_total(times_weight(caption, text_proj)).astype(low)
    keys_ca = times_weight(context, key_cross).astype(low)
    values_ca = times_weight(context, value_cross).astype(low)
    normed_cross, inv_cross = normalize(resid_mid)
    image_cross = group_rows((normed_cross * gain_two).astype(low))
    query_ca = times_weight(image_cross, query_cross).astype(low)
    attended_ca, total_ca = attend(query_ca, keys_ca, values_ca)
    resid_late = resid_mid + own_rows(times_weight(attended_ca, out_cross))
    normed_feed, inv_feed = normalize(resid_late)
    d_result = cotangent.astype(jnp.float32) * token_mask[:, :, None].astype(jnp.float32)
    d_image = group_rows(d_result.astype(low))
    image_feed = group_rows((normed_feed * gain_three).astype(low))
    pre_act = times_weight(image_feed, up_proj)
    gelu_out, gelu_pull = jax.vjp(jax.nn.gelu, pre_act)
    activ = gelu_out.astype(low)
    resid_out = resid_late + feed_back(times_weight(activ, down_proj))
    d_pre = gelu_pull(against(d_image, down_proj))[0].astype(low)
    part_down = contract(activ, d_image)
    part_up = contract(image_feed, d_pre)
    d_hidden_feed = feed_back(against(d_pre, up_proj))
    part_gain_feed = jnp.sum(d_hidden_feed * normed_feed, axis=(0, 1))
    d_late = d_result + norm_back(d_hidden_feed * gain_three, normed_feed, inv_feed)
    d_image_cross = group_rows(d_late.astype(low))
    part_out_cross = contract(attended_ca, d_image_cross)
    d_attended_ca = against(d_image_cross, out_cross).astype(low)
    d_query_ca, d_keys_ca, d_values_ca = attend_back(
        query_ca, keys_ca, values_ca, total_ca, d_attended_ca
    )
    part_query_cross = contract(image_cross, d_query_ca)
    part_key_cross = contract(context, d_keys_ca)
    part_value_cross = contract(context, d_values_ca)
    d_hidden_cross = own_rows(against(d_query_ca, query_cross))
    d_context = text_total(against(d_keys_ca, key_cross) + against(d_values_ca, value_cross))
    d_context = d_context.astype(low)
    part_text = contract(caption, d_context)
    d_words = against(d_context, text_proj).astype(low)
    part_gain_cross = jnp.sum(d_hidden_cross * normed_cross, axis=(0, 1))
    d_mid = d_late + norm_back(d_hidden_cross * gain_two, normed_cross, inv_cross)
    d_image_self = group_rows(d_mid.astype(low))
    part_out_self = contract(attended_sa, d_image_self)
    d_attended_sa = against(d_image_self, out_self).astype(low)
    d_query_sa, d_keys_sa, d_values_sa = attend_back(
        query_sa, keys_sa, values_sa, total_sa, d_attended_sa
    )
    part_query_self = contract(image_self, d_query_sa)
    part_key_self = contract(image_self, d_keys_sa)
    part_value_self = contract(image_self, d_values_sa)
    d_hidden_self = own_rows(
        against(d_query_sa, query_self)
        + against(d_keys_sa, key_self)
        + against(d_values_sa, value_self)
    )
    part_gain_self = jnp.sum(d_hidden_self * normed_self, axis=(0, 1))
    d_input = d_mid + norm_back(d_hidden_self * gain_one, normed_self, inv_self)
    parts = (
        part_text,
        part_query_self,
        part_key_self,
        part_value_self,
        part_out_self,
        part_query_cross,
        part_key_cross,
        part_value_cross,
        part_out_cross,
        part_up,
        part_down,
    )
    dims = (1, 0, 0, 0, 1, 0, 0, 0, 1, 0, 1)
    summed = [
        lax.psum_scatter(part, WIDE, scatter_dimension=dim, tiled=True)
        for part, dim in zip(parts, dims)
    ]
    gains = lax.psum((part_gain_self, part_gain_cross, part_gain_feed), (WIDE, NARROW))
    return (
        resid_out.astype(low),
        d_input.astype(low),
        d_words,
        *gains,
        *[part.astype(jnp.float32) for part in summed],
    )


RING = 6
HELD = 7


def send(src, dst, sems, index, peer):
    return pltpu.make_async_remote_copy(
        src_ref=src,
        dst_ref=dst,
        send_sem=sems.at[(0,) + index],
        recv_sem=sems.at[(1,) + index],
        device_id=peer,
        device_id_type=MESH,
    )


def greet(barrier, peer):
    pl.semaphore_signal(barrier, inc=1, device_id=peer, device_id_type=MESH)


def each_slab(count, step, slab=16):
    def body(i, carry):
        step(pl.ds(pl.multiple_of(i * slab, slab), slab))
        return carry

    lax.fori_loop(0, count // slab, body, 0)


class Wide:
    def __init__(self, pairs, units, refs):
        (self.mine, self.theirs, self.fromy, self.right, self.left, self.stage,
         self.aslot, self.bslot, self.ysem, self.rsem, self.lsem, self.asem, self.bsem,
         self.osem, self.rfree, self.lfree) = refs
        self.pairs, self.units = pairs, units
        me = lax.axis_index(WIDE)
        self.z, self.y = me // 2, me % 2
        self.has_right, self.has_left = self.z < pairs - 1, self.z > 0
        self.peer = {WIDE: self.z * 2 + 1 - self.y}
        self.next = {WIDE: jnp.minimum(self.z + 1, pairs - 1) * 2 + self.y}
        self.last = {WIDE: jnp.maximum(self.z - 1, 0) * 2 + self.y}
        self.summed = [i for i, unit in enumerate(units) if not unit.trade]
        group = -1
        for i, unit in enumerate(units):
            if i == 0 or unit.rows is not units[i - 1].rows:
                group += 1
            unit.group = group
        self.blk, self.cols = self.mine.shape[2], self.mine.shape[3]

    def meet(self, barrier):
        greet(barrier, self.peer)

        @pl.when(self.has_right)
        def _():
            greet(barrier, self.next)

        @pl.when(self.has_left)
        def _():
            greet(barrier, self.last)

        return 1 + self.has_right.astype(jnp.int32) + self.has_left.astype(jnp.int32)

    def trade(self, i):
        unit = self.units[i]
        return send(unit.columns, unit.nb_columns, unit.sems, (i,), self.peer)

    def loads(self, i):
        unit = self.units[i]
        s, rows = unit.group % 2, unit.count
        copies = []
        if i == 0 or self.units[i - 1].group != unit.group:
            for k in range(self.pairs):
                for part in (0, 1):
                    if part == 0 or not unit.trade:
                        at = (k * 2 + (self.y if part == 0 else 1 - self.y)) * self.blk
                        src = unit.rows.at[:, pl.ds(pl.multiple_of(at, self.blk), self.blk)]
                    else:
                        src = unit.nb_rows.at[:, pl.ds(k * self.blk, self.blk)]
                    copies.append(
                        pltpu.make_async_copy(
                            src, self.aslot.at[s, part, k, pl.ds(0, rows)], self.asem.at[s, part, k]
                        )
                    )
        q = i % 2
        copies.append(
            pltpu.make_async_copy(
                unit.columns, self.bslot.at[q, 0, pl.ds(0, rows)], self.bsem.at[q, 0]
            )
        )
        if unit.trade:
            copies.append(
                pltpu.make_async_copy(
                    unit.nb_columns, self.bslot.at[q, 1, pl.ds(0, rows)], self.bsem.at[q, 1]
                )
            )
        return copies

    def load(self, i):
        unit = self.units[i]
        if unit.trade:
            self.trade(i).wait_recv()
            if unit.halves is not None and (i == 0 or self.units[i - 1].group != unit.group):
                unit.halves.arrive()
        for copy in self.loads(i):
            copy.start()

    def y_copy(self, i, k):
        n = self.summed.index(i)
        return send(self.theirs.at[n % 2, k], self.fromy.at[n, k], self.ysem, (n, k), self.peer)

    def compute(self, i):
        unit = self.units[i]
        s, q, g, rows = unit.group % 2, i % 2, i % HELD, unit.count
        for copy in self.loads(i):
            copy.wait()
        if i >= HELD:
            self.sent(i - HELD)
        if not unit.trade:
            n = self.summed.index(i)
            if n >= 2:
                for k in range(self.pairs):
                    self.y_copy(self.summed[n - 2], k).wait_send()

            def far(k, carry):
                self.theirs[n % 2, k] = lax.dot_general(
                    self.aslot[s, 1, k, :rows], self.bslot[q, 0, :rows], FIRST,
                    preferred_element_type=F32,
                ).astype(LOW)
                return carry

            lax.fori_loop(0, self.pairs, far, 0)
            for k in range(self.pairs):
                self.y_copy(i, k).start()

        def near(k, carry):
            total = lax.dot_general(
                self.aslot[s, 0, k, :rows], self.bslot[q, 0, :rows], FIRST,
                preferred_element_type=F32,
            )
            if unit.trade:
                total = total + lax.dot_general(
                    self.aslot[s, 1, k, :rows], self.bslot[q, 1, :rows], FIRST,
                    preferred_element_type=F32,
                )
            self.mine[g, k] = total.astype(LOW)
            return carry

        lax.fori_loop(0, self.pairs, near, 0)

    def add(self, dst, src):
        def step(s):
            dst[s, :] = dst[s, :] + src[s, :]

        each_slab(self.blk, step, 64)

    def y_add(self, i):
        n = self.summed.index(i)
        for k in range(self.pairs):
            self.y_copy(i, k).wait_recv()
            self.add(self.mine.at[i % HELD, k], self.fromy.at[n, k])

    def r_copy(self, i, t):
        d = jnp.clip(self.pairs - t + self.z, 0, self.pairs - 1)
        return send(self.mine.at[i % HELD, d], self.right.at[i % RING, t - 1], self.rsem, (i, t - 1), self.next)

    def l_copy(self, i, t):
        d = jnp.clip(t - self.pairs + self.z, 0, self.pairs - 1)
        return send(self.mine.at[i % HELD, d], self.left.at[i % RING, t - 1], self.lsem, (i, t - 1), self.last)

    def sends_right(self, t):
        return self.has_right & (t >= self.z + 1)

    def sends_left(self, t):
        return self.has_left & (t >= self.pairs - self.z)

    def step(self, i, t):
        g, r = i % HELD, i % RING
        if t == 1 and i >= RING:

            @pl.when(self.has_right)
            def _():
                pl.semaphore_wait(self.rfree, 1)

            @pl.when(self.has_left)
            def _():
                pl.semaphore_wait(self.lfree, 1)

        @pl.when(self.sends_right(t))
        def _():
            if t > 1:

                @pl.when(self.has_left & (t - 1 >= self.z))
                def _():
                    self.r_copy(i, t - 1).wait_recv()
                    d = jnp.clip(self.pairs - t + self.z, 0, self.pairs - 1)
                    self.add(self.mine.at[g, d], self.right.at[r, t - 2])

            self.r_copy(i, t).start()

        @pl.when(self.sends_left(t))
        def _():
            if t > 1:

                @pl.when(self.has_right & (t - 1 >= self.pairs - 1 - self.z))
                def _():
                    self.l_copy(i, t - 1).wait_recv()
                    d = jnp.clip(t - self.pairs + self.z, 0, self.pairs - 1)
                    self.add(self.mine.at[g, d], self.left.at[r, t - 2])

            self.l_copy(i, t).start()

    def out_copy(self, i):
        return pltpu.make_async_copy(self.stage.at[i % 2], self.units[i].out, self.osem.at[i % 2])

    def final(self, i):
        g, r, t = i % HELD, i % RING, self.pairs - 1

        @pl.when(self.has_left)
        def _():
            self.r_copy(i, t).wait_recv()
            self.add(self.mine.at[g, self.z], self.right.at[r, t - 1])

        @pl.when(self.has_right)
        def _():
            self.l_copy(i, t).wait_recv()
            self.add(self.mine.at[g, self.z], self.left.at[r, t - 1])

        if i + RING < len(self.units):

            @pl.when(self.has_left)
            def _():
                pl.semaphore_signal(self.rfree, inc=1, device_id=self.last, device_id_type=MESH)

            @pl.when(self.has_right)
            def _():
                pl.semaphore_signal(self.lfree, inc=1, device_id=self.next, device_id_type=MESH)

        if i >= 2:
            self.out_copy(i - 2).wait()

        def step(s):
            self.stage[i % 2, s, :] = self.mine[g, self.z, s, :]

        each_slab(self.blk, step, 64)
        self.out_copy(i).start()

    def sent(self, i):
        for t in range(1, self.pairs):

            @pl.when(self.sends_right(t))
            def _():
                self.r_copy(i, t).wait_send()

            @pl.when(self.sends_left(t))
            def _():
                self.l_copy(i, t).wait_send()

    def lead(self, i):
        return 1 if self.units[i].trade else 2

    def ask(self, i):
        if i < len(self.units) and self.units[i].trade:
            self.trade(i).start()

    def tick(self, k):
        count, pairs = len(self.units), self.pairs
        due = [i for i in range(count) if max(j - self.lead(j) for j in range(i + 1)) == k]
        for i in due[:1]:
            self.load(i)
        if k >= 0:
            self.ask(k + 4)
        for t in range(pairs - 1, 1, -1):
            if 0 <= k - (t - 1) < count:
                self.step(k - (t - 1), t)
        if 0 <= k < count:
            if not self.units[k].trade:
                self.y_add(k)
            self.step(k, 1)
        if 0 <= k - (pairs - 1) < count:
            self.final(k - (pairs - 1))
        for n, i in enumerate(due):
            if n > 0:
                self.load(i)
            self.compute(i)

    def drain(self):
        count = len(self.units)
        for i in range(max(0, count - 2), count):
            self.out_copy(i).wait()
        for i in range(max(0, count - HELD), count):
            self.sent(i)
        for i in self.summed[-2:]:
            for k in range(self.pairs):
                self.y_copy(i, k).wait_send()
        for i, unit in enumerate(self.units):
            if unit.trade:
                self.trade(i).wait_send()


VM = pl.BlockSpec(memory_space=pltpu.VMEM)
HB = pl.BlockSpec(memory_space=pl.ANY)


def norm_rows(rows):
    centre = jnp.mean(rows, axis=-1, keepdims=True)
    centred = rows - centre
    variance = jnp.mean(centred * centred, axis=-1, keepdims=True)
    inv_std = lax.rsqrt(variance + 1e-05)
    return centred * inv_std, inv_std


class Narrow:
    def __init__(self):
        self.me = lax.axis_index(NARROW)
        x, c = self.me // 2, self.me % 2
        self.core_at = x * 2 + 1 - c
        self.chip_at = (1 - x) * 2 + c
        self.far_at = (1 - x) * 2 + 1 - c
        self.core = {NARROW: self.core_at}
        self.chip = {NARROW: self.chip_at}

    def meet(self, barrier):
        greet(barrier, self.core)
        greet(barrier, self.chip)
        return 2


class Gather:
    def __init__(self, net, full, own, sems):
        self.net, self.full, self.own, self.sems = net, full, own, sems

    def place(self, b, who):
        at = (b * 4 + who) * self.own
        return self.full.at[pl.ds(pl.multiple_of(at, self.own), self.own), :]

    def mine(self, b):
        return self.place(b, self.net.me)

    def to_core(self, b):
        return send(self.mine(b), self.mine(b), self.sems, (b, 0), self.net.core)

    def to_chip(self, b):
        return send(self.mine(b), self.mine(b), self.sems, (b, 1), self.net.chip)

    def onward(self, b):
        block = self.place(b, self.net.chip_at)
        return send(block, block, self.sems, (b, 2), self.net.core)

    def start(self, b):
        self.to_chip(b).start()
        self.to_core(b).start()

    def forward(self, b):
        self.to_chip(b).wait_recv()
        self.onward(b).start()

    def finish(self, b):
        self.to_core(b).wait_recv()
        self.onward(b).wait_recv()
        self.to_core(b).wait_send()
        self.to_chip(b).wait_send()
        self.onward(b).wait_send()


class Scatter:
    def __init__(self, net, part, landed, outgoing, arrived, sems):
        self.net, self.part, self.landed = net, part, landed
        self.outgoing, self.arrived, self.sems = outgoing, arrived, sems
        self.own = part.shape[1] // 4

    def rows(self, b, who):
        return self.part.at[b, pl.ds(pl.multiple_of(who * self.own, self.own), self.own), :]

    def core_copy(self, b, k):
        who = self.net.far_at if k == 0 else self.net.core_at
        return send(self.rows(b, who), self.landed.at[b, k], self.sems, (b, k), self.net.core)

    def chip_copy(self, b):
        return send(self.outgoing.at[b], self.arrived.at[b], self.sems, (b, 2), self.net.chip)

    def start(self, b):
        self.core_copy(b, 0).start()
        self.core_copy(b, 1).start()

    def cross(self, b):
        self.core_copy(b, 0).wait_recv()
        mine = self.rows(b, self.net.chip_at)

        def step(s):
            total = mine[s, :] + self.landed[b, 0, s, :]
            self.outgoing[b, s, :] = total.astype(self.outgoing.dtype)

        each_slab(self.own, step)
        self.chip_copy(b).start()

    def ready(self, b):
        self.core_copy(b, 1).wait_recv()
        self.chip_copy(b).wait_recv()

    def total(self, b, s):
        near = self.rows(b, self.net.me)[s, :] + self.landed[b, 1, s, :]
        return near + self.arrived[b, s, :].astype(F32)

    def finish(self, b):
        self.core_copy(b, 0).wait_send()
        self.core_copy(b, 1).wait_send()
        self.chip_copy(b).wait_send()


class Halves:
    def __init__(self, full, there, pairs, sems, index):
        me = lax.axis_index(WIDE)
        y = me % 2
        blk = full.shape[1] // (2 * pairs)
        peer = {WIDE: me + 1 - 2 * y}
        self.copies = [
            send(
                full.at[:, pl.ds(pl.multiple_of((2 * k + 1 - y) * blk, blk), blk)],
                there.at[:, pl.ds(k * blk, blk)], sems, (index, k), peer,
            )
            for k in range(pairs)
        ]

    def start(self):
        for copy in self.copies:
            copy.start()

    def arrive(self):
        for copy in self.copies:
            copy.wait_recv()

    def leave(self):
        for copy in self.copies:
            copy.wait_send()


def scatter_scratch(images, own, width):
    return [
        pltpu.VMEM((images, 4 * own, width), F32),
        pltpu.VMEM((images, 2, own, width), F32),
        pltpu.VMEM((images, own, width), LOW),
        pltpu.VMEM((images, own, width), LOW),
        pltpu.SemaphoreType.DMA((2, images, 3)),
    ]


def params(number, limit):
    return pltpu.CompilerParams(
        collective_id=number, has_side_effects=True, vmem_limit_bytes=limit * 1024 * 1024
    )


class Copies:
    def __init__(self, sems):
        self.sems, self.used, self.open = sems, 0, []

    def start(self, src, dst):
        copy = pltpu.make_async_copy(src, dst, self.sems.at[self.used])
        self.used += 1
        copy.start()
        return copy

    def later(self, src, dst):
        self.open.append(self.start(src, dst))

    def close(self):
        for copy in self.open:
            copy.wait()


def columns_of(width, step, tile=512):
    def body(j, carry):
        step(pl.ds(pl.multiple_of(j * tile, tile), tile))
        return carry

    lax.fori_loop(0, width // tile, body, 0)


def dot(left, right, dims=(((1,), (0,)), ((), ()))):
    return lax.dot_general(left, right, dims, preferred_element_type=F32)


def softmax_parts(q, k):
    scores = dot(q, k, LAST) * (1.0 / math.sqrt(HEAD))
    powers = jnp.exp(scores - jnp.max(scores, axis=-1, keepdims=True))
    return powers / jnp.sum(powers, axis=-1, keepdims=True)


def head_columns(j):
    return pl.ds(pl.multiple_of(j * HEAD, HEAD), HEAD)


def heads_forward(b, images, query, keys, values, out):
    many, some = query.shape[0] // images, keys.shape[0] // images
    asked, told = pl.ds(b * many, many), pl.ds(b * some, some)

    def body(j, carry):
        cols = head_columns(j)
        probs = softmax_parts(query[asked, cols], keys[told, cols])
        out[asked, cols] = dot(probs.astype(LOW), values[told, cols]).astype(LOW)
        return carry

    lax.fori_loop(0, query.shape[1] // HEAD, body, 0)


def heads_back(images, query, keys, values, d_att):
    heads = query.shape[1] // HEAD
    many, some = query.shape[0] // images, keys.shape[0] // images
    scale = 1.0 / math.sqrt(HEAD)

    def body(j, carry):
        b = j // heads
        cols = head_columns(j % heads)
        asked = pl.ds(pl.multiple_of(b * many, many), many)
        told = pl.ds(pl.multiple_of(b * some, some), some)
        q, k, v, d = query[asked, cols], keys[told, cols], values[told, cols], d_att[asked, cols]
        probs = softmax_parts(q, k)
        d_probs = dot(d, v, LAST)
        weighted = jnp.sum(probs * d_probs, axis=-1, keepdims=True)
        d_scores = (probs * (d_probs - weighted)).astype(LOW)
        values[told, cols] = dot(probs.astype(LOW), d, FIRST).astype(LOW)
        keys[told, cols] = (dot(d_scores, q, FIRST) * scale).astype(LOW)
        query[asked, cols] = (dot(d_scores, k) * scale).astype(LOW)
        return carry

    lax.fori_loop(0, images * heads, body, 0)


def gelu(u):
    turn = jnp.tanh(math.sqrt(2.0 / math.pi) * (u + 0.044715 * (u * u * u)))
    return 0.5 * u * (1.0 + turn)


def gelu_slope(u):
    c = math.sqrt(2.0 / math.pi)
    turn = jnp.tanh(c * (u + 0.044715 * (u * u * u)))
    return 0.5 * (1.0 + turn) + 0.5 * u * (1.0 - turn * turn) * (c * (1.0 + 0.134145 * (u * u)))


def flat(array):
    return array.reshape(array.shape[0] * array.shape[1], array.shape[2])


def forward_all(pairs, number, given):
    t = given
    images, own, width = t.tokens.shape
    length, words = 4 * own, t.caption.shape[1]
    inner, ff, states = t.query_self.shape[1], t.up_proj.shape[1], t.caption.shape[2]
    rows, word_rows, word_own = images * length, images * words, words // 4
    chunks, text_chunks = ff // inner, states // inner
    half = width // 2
    vars_in = dict(
        tokens=t.tokens, caption=flat(t.caption), cotangent=t.cotangent, text_proj=t.text_proj,
        query_self=t.query_self, key_self=t.key_self, value_self=t.value_self, out_self=t.out_self,
        query_cross=t.query_cross, key_cross=t.key_cross, value_cross=t.value_cross,
        out_cross=t.out_cross, up_proj=t.up_proj, down_proj=t.down_proj,
    )
    sds = jax.ShapeDtypeStruct
    outs = dict(
        image_self=sds((rows, width), LOW), image_cross=sds((rows, width), LOW),
        image_feed=sds((rows, width), LOW), d_image=sds((rows, width), LOW),
        context=sds((word_rows, width), LOW),
        query_sa=sds((rows, inner), LOW), keys_sa=sds((rows, inner), LOW), values_sa=sds((rows, inner), LOW),
        query_ca=sds((rows, inner), LOW), keys_ca=sds((word_rows, inner), LOW), values_ca=sds((word_rows, inner), LOW),
        attended_sa=sds((rows, inner), LOW), attended_ca=sds((rows, inner), LOW),
        resid_mid=sds((images, own, width), F32), resid_late=sds((images, own, width), F32),
        activ=sds((rows, ff), LOW), d_pre=sds((rows, ff), LOW),
        nb_self=sds((rows, half), LOW), nb_cross=sds((rows, half), LOW), nb_low=sds((rows, half), LOW),
        nb_context=sds((word_rows, half), LOW),
    )

    def kernel(*refs):
        h = types.SimpleNamespace(**dict(zip(vars_in, refs)))
        refs = refs[len(vars_in):]
        marks, gain_self, gain_cross, gain_feed = refs[:4]
        refs = refs[4:]
        o = types.SimpleNamespace(**dict(zip(outs, refs)))
        refs = refs[len(outs):]
        scatter_refs, text_refs = refs[:5], refs[5:10]
        (full_s, full_c, full_f, full_d, full_x, gsem_s, gsem_c, gsem_f, gsem_d, gsem_x,
         wn, wt, tok, cot, cap, sq, sk, sv, xq, xk, xv, att_s, att_c, mid, late, act, dpre,
         fsem, osem, hsem) = refs[10:]
        net = Narrow()
        fetch, store = Copies(fsem), Copies(osem)
        barrier = pltpu.get_barrier_semaphore()
        me = lax.axis_index(WIDE)
        greet(barrier, {WIDE: me + 1 - 2 * (me % 2)})
        others = net.meet(barrier) + 1

        def whole(j, ref):
            return fetch.start(ref, wn.at[j])

        def band(j, ref, c):
            return fetch.start(ref.at[pl.ds(c * inner, inner)], wt.at[j])

        need_tok = fetch.start(h.tokens, tok)
        need_cap = fetch.start(h.caption, cap)
        need_proj = [band(c, h.text_proj, c) for c in range(text_chunks)]
        need_cot = fetch.start(h.cotangent, cot)
        need_qkv = [whole(j, ref) for j, ref in enumerate((h.query_self, h.key_self, h.value_self))]
        need_out_self = fetch.start(h.out_self, wt.at[2])
        need_kv = [whole(4, h.key_cross), whole(5, h.value_cross)]
        need_query_cross = whole(3, h.query_cross)
        need_out_cross = fetch.start(h.out_cross, wt.at[3])
        need_up = {3: fetch.start(h.up_proj.at[:, pl.ds(3 * inner, inner)], wn.at[6])}
        gather_s = Gather(net, full_s, own, gsem_s)
        gather_c = Gather(net, full_c, own, gsem_c)
        gather_f = Gather(net, full_f, own, gsem_f)
        gather_d = Gather(net, full_d, own, gsem_d)
        gather_x = Gather(net, full_x, word_own, gsem_x)
        scatter, text = Scatter(net, *scatter_refs), Scatter(net, *text_refs)
        part = scatter.part

        def of(b, n=length):
            return pl.ds(b * n, n)

        need_tok.wait()
        pl.semaphore_wait(barrier, others)
        for b in range(images):
            mine = gather_s.mine(b)

            def step(s, b=b, mine=mine):
                normed, _ = norm_rows(tok[b, s, :].astype(F32))
                mine[s, :] = (normed * gain_self[...].astype(F32)[None]).astype(LOW)

            each_slab(own, step)
            gather_s.start(b)
        need_cap.wait()
        for need in need_proj:
            need.wait()
        for b in range(images):

            def step(cols, b=b):
                total = None
                for c in range(text_chunks):
                    term = dot(cap[of(b, words), pl.ds(c * inner, inner)], wt[c, :, cols])
                    total = term if total is None else total + term
                text.part[b, :, cols] = total

            columns_of(width, step)
            text.start(b)
        need_cot.wait()
        for b in range(images):
            mine = gather_d.mine(b)

            def step(s, b=b, mine=mine):
                mine[s, :] = (cot[b, s, :].astype(F32) * marks[b, s, :]).astype(LOW)

            each_slab(own, step)

        def project(b, source, weights, targets, n=length):
            for j, target in zip(weights, targets):
                target[of(b, n), :] = dot(source[of(b, n), :], wn[j]).astype(LOW)

        def back_out(b, attended, j):
            def step(cols):
                part[b, :, cols] = dot(attended[of(b), :], wt[j, :, cols])

            columns_of(width, step)
            scatter.start(b)

        need_down = {c: band(c, h.down_proj, c) for c in range(text_chunks)}
        gather_s.forward(0)
        text.cross(0)
        text.cross(1)
        gather_d.start(0)
        for b in range(images):
            gather_s.finish(b)
            if b == 0:
                for need in need_qkv:
                    need.wait()
            project(b, full_s, (0, 1, 2), (sq, sk, sv))
            if b + 1 < images:
                gather_s.forward(b + 1)
            heads_forward(b, images, sq, sk, sv, att_s)
            if b == 0:
                need_out_self.wait()
            back_out(b, att_s, 2)
            if b == 0:
                scatter.cross(b)
        store.later(full_s, o.image_self)
        for ref, out in ((sq, o.query_sa), (sk, o.keys_sa), (sv, o.values_sa), (att_s, o.attended_sa)):
            store.later(ref, out)
        for c in range(3):
            need_up[c] = fetch.start(h.up_proj.at[:, pl.ds(c * inner, inner)], wn.at[c])
        need_down[2] = band(2, h.down_proj, 2)
        for b in range(images):
            text.ready(b)
            mine = gather_x.mine(b)

            def step(s, b=b, mine=mine):
                mine[s, :] = text.total(b, s).astype(LOW)

            each_slab(word_own, step)
        scatter.cross(1)
        for b in range(images):
            gather_x.start(b)
        halves_self = Halves(full_s, o.nb_self, pairs, hsem, 0)
        halves_self.start()

        def rows_out(b, source, target, gain, gather):
            scatter.ready(b)
            mine = gather.mine(b)

            def step(s):
                kept = source[b, s, :].astype(F32) + scatter.total(b, s)
                target[b, s, :] = kept
                normed, _ = norm_rows(kept)
                mine[s, :] = (normed * gain[...].astype(F32)[None]).astype(LOW)

            each_slab(own, step)
            gather.start(b)

        rows_out(0, tok, mid, gain_cross, gather_c)
        gather_d.start(1)
        for b in range(images):
            gather_x.forward(b)
        rows_out(1, tok, mid, gain_cross, gather_c)
        store.later(mid, o.resid_mid)
        for need in need_kv:
            need.wait()
        for b in range(images):
            gather_x.finish(b)
            project(b, full_x, (4, 5), (xk, xv), words)
            text.finish(b)
        halves_context = Halves(full_x, o.nb_context, pairs, hsem, 1)
        halves_context.start()
        store.later(full_x, o.context)
        store.later(xk, o.keys_ca)
        store.later(xv, o.values_ca)
        need_query_cross.wait()
        gather_c.forward(0)
        for b in range(images):
            gather_d.forward(b)
        for b in range(images):
            gather_c.finish(b)
            project(b, full_c, (3,), (xq,))
            if b + 1 < images:
                gather_c.forward(b + 1)
            heads_forward(b, images, xq, xk, xv, att_c)
            scatter.finish(b)
            if b == 0:
                need_out_cross.wait()
            back_out(b, att_c, 3)
            if b == 0:
                scatter.cross(b)
        store.later(full_c, o.image_cross)
        store.later(xq, o.query_ca)
        store.later(att_c, o.attended_ca)
        need_down[3] = band(3, h.down_proj, 3)
        for b in range(images):
            gather_d.finish(b)
        halves_low = Halves(full_d, o.nb_low, pairs, hsem, 2)
        halves_low.start()
        scatter.cross(1)
        store.later(full_d, o.d_image)
        rows_out(0, mid, late, gain_feed, gather_f)
        rows_out(1, mid, late, gain_feed, gather_f)
        store.later(late, o.resid_late)
        halves_cross = Halves(full_c, o.nb_cross, pairs, hsem, 3)
        halves_cross.start()
        gather_f.forward(0)
        for b in range(images):
            gather_f.finish(b)
            scatter.finish(b)
            for c in range(chunks):
                if b == 0:
                    need_up[c].wait()
                cols = pl.ds(c * inner, inner)
                part[b, :, cols] = dot(full_f[of(b), :], wn[6 if c == 3 else c])
                if b == 0 and c == 1:
                    gather_f.forward(1)

                def step(s, b=b, cols=cols):
                    act[pl.ds(pl.multiple_of(b * length + s.start, 16), 16), cols] = gelu(part[b, s, cols]).astype(LOW)

                each_slab(length, step)
        store.later(act, o.activ)
        store.later(full_f, o.image_feed)
        for c in range(chunks):
            need_down[c].wait()
            cols = pl.ds(c * inner, inner)
            for b in range(images):
                slope = dot(full_d[of(b), :], wt[c], LAST)
                dpre[of(b), cols] = (gelu_slope(part[b, :, cols]) * slope).astype(LOW)
            store.later(dpre.at[:, cols], o.d_pre.at[:, cols])
        for halves in (halves_self, halves_context, halves_low, halves_cross):
            halves.arrive()
            halves.leave()
        store.close()

    V, DS = pltpu.VMEM, pltpu.SemaphoreType.DMA
    gsem = DS((2, images, 3))
    scratch = scatter_scratch(images, own, width) + scatter_scratch(images, word_own, width)
    scratch += [V((rows, width), LOW)] * 4 + [V((word_rows, width), LOW)] + [gsem] * 5
    scratch += [
        V((7, width, inner), LOW), V((4, inner, width), LOW),
        V((images, own, width), LOW), V((images, own, width), LOW), V((word_rows, states), LOW),
        V((rows, inner), LOW), V((rows, inner), LOW), V((rows, inner), LOW),
        V((rows, inner), LOW), V((word_rows, inner), LOW), V((word_rows, inner), LOW),
        V((rows, inner), LOW), V((rows, inner), LOW),
        V((images, own, width), F32), V((images, own, width), F32), V((rows, ff), LOW), V((rows, ff), LOW),
        DS((40,)), DS((40,)), DS((2, 4, pairs)),
    ]
    result = pl.pallas_call(
        kernel,
        out_shape=list(outs.values()),
        in_specs=[HB] * len(vars_in) + [VM] * 4,
        out_specs=[HB] * len(outs),
        scratch_shapes=scratch,
        compiler_params=params(number, 62),
        name="forward_all",
    )(*vars_in.values(), t.marks, *t.gains)
    return types.SimpleNamespace(**dict(zip(outs, result)))


def backward_all(pairs, number, given, kept):
    t = given
    images, own, width = t.tokens.shape
    length, words = 4 * own, t.caption.shape[1]
    inner, ff, states = t.query_self.shape[1], t.up_proj.shape[1], t.caption.shape[2]
    rows, word_rows, word_own = images * length, images * words, words // 4
    chunks, text_chunks = ff // inner, states // inner
    half, blk = width // 2, width // (2 * pairs)
    count = 2 * chunks + text_chunks + 8
    vars_in = dict(
        vars(kept),
        tokens=t.tokens, caption=flat(t.caption), cotangent=t.cotangent, text_proj=t.text_proj,
        query_self=t.query_self, key_self=t.key_self, value_self=t.value_self, out_self=t.out_self,
        query_cross=t.query_cross, key_cross=t.key_cross, value_cross=t.value_cross,
        out_cross=t.out_cross, up_proj=t.up_proj, down_proj=t.down_proj,
    )

    def kernel(*refs):
        h = types.SimpleNamespace(**dict(zip(vars_in, refs)))
        refs = refs[len(vars_in):]
        marks, gain_self, gain_cross, gain_feed = refs[:4]
        grads_out, words_out, tokens_out, layer_out, gain_out, nb_cols, nb_feed = refs[4:11]
        refs = refs[11:]
        scatter_refs = refs[:5]
        (full_c, full_s, full_x, gsem_c, gsem_s, gsem_x, text_sem,
         big, d_att, wa, wb, xq, xk, xv, sq, sk, sv, cot, late, mid, tok, low_rows, word_grad,
         fsem, osem, nbsem, hsem, gacc, gland, gsems) = refs[5:35]
        net = Narrow()
        units = []

        def unit(trade, rows_ref, nb_rows, columns, size, halves=None):
            i = len(units)
            units.append(types.SimpleNamespace(
                trade=trade, rows=rows_ref, nb_rows=nb_rows, columns=columns, count=size, halves=halves,
                nb_columns=nb_cols.at[i, pl.ds(0, size)], sems=nbsem, out=grads_out.at[i],
            ))

        def chunk(ref, c):
            return ref.at[:, pl.ds(c * inner, inner)]

        halves_feed = Halves(h.image_feed, nb_feed, pairs, hsem, 0)
        for c in range(chunks):
            unit(True, h.d_image, h.nb_low, chunk(h.activ, c), rows)
        for c in range(chunks):
            unit(True, h.image_feed, nb_feed, chunk(h.d_pre, c), rows, halves_feed)
        unit(False, full_c, None, h.attended_ca, rows)
        unit(True, h.image_cross, h.nb_cross, xq, rows)
        unit(True, h.context, h.nb_context, xk, word_rows)
        unit(True, h.context, h.nb_context, xv, word_rows)
        for c in range(text_chunks):
            unit(False, full_x, None, chunk(h.caption, c), word_rows)
        unit(False, full_s, None, h.attended_sa, rows)
        unit(True, h.image_self, h.nb_self, sq, rows)
        unit(True, h.image_self, h.nb_self, sk, rows)
        unit(True, h.image_self, h.nb_self, sv, rows)
        wide = Wide(pairs, units, refs[35:])
        fetch, store = Copies(fsem), Copies(osem)

        def of(b, n=length):
            return pl.ds(b * n, n)

        barrier = pltpu.get_barrier_semaphore()
        far = {WIDE: (wide.z + 2) % pairs * 2 + wide.y}
        near = {WIDE: (wide.z + 1 - 2 * (wide.z % 2)) * 2 + wide.y}
        greet(barrier, far)
        others = wide.meet(barrier) + net.meet(barrier) + 1

        def up_chunk(c):
            return fetch.start(chunk(h.up_proj, c), wa.at[c % 2])

        need_up = {c: up_chunk(c) for c in range(2)}
        need_pre = fetch.start(h.d_pre, big)
        need_cot = fetch.start(h.cotangent, cot)
        need_late = fetch.start(h.resid_late, late)
        need_out = fetch.start(h.out_cross, wb)
        need_ca = [fetch.start(a, b) for a, b in ((h.query_ca, xq), (h.keys_ca, xk), (h.values_ca, xv))]
        need_mid = fetch.start(h.resid_mid, mid)
        need_sa = [fetch.start(a, b) for a, b in ((h.query_sa, sq), (h.keys_sa, sk), (h.values_sa, sv))]
        need_tok = fetch.start(h.tokens, tok)
        pl.semaphore_wait(barrier, others)
        wide.ask(0)
        wide.ask(1)
        scatter = Scatter(net, *scatter_refs)
        part = scatter.part
        gather_c, gather_s = Gather(net, full_c, own, gsem_c), Gather(net, full_s, own, gsem_s)
        gather_x = Gather(net, full_x, word_own, gsem_x)

        need_pre.wait()
        for c in range(chunks):
            need_up[c].wait()
            for b in range(images):

                def step(cols, b=b, c=c):
                    term = dot(big[of(b), pl.ds(c * inner, inner)], wa[c % 2, cols, :], LAST)
                    part[b, :, cols] = term if c == 0 else part[b, :, cols] + term

                columns_of(width, step)
                if c == chunks - 1:
                    scatter.start(b)
            if c + 2 < chunks:
                need_up[c + 2] = up_chunk(c + 2)
        need_query = fetch.start(h.query_cross, wa.at[0])
        need_key = fetch.start(h.key_cross, wa.at[1])
        halves_feed.start()
        gacc[...] = jnp.zeros_like(gacc)

        def back_rows(b, above, mask, source, gain, slot, keep, mine):
            scatter.ready(b)

            def step(s):
                d_hidden = scatter.total(b, s)
                normed, inv_std = norm_rows(source[b, s, :].astype(F32))
                gacc[slot : slot + 1, :] += jnp.sum(d_hidden * normed, axis=0, keepdims=True)
                top = above[b, s, :].astype(F32)
                if mask is not None:
                    top = top * mask[b, s, :]
                scaled = d_hidden * gain[...].astype(F32)[None]
                inside = scaled - jnp.mean(scaled, axis=-1, keepdims=True)
                inside = inside - normed * jnp.mean(scaled * normed, axis=-1, keepdims=True)
                d_rows = top + inv_std * inside
                if keep is not None:
                    keep[b, s, :] = d_rows
                mine[s, :] = d_rows.astype(LOW)

            each_slab(own, step)

        def multiply(b, target, lefts, rights, n=length):
            def step(cols):
                total = None
                for left, j in zip(lefts, rights):
                    term = dot(left[of(b, n), :], wa[j, cols, :], LAST)
                    total = term if total is None else total + term
                target[b, :, cols] = total

            columns_of(width, step)

        def out_back(b, full):
            d_att[of(b), :] = dot(full[of(b), :], wb[...], LAST).astype(LOW)

        wide.tick(-1)
        for b in range(images):
            scatter.cross(b)
        wide.tick(0)
        need_cot.wait()
        need_late.wait()
        for b in range(images):
            back_rows(b, cot, marks, late, gain_feed, 2, late, gather_c.mine(b))
            gather_c.start(b)
        wide.ask(2)
        wide.ask(3)
        for b in range(images):
            gather_c.forward(b)
        wide.tick(1)
        need_out.wait()
        for b in range(images):
            scatter.finish(b)
            gather_c.finish(b)
            out_back(b, full_c)
        need_out = fetch.start(h.out_self, wb)
        for need in need_ca:
            need.wait()
        heads_back(images, xq, xk, xv, d_att)
        wide.tick(2)
        need_query.wait()
        for b in range(images):
            multiply(b, part, [xq], [0])
            scatter.start(b)
        need_value = fetch.start(h.value_cross, wa.at[0])
        for b in range(images):
            scatter.cross(b)
        need_mid.wait()
        for b in range(images):
            back_rows(b, late, None, mid, gain_cross, 1, mid, gather_s.mine(b))
            gather_s.start(b)
        wide.tick(3)
        need_again = fetch.start(h.resid_late, late)
        for b in range(images):
            gather_s.forward(b)
        for b in range(images):
            scatter.finish(b)
            gather_s.finish(b)
        text = Scatter(
            net, part.at[:, pl.ds(0, words)], scatter.landed.at[:, :, pl.ds(0, word_own)],
            scatter.outgoing.at[:, pl.ds(0, word_own)], scatter.arrived.at[:, pl.ds(0, word_own)], text_sem,
        )
        need_key.wait()
        need_value.wait()
        for b in range(images):
            multiply(b, text.part, [xk, xv], [1, 0], words)
            text.start(b)
        need_qkv = [fetch.start(h.query_self, wa.at[0]), fetch.start(h.key_self, wa.at[1])]
        need_out.wait()
        for b in range(images):
            out_back(b, full_s)
        need_text = fetch.start(h.text_proj.at[pl.ds(0, inner)], wb)
        wide.tick(4)
        for b in range(images):
            text.cross(b)
        for need in need_sa:
            need.wait()
        heads_back(images, sq, sk, sv, d_att)
        for b in range(images):
            text.ready(b)
            mine = gather_x.mine(b)

            def step(s, b=b, mine=mine):
                mine[s, :] = text.total(b, s).astype(LOW)

            each_slab(word_own, step)
            gather_x.start(b)
        for b in range(images):
            gather_x.forward(b)
        wide.tick(5)
        for b in range(images):
            text.finish(b)
            gather_x.finish(b)
        for c in range(text_chunks):
            need_text.wait()
            word_grad[:, pl.ds(c * inner, inner)] = dot(full_x[...], wb[...], LAST).astype(LOW)
            if c + 1 < text_chunks:
                need_text = fetch.start(h.text_proj.at[pl.ds((c + 1) * inner, inner)], wb)
        store.later(word_grad, words_out)
        need_down = fetch.start(h.down_proj.at[pl.ds(0, inner)], wb)
        for need in need_qkv:
            need.wait()
        for b in range(images):
            multiply(b, part, [sq, sk], [0, 1])
        need_value = fetch.start(h.value_self, wa.at[0])
        need_act = fetch.start(h.activ, big)
        need_value.wait()
        for b in range(images):

            def step(cols, b=b):
                part[b, :, cols] += dot(sv[of(b), :], wa[0, cols, :], LAST)

            columns_of(width, step)
            scatter.start(b)
        wide.tick(6)
        for b in range(images):
            scatter.cross(b)
        need_tok.wait()
        for b in range(images):
            back_rows(b, mid, None, tok, gain_self, 0, None, low_rows.at[b])
        store.later(low_rows, tokens_out)
        for b in range(images):
            scatter.finish(b)
        wide.tick(7)
        for j, peer in enumerate((net.core, net.chip, wide.peer, near, far)):
            trip = send(gacc, gland.at[j], gsems, (j,), peer)
            trip.start()
            trip.wait()
            gacc[...] = gacc[...] + gland[j]
        store.later(gacc, gain_out)
        wide.tick(8)
        need_act.wait()
        for c in range(chunks):
            need_down.wait()
            for b in range(images):

                def step(cols, b=b, c=c):
                    term = dot(big[of(b), pl.ds(c * inner, inner)], wb[:, cols])
                    part[b, :, cols] = term if c == 0 else part[b, :, cols] + term

                columns_of(width, step)
            if c + 1 < chunks:
                need_down = fetch.start(h.down_proj.at[pl.ds((c + 1) * inner, inner)], wb)
        for b in range(images):
            scatter.start(b)
        wide.tick(9)
        for b in range(images):
            scatter.cross(b)
        wide.tick(10)
        need_again.wait()
        for b in range(images):
            scatter.ready(b)

            def step(s, b=b):
                tok[b, s, :] = (late[b, s, :] + scatter.total(b, s)).astype(LOW)

            each_slab(own, step)
            scatter.finish(b)
        store.later(tok, layer_out)
        for k in range(11, count + pairs - 1):
            wide.tick(k)
        wide.drain()
        halves_feed.leave()
        store.close()

    V, DS = pltpu.VMEM, pltpu.SemaphoreType.DMA
    gsem = DS((2, images, 3))
    sums = 2 + text_chunks
    scratch = scatter_scratch(images, own, width)
    scratch += [V((rows, width), LOW), V((rows, width), LOW), V((word_rows, width), LOW)] + [gsem] * 4
    scratch += [
        V((rows, ff), LOW), V((rows, inner), LOW), V((2, width, inner), LOW), V((inner, width), LOW),
        V((rows, inner), LOW), V((word_rows, inner), LOW), V((word_rows, inner), LOW),
        V((rows, inner), LOW), V((rows, inner), LOW), V((rows, inner), LOW),
        V((images, own, width), LOW), V((images, own, width), F32), V((images, own, width), F32),
        V((images, own, width), LOW), V((images, own, width), LOW), V((word_rows, states), LOW),
        DS((40,)), DS((8,)), DS((2, count)), DS((2, 1, pairs)), V((8, width), F32), V((5, 8, width), F32), DS((2, 5)),
    ]
    scratch += [
        V((HELD, pairs, blk, inner), LOW), V((2, pairs, blk, inner), LOW), V((sums, pairs, blk, inner), LOW),
        V((RING, pairs - 1, blk, inner), LOW), V((RING, pairs - 1, blk, inner), LOW), V((2, blk, inner), LOW),
        V((2, 2, pairs, rows, blk), LOW), V((2, 2, rows, inner), LOW),
        DS((2, sums, pairs)), DS((2, count, pairs - 1)), DS((2, count, pairs - 1)),
        DS((2, 2, pairs)), DS((2, 2)), DS((2,)),
        pltpu.SemaphoreType.REGULAR, pltpu.SemaphoreType.REGULAR,
    ]
    sds = jax.ShapeDtypeStruct
    result = pl.pallas_call(
        kernel,
        out_shape=[
            sds((count, blk, inner), LOW), sds((word_rows, states), LOW), sds((images, own, width), LOW),
            sds((images, own, width), LOW), sds((8, width), F32), sds((count, rows, inner), LOW), sds((rows, half), LOW),
        ],
        in_specs=[HB] * len(vars_in) + [VM] * 4,
        out_specs=[HB] * 7,
        scratch_shapes=scratch,
        compiler_params=params(number, 62),
        name="backward_all",
    )(*vars_in.values(), t.marks, *t.gains)
    return result[:5]


def spread(blocks, places, shapes, whole, gains):
    count, blk, inner = blocks.shape
    more = len(whole)

    def kernel(*refs):
        blocks_ref, whole_in, gains_ref, refs = refs[0], refs[1 : 1 + more], refs[1 + more], refs[2 + more :]
        outs, whole_out, refs = refs[: len(shapes)], refs[len(shapes) : len(shapes) + more], refs[len(shapes) + more :]
        gains_out, refs = refs[:3], refs[3:]
        for j, row in enumerate(gains_out):
            row[...] = gains_ref[j, :]
        held, flat_stage, turned_stage, isem, osem, wsem = refs
        ins = [pltpu.make_async_copy(blocks_ref.at[i], held.at[i], isem.at[i]) for i in range(count)]
        for copy in ins:
            copy.start()
        done, plain, turns = [], 0, 0
        for j in range(more):
            done.append(pltpu.make_async_copy(whole_in[j], whole_out[j], wsem.at[j]))
            done[-1].start()
        for i, (which, row, col, turned) in enumerate(places):
            ins[i].wait()
            if turned:
                stage = turned_stage.at[turns]
                turns += 1
                for j in range(0, inner, 128):
                    stage[pl.ds(j, 128), :] = held[i, :, pl.ds(j, 128)].astype(F32).T
                place = outs[which].at[pl.ds(row, inner), pl.ds(col, blk)]
            else:
                stage = flat_stage.at[plain]
                plain += 1
                stage[...] = held[i].astype(F32)
                place = outs[which].at[pl.ds(row, blk), pl.ds(col, inner)]
            done.append(pltpu.make_async_copy(stage, place, osem.at[i]))
            done[-1].start()
        for copy in done:
            copy.wait()

    turns = sum(1 for place in places if place[3])
    V, DS = pltpu.VMEM, pltpu.SemaphoreType.DMA
    return pl.pallas_call(
        kernel,
        out_shape=[jax.ShapeDtypeStruct(shape, F32) for shape in shapes]
        + [jax.ShapeDtypeStruct(array.shape, array.dtype) for array in whole]
        + [jax.ShapeDtypeStruct(gains.shape[1:], F32)] * 3,
        in_specs=[HB] * (1 + more) + [VM],
        out_specs=[HB] * (len(shapes) + more) + [VM] * 3,
        scratch_shapes=[
            V((count, blk, inner), LOW), V((count - turns, blk, inner), F32), V((turns, inner, blk), F32),
            DS((count,)), DS((count,)), DS((more,)),
        ],
        compiler_params=pltpu.CompilerParams(vmem_limit_bytes=62 * 1024 * 1024),
        name="spread",
    )(blocks, *whole, gains)


def by_kernels(
    tokens, caption, token_mask, cotangent, gain_self, gain_cross, gain_feed, text_proj,
    query_self, key_self, value_self, out_self, query_cross, key_cross, value_cross, out_cross, up_proj, down_proj,
):
    given = types.SimpleNamespace(
        tokens=tokens, caption=caption, cotangent=cotangent, text_proj=text_proj,
        query_self=query_self, key_self=key_self, value_self=value_self, out_self=out_self,
        query_cross=query_cross, key_cross=key_cross, value_cross=value_cross, out_cross=out_cross,
        up_proj=up_proj, down_proj=down_proj, marks=token_mask[:, :, None].astype(F32),
        gains=[gain_self, gain_cross, gain_feed],
    )
    pairs = lax.axis_size(WIDE) // 2
    kept = forward_all(pairs, 1, given)
    grads, d_words, d_tokens, layer_out, gains = backward_all(pairs, 2, given, kept)
    inner = query_self.shape[1]
    blk = query_self.shape[0] // (2 * pairs)
    ff, text = up_proj.shape[1] // inner, caption.shape[2] // inner
    places = [(10, c * inner, 0, True) for c in range(ff)]
    places += [(9, 0, c * inner, False) for c in range(ff)]
    places += [(8, 0, 0, True), (5, 0, 0, False), (6, 0, 0, False), (7, 0, 0, False)]
    places += [(0, c * inner, 0, True) for c in range(text)]
    places += [(4, 0, 0, True), (1, 0, 0, False), (2, 0, 0, False), (3, 0, 0, False)]
    shapes = [(text * inner, blk)] + [(blk, inner)] * 3 + [(inner, blk)] + [(blk, inner)] * 3 + [(inner, blk)]
    shapes += [(blk, ff * inner), (ff * inner, blk)]
    out = spread(grads, places, shapes, [layer_out, d_tokens, d_words], gains)
    sums, (layer_out, d_tokens, d_words, *gains) = out[: len(shapes)], out[len(shapes) :]
    return (layer_out, d_tokens, d_words.reshape(caption.shape), *gains, *sums)


def local(
    tokens,
    caption,
    token_mask,
    cotangent,
    gain_self,
    gain_cross,
    gain_feed,
    text_proj,
    query_self,
    key_self,
    value_self,
    out_self,
    query_cross,
    key_cross,
    value_cross,
    out_cross,
    up_proj,
    down_proj,
):
    given = (tokens, caption, token_mask, cotangent, gain_self, gain_cross, gain_feed, text_proj, query_self, key_self, value_self, out_self, query_cross, key_cross, value_cross, out_cross, up_proj, down_proj)
    if lax.axis_size(WIDE) != 8 or lax.axis_size(NARROW) != 4:
        return by_collectives(*given)
    return by_kernels(*given)


def solution(mesh):
    in_specs = (
        P(WIDE, NARROW, None),
        P(WIDE, None, NARROW),
        P(WIDE, NARROW),
        P(WIDE, NARROW, None),
        P(),
        P(),
        P(),
        P(NARROW, None),
        P(None, NARROW),
        P(None, NARROW),
        P(None, NARROW),
        P(NARROW, None),
        P(None, NARROW),
        P(None, NARROW),
        P(None, NARROW),
        P(NARROW, None),
        P(None, NARROW),
        P(NARROW, None),
    )
    out_specs = (
        P(WIDE, NARROW, None),
        P(WIDE, NARROW, None),
        P(WIDE, None, NARROW),
        P(),
        P(),
        P(),
        P(NARROW, WIDE),
        P(WIDE, NARROW),
        P(WIDE, NARROW),
        P(WIDE, NARROW),
        P(NARROW, WIDE),
        P(WIDE, NARROW),
        P(WIDE, NARROW),
        P(WIDE, NARROW),
        P(NARROW, WIDE),
        P(WIDE, NARROW),
        P(NARROW, WIDE),
    )
    return jax.shard_map(local, mesh=mesh, in_specs=in_specs, out_specs=out_specs, check_vma=False)
```

time: 1060 us -> 578 us (0.55)
  waiting for transfers between devices: 283 us -> 0 us
  Pallas kernels: 396 us -> 567 us
  matrix products: 148 us -> 0 us
  blocking collectives: 147 us -> 0 us
  other arithmetic: 40 us -> 0.68 us
  local copies, waits for them, and re-layouts: 24.7 us -> 0.74 us
  between operations: 15.3 us -> 1.14 us
    reduce_scatter x6 -> x0, waiting for transfers between devices: 186 us -> none  [own_rows(): return lax.psum_scatter(partial, 'narrow', scatter_dimension=1, tiled=True)]
    pallas_call x1 -> x3, Pallas kernels: 396 us -> 567 us  [the longest x1 396 us: backward_all(): pl.pallas_call(kernel, out_shape=[sds((count, blk, inner), LOW), sds((wor...]
    dot_general x45 -> x0, matrix products: 148 us -> none  [the longest x11 52.1 us: times_weight(): return jnp.dot(left, right, preferred_element_type=jnp.float32)]
    psum x3 -> x0, blocking collectives: 147 us -> none  [the longest x2 104 us: text_total(): return lax.psum(partial, 'narrow')]
    all_gather x6 -> x0, waiting for transfers between devices: 96 us -> none  [group_rows(): return lax.all_gather(piece, 'narrow', axis=1, tiled=True)]
    convert_element_type x24 -> x1, other arithmetic: 27.5 us -> 0.68 us  [by_kernels(): token_mask[:, :, None].astype(F32)]
    unnamed x142 -> x0, local copies, waits for them, and re-layouts: 16.7 us -> none
    reduce_sum x11 -> x0, other arithmetic: 12.5 us -> none  [the longest x3 4.4 us: normalize(): centre = jnp.mean(rows, axis=-1, keepdims=True)]
  transfers between devices with their start and end apart: 12 -> 0, of which waited for: 10 -> 0; matrix products, arithmetic and copies ran while one was open for 9% -> 0% of each run, Pallas kernels for 38% -> 0%
where the time goes in v3:
time: 578 us; the launch traced here: 569 us
  Pallas kernels  567 us (98%)
    pallas_call x1, Pallas kernels, backward_all(): pl.pallas_call(kernel, out_shape=[sds((count, blk, inner), LOW), sds((wor...  396 us
    pallas_call x1, Pallas kernels, forward_all(): pl.pallas_call(kernel, out_shape=list(outs.values()), in_specs=[HB] * len...  120 us
    pallas_call x1, Pallas kernels, spread(): pl.pallas_call(kernel, out_shape=[jax.ShapeDtypeStruct(shape, F32) for sh...  50.6 us

profile of v3, /device:TPU:0, one launch (start us, length us, event | category | flops | bytes accessed | tf_op | source)
XLA Modules:
  0.0 569.4 jit_solution(15146374609749365048)
XLA Ops:
  0.7 0.7 convert_bitcast_fusion
  1.3 0.7 copy.35.refs_14_.refs_35_
  2.1 119.9 %forward_all.1 = (bf16[512,2048]{1,0:T(8,128)(2,1)}, bf16[512,2048]{1,0:T(8,128)(2,1)}, bf16[512,2048]{1,0:T(8,128)(2,1)}, bf16[512,2048]{1,0:T(8,128)(2,1)}, bf...) custom-call(bf16[2,64,2048]{2,1,0:T(8,128)(2,1)} %refs_21_.1, ...), custom_call_target="tpu_custom_call" | custom-call | tf_op jit(solution)/shard_map/forward_all/pallas_call | solution.py:1029
  121.9 396.4 %backward_all.1 = (bf16[18,256,512]{2,1,0:T(8,128)(2,1)}, bf16[256,1024]{1,0:T(8,128)(2,1)}, bf16[2,64,2048]{2,1,0:T(8,128)(2,1)}, bf16[2,64,2048]{2,1,0:T(8,128...) custom-call(bf16[512,2048]{1,0:T(8,128)(2,1)} %get-tuple-element.60.refs_0_, ...), custom_call_target="tpu_custom_call" | custom-call | tf_op jit(solution)/shard_map/backward_all/pallas_call | solution.py:1351
  518.4 50.6 %spread.1 = (f32[1024,256]{1,0:T(8,128)}, f32[256,512]{1,0:T(8,128)}, f32[256,512]{1,0:T(8,128)}, f32[256,512]{1,0:T(8,128)}, f32[512,256]{1,0:T(8,128)}, /*inde...) custom-call(bf16[18,256,512]{2,1,0:T(8,128)(2,1)} %get-tuple-element, ...), custom_call_target="tpu_custom_call" | custom-call | tf_op jit(solution)/shard_map/spread/pallas_call | solution.py:1404

commit v4 on v3

--- a/solution.py
+++ b/solution.py
@@ -225,7 +225,7 @@
 
 
 RING = 6
-HELD = 7
+HELD = 8
 
 
 def send(src, dst, sems, index, peer):
@@ -257,6 +257,7 @@
          self.aslot, self.bslot, self.ysem, self.rsem, self.lsem, self.asem, self.bsem,
          self.osem, self.rfree, self.lfree) = refs
         self.pairs, self.units = pairs, units
+        self.asked, self.released, self.gone = set(), set(), set()
         me = lax.axis_index(WIDE)
         self.z, self.y = me // 2, me % 2
         self.has_right, self.has_left = self.z < pairs - 1, self.z > 0
@@ -322,7 +323,8 @@
     def load(self, i):
         unit = self.units[i]
         if unit.trade:
-            self.trade(i).wait_recv()
+            if not unit.early:
+                self.trade(i).wait_recv()
             if unit.halves is not None and (i == 0 or self.units[i - 1].group != unit.group):
                 unit.halves.arrive()
         for copy in self.loads(i):
@@ -397,40 +399,52 @@
     def sends_left(self, t):
         return self.has_left & (t >= self.pairs - self.z)
 
+    def credit(self, i, free, when):
+        if i >= RING:
+
+            @pl.when(when)
+            def _():
+                pl.semaphore_wait(free, 1)
+
+    def release(self, i):
+        if i in self.released:
+            return
+        self.released.add(i)
+        if not self.units[i].trade:
+            self.y_add(i)
+
+        @pl.when(self.z == 0)
+        def _():
+            if i >= RING:
+                pl.semaphore_wait(self.rfree, 1)
+            for t in range(1, self.pairs):
+                self.r_copy(i, t).start()
+
+        @pl.when(self.z == self.pairs - 1)
+        def _():
+            if i >= RING:
+                pl.semaphore_wait(self.lfree, 1)
+            for t in range(1, self.pairs):
+                self.l_copy(i, t).start()
+
     def step(self, i, t):
         g, r = i % HELD, i % RING
-        if t == 1 and i >= RING:
-
-            @pl.when(self.has_right)
-            def _():
-                pl.semaphore_wait(self.rfree, 1)
-
-            @pl.when(self.has_left)
-            def _():
-                pl.semaphore_wait(self.lfree, 1)
-
-        @pl.when(self.sends_right(t))
+        first_right, first_left = t == self.z + 1, t == self.pairs - self.z
+
+        @pl.when(self.sends_right(t) & self.has_left)
         def _():
-            if t > 1:
-
-                @pl.when(self.has_left & (t - 1 >= self.z))
-                def _():
-                    self.r_copy(i, t - 1).wait_recv()
-                    d = jnp.clip(self.pairs - t + self.z, 0, self.pairs - 1)
-                    self.add(self.mine.at[g, d], self.right.at[r, t - 2])
-
+            self.credit(i, self.rfree, first_right)
+            self.r_copy(i, t - 1).wait_recv()
+            d = jnp.clip(self.pairs - t + self.z, 0, self.pairs - 1)
+            self.add(self.mine.at[g, d], self.right.at[r, t - 2])
             self.r_copy(i, t).start()
 
-        @pl.when(self.sends_left(t))
+        @pl.when(self.sends_left(t) & self.has_right)
         def _():
-            if t > 1:
-
-                @pl.when(self.has_right & (t - 1 >= self.pairs - 1 - self.z))
-                def _():
-                    self.l_copy(i, t - 1).wait_recv()
-                    d = jnp.clip(t - self.pairs + self.z, 0, self.pairs - 1)
-                    self.add(self.mine.at[g, d], self.left.at[r, t - 2])
-
+            self.credit(i, self.lfree, first_left)
+            self.l_copy(i, t - 1).wait_recv()
+            d = jnp.clip(t - self.pairs + self.z, 0, self.pairs - 1)
+            self.add(self.mine.at[g, d], self.left.at[r, t - 2])
             self.l_copy(i, t).start()
 
     def out_copy(self, i):
@@ -479,33 +493,32 @@
             def _():
                 self.l_copy(i, t).wait_send()
 
-    def lead(self, i):
-        return 1 if self.units[i].trade else 2
-
     def ask(self, i):
-        if i < len(self.units) and self.units[i].trade:
+        if i < len(self.units) and self.units[i].trade and not self.units[i].early and i not in self.asked:
+            self.asked.add(i)
             self.trade(i).start()
 
-    def tick(self, k):
+    def move(self, k):
         count, pairs = len(self.units), self.pairs
-        due = [i for i in range(count) if max(j - self.lead(j) for j in range(i + 1)) == k]
-        for i in due[:1]:
-            self.load(i)
-        if k >= 0:
-            self.ask(k + 4)
         for t in range(pairs - 1, 1, -1):
             if 0 <= k - (t - 1) < count:
                 self.step(k - (t - 1), t)
-        if 0 <= k < count:
-            if not self.units[k].trade:
-                self.y_add(k)
-            self.step(k, 1)
         if 0 <= k - (pairs - 1) < count:
             self.final(k - (pairs - 1))
-        for n, i in enumerate(due):
-            if n > 0:
-                self.load(i)
-            self.compute(i)
+        if k + 1 < count and not self.units[k + 1].trade:
+            self.release(k + 1)
+
+    def leave(self, i):
+        if self.units[i].trade and not self.units[i].early and i not in self.gone:
+            self.gone.add(i)
+            self.trade(i).wait_send()
+
+    def multiply(self, i):
+        self.load(i)
+        self.compute(i)
+        if self.units[i].trade:
+            for j in range(i + 1):
+                self.release(j)
 
     def drain(self):
         count = len(self.units)
@@ -516,9 +529,8 @@
         for i in self.summed[-2:]:
             for k in range(self.pairs):
                 self.y_copy(i, k).wait_send()
-        for i, unit in enumerate(self.units):
-            if unit.trade:
-                self.trade(i).wait_send()
+        for i in range(count):
+            self.leave(i)
 
 
 VM = pl.BlockSpec(memory_space=pltpu.VMEM)
@@ -632,38 +644,44 @@
 
 
 class Halves:
-    def __init__(self, full, there, pairs, sems, index):
+    def __init__(self, net, full, there, pairs, sems, index):
         me = lax.axis_index(WIDE)
-        y = me % 2
+        y, rows = me % 2, full.shape[0] // 2
         blk = full.shape[1] // (2 * pairs)
-        peer = {WIDE: me + 1 - 2 * y}
+        span = pl.ds(pl.multiple_of(net.me % 2 * rows, rows), rows)
         self.copies = [
             send(
-                full.at[:, pl.ds(pl.multiple_of((2 * k + 1 - y) * blk, blk), blk)],
-                there.at[:, pl.ds(k * blk, blk)], sems, (index, k), peer,
+                full.at[span, pl.ds(pl.multiple_of((2 * k + 1 - y) * blk, blk), blk)],
+                there.at[span, pl.ds(k * blk, blk)], sems, (index, k), {WIDE: me + 1 - 2 * y},
             )
             for k in range(pairs)
         ]
+        self.onward = send(there.at[span], there.at[span], sems, (index, pairs), net.core)
 
     def start(self):
         for copy in self.copies:
             copy.start()
 
-    def arrive(self):
+    def forward(self):
         for copy in self.copies:
             copy.wait_recv()
+        self.onward.start()
+
+    def arrive(self):
+        self.onward.wait_recv()
 
     def leave(self):
         for copy in self.copies:
             copy.wait_send()
-
-
-def scatter_scratch(images, own, width):
+        self.onward.wait_send()
+
+
+def scatter_scratch(images, own, width, hop=LOW):
     return [
         pltpu.VMEM((images, 4 * own, width), F32),
         pltpu.VMEM((images, 2, own, width), F32),
-        pltpu.VMEM((images, own, width), LOW),
-        pltpu.VMEM((images, own, width), LOW),
+        pltpu.VMEM((images, own, width), hop),
+        pltpu.VMEM((images, own, width), hop),
         pltpu.SemaphoreType.DMA((2, images, 3)),
     ]
 
@@ -777,7 +795,7 @@
         tokens=t.tokens, caption=flat(t.caption), cotangent=t.cotangent, text_proj=t.text_proj,
         query_self=t.query_self, key_self=t.key_self, value_self=t.value_self, out_self=t.out_self,
         query_cross=t.query_cross, key_cross=t.key_cross, value_cross=t.value_cross,
-        out_cross=t.out_cross, up_proj=t.up_proj, down_proj=t.down_proj,
+        out_cross=t.out_cross, up_proj=t.up_proj,
     )
     sds = jax.ShapeDtypeStruct
     outs = dict(
@@ -788,9 +806,9 @@
         query_ca=sds((rows, inner), LOW), keys_ca=sds((word_rows, inner), LOW), values_ca=sds((word_rows, inner), LOW),
         attended_sa=sds((rows, inner), LOW), attended_ca=sds((rows, inner), LOW),
         resid_mid=sds((images, own, width), F32), resid_late=sds((images, own, width), F32),
-        activ=sds((rows, ff), LOW), d_pre=sds((rows, ff), LOW),
-        nb_self=sds((rows, half), LOW), nb_cross=sds((rows, half), LOW), nb_low=sds((rows, half), LOW),
-        nb_context=sds((word_rows, half), LOW),
+        activ=sds((rows, ff), LOW), pre_act=sds((images, length, ff), F32),
+        nb_self=sds((rows, half), LOW), nb_low=sds((rows, half), LOW),
+        nb_context=sds((word_rows, half), LOW), nb_first=sds((rows, inner), LOW),
     )
 
     def kernel(*refs):
@@ -802,8 +820,8 @@
         refs = refs[len(outs):]
         scatter_refs, text_refs = refs[:5], refs[5:10]
         (full_s, full_c, full_f, full_d, full_x, gsem_s, gsem_c, gsem_f, gsem_d, gsem_x,
-         wn, wt, tok, cot, cap, sq, sk, sv, xq, xk, xv, att_s, att_c, mid, late, act, dpre,
-         fsem, osem, hsem) = refs[10:]
+         wn, wt, tok, cot, cap, sq, sk, sv, xq, xk, xv, att_s, att_c, mid, late, act,
+         fsem, osem, hsem, asem) = refs[10:]
         net = Narrow()
         fetch, store = Copies(fsem), Copies(osem)
         barrier = pltpu.get_barrier_semaphore()
@@ -883,7 +901,6 @@
             columns_of(width, step)
             scatter.start(b)
 
-        need_down = {c: band(c, h.down_proj, c) for c in range(text_chunks)}
         gather_s.forward(0)
         text.cross(0)
         text.cross(1)
@@ -907,7 +924,6 @@
             store.later(ref, out)
         for c in range(3):
             need_up[c] = fetch.start(h.up_proj.at[:, pl.ds(c * inner, inner)], wn.at[c])
-        need_down[2] = band(2, h.down_proj, 2)
         for b in range(images):
             text.ready(b)
             mine = gather_x.mine(b)
@@ -919,7 +935,7 @@
         scatter.cross(1)
         for b in range(images):
             gather_x.start(b)
-        halves_self = Halves(full_s, o.nb_self, pairs, hsem, 0)
+        halves_self = Halves(net, full_s, o.nb_self, pairs, hsem, 0)
         halves_self.start()
 
         def rows_out(b, source, target, gain, gather):
@@ -947,15 +963,13 @@
             gather_x.finish(b)
             project(b, full_x, (4, 5), (xk, xv), words)
             text.finish(b)
-        halves_context = Halves(full_x, o.nb_context, pairs, hsem, 1)
+        halves_context = Halves(net, full_x, o.nb_context, pairs, hsem, 1)
         halves_context.start()
         store.later(full_x, o.context)
         store.later(xk, o.keys_ca)
         store.later(xv, o.values_ca)
         need_query_cross.wait()
         gather_c.forward(0)
-        for b in range(images):
-            gather_d.forward(b)
         for b in range(images):
             gather_c.finish(b)
             project(b, full_c, (3,), (xq,))
@@ -967,22 +981,28 @@
                 need_out_cross.wait()
             back_out(b, att_c, 3)
             if b == 0:
+                for j in range(images):
+                    gather_d.forward(j)
                 scatter.cross(b)
+                for j in range(images):
+                    gather_d.finish(j)
+                halves_low = Halves(net, full_d, o.nb_low, pairs, hsem, 2)
+                halves_low.start()
+                store.later(full_d, o.d_image)
         store.later(full_c, o.image_cross)
         store.later(xq, o.query_ca)
         store.later(att_c, o.attended_ca)
-        need_down[3] = band(3, h.down_proj, 3)
-        for b in range(images):
-            gather_d.finish(b)
-        halves_low = Halves(full_d, o.nb_low, pairs, hsem, 2)
-        halves_low.start()
         scatter.cross(1)
-        store.later(full_d, o.d_image)
+        halves_self.forward()
+        halves_context.forward()
         rows_out(0, mid, late, gain_feed, gather_f)
         rows_out(1, mid, late, gain_feed, gather_f)
         store.later(late, o.resid_late)
-        halves_cross = Halves(full_c, o.nb_cross, pairs, hsem, 3)
-        halves_cross.start()
+        halves_low.forward()
+        first = [
+            send(act.at[of(b), pl.ds(0, inner)], o.nb_first.at[of(b)], asem, (b,), {WIDE: me + 1 - 2 * (me % 2)})
+            for b in range(images)
+        ]
         gather_f.forward(0)
         for b in range(images):
             gather_f.finish(b)
@@ -999,23 +1019,21 @@
                     act[pl.ds(pl.multiple_of(b * length + s.start, 16), 16), cols] = gelu(part[b, s, cols]).astype(LOW)
 
                 each_slab(length, step)
+                if c == 0:
+                    first[b].start()
         store.later(act, o.activ)
+        store.later(part, o.pre_act)
         store.later(full_f, o.image_feed)
-        for c in range(chunks):
-            need_down[c].wait()
-            cols = pl.ds(c * inner, inner)
-            for b in range(images):
-                slope = dot(full_d[of(b), :], wt[c], LAST)
-                dpre[of(b), cols] = (gelu_slope(part[b, :, cols]) * slope).astype(LOW)
-            store.later(dpre.at[:, cols], o.d_pre.at[:, cols])
-        for halves in (halves_self, halves_context, halves_low, halves_cross):
+        for halves in (halves_self, halves_context, halves_low):
             halves.arrive()
             halves.leave()
+        for copy in first:
+            copy.wait()
         store.close()
 
     V, DS = pltpu.VMEM, pltpu.SemaphoreType.DMA
     gsem = DS((2, images, 3))
-    scratch = scatter_scratch(images, own, width) + scatter_scratch(images, word_own, width)
+    scratch = scatter_scratch(images, own, width) + scatter_scratch(images, word_own, width, F32)
     scratch += [V((rows, width), LOW)] * 4 + [V((word_rows, width), LOW)] + [gsem] * 5
     scratch += [
         V((7, width, inner), LOW), V((4, inner, width), LOW),
@@ -1023,8 +1041,8 @@
         V((rows, inner), LOW), V((rows, inner), LOW), V((rows, inner), LOW),
         V((rows, inner), LOW), V((word_rows, inner), LOW), V((word_rows, inner), LOW),
         V((rows, inner), LOW), V((rows, inner), LOW),
-        V((images, own, width), F32), V((images, own, width), F32), V((rows, ff), LOW), V((rows, ff), LOW),
-        DS((40,)), DS((40,)), DS((2, 4, pairs)),
+        V((images, own, width), F32), V((images, own, width), F32), V((rows, ff), LOW),
+        DS((40,)), DS((40,)), DS((2, 3, pairs + 1)), DS((2, images)),
     ]
     result = pl.pallas_call(
         kernel,
@@ -1059,8 +1077,8 @@
         h = types.SimpleNamespace(**dict(zip(vars_in, refs)))
         refs = refs[len(vars_in):]
         marks, gain_self, gain_cross, gain_feed = refs[:4]
-        grads_out, words_out, tokens_out, layer_out, gain_out, nb_cols, nb_feed = refs[4:11]
-        refs = refs[11:]
+        grads_out, words_out, tokens_out, layer_out, gain_out, nb_cols, nb_feed, nb_cross = refs[4:12]
+        refs = refs[12:]
         scatter_refs = refs[:5]
         (full_c, full_s, full_x, gsem_c, gsem_s, gsem_x, text_sem,
          big, d_att, wa, wb, xq, xk, xv, sq, sk, sv, cot, late, mid, tok, low_rows, word_grad,
@@ -1068,25 +1086,27 @@
         net = Narrow()
         units = []
 
-        def unit(trade, rows_ref, nb_rows, columns, size, halves=None):
+        def unit(trade, rows_ref, nb_rows, columns, size, halves=None, early=None):
             i = len(units)
+            there = nb_cols.at[i, pl.ds(0, size)] if early is None else early
             units.append(types.SimpleNamespace(
                 trade=trade, rows=rows_ref, nb_rows=nb_rows, columns=columns, count=size, halves=halves,
-                nb_columns=nb_cols.at[i, pl.ds(0, size)], sems=nbsem, out=grads_out.at[i],
+                nb_columns=there, sems=nbsem, out=grads_out.at[i], early=early is not None,
             ))
 
         def chunk(ref, c):
             return ref.at[:, pl.ds(c * inner, inner)]
 
-        halves_feed = Halves(h.image_feed, nb_feed, pairs, hsem, 0)
+        halves_feed = Halves(net, h.image_feed, nb_feed, pairs, hsem, 0)
         for c in range(chunks):
-            unit(True, h.d_image, h.nb_low, chunk(h.activ, c), rows)
+            unit(True, h.d_image, h.nb_low, chunk(h.activ, c), rows, None, h.nb_first if c == 0 else None)
         for c in range(chunks):
-            unit(True, h.image_feed, nb_feed, chunk(h.d_pre, c), rows, halves_feed)
+            unit(True, h.image_feed, nb_feed, chunk(big, c), rows, halves_feed)
         unit(False, full_c, None, h.attended_ca, rows)
-        unit(True, h.image_cross, h.nb_cross, xq, rows)
         unit(True, h.context, h.nb_context, xk, word_rows)
         unit(True, h.context, h.nb_context, xv, word_rows)
+        halves_cross = Halves(net, h.image_cross, nb_cross, pairs, hsem, 1)
+        unit(True, h.image_cross, nb_cross, xq, rows, halves_cross)
         for c in range(text_chunks):
             unit(False, full_x, None, chunk(h.caption, c), word_rows)
         unit(False, full_s, None, h.attended_sa, rows)
@@ -1108,24 +1128,47 @@
         def up_chunk(c):
             return fetch.start(chunk(h.up_proj, c), wa.at[c % 2])
 
+        need_image = fetch.start(h.d_image, full_s)
+
+        def down_chunk(c):
+            return fetch.start(h.down_proj.at[pl.ds(c * inner, inner)], wb.at[c % 2])
+
+        need_down = {c: down_chunk(c) for c in range(2)}
+        need_pre = fetch.start(h.pre_act, scatter_refs[0])
         need_up = {c: up_chunk(c) for c in range(2)}
-        need_pre = fetch.start(h.d_pre, big)
         need_cot = fetch.start(h.cotangent, cot)
         need_late = fetch.start(h.resid_late, late)
-        need_out = fetch.start(h.out_cross, wb)
         need_ca = [fetch.start(a, b) for a, b in ((h.query_ca, xq), (h.keys_ca, xk), (h.values_ca, xv))]
         need_mid = fetch.start(h.resid_mid, mid)
         need_sa = [fetch.start(a, b) for a, b in ((h.query_sa, sq), (h.keys_sa, sk), (h.values_sa, sv))]
         need_tok = fetch.start(h.tokens, tok)
         pl.semaphore_wait(barrier, others)
-        wide.ask(0)
         wide.ask(1)
+        wide.ask(2)
+        wide.multiply(0)
         scatter = Scatter(net, *scatter_refs)
         part = scatter.part
         gather_c, gather_s = Gather(net, full_c, own, gsem_c), Gather(net, full_s, own, gsem_s)
         gather_x = Gather(net, full_x, word_own, gsem_x)
 
+        need_image.wait()
         need_pre.wait()
+        for c in range(chunks):
+            need_down[c].wait()
+            cols = pl.ds(c * inner, inner)
+            for b in range(images):
+                slope = dot(full_s[of(b), :], wb[c % 2], LAST)
+                big[of(b), cols] = (gelu_slope(part[b, :, cols]) * slope).astype(LOW)
+            if c + 2 < chunks:
+                need_down[c + 2] = down_chunk(c + 2)
+            if c == 1:
+                wide.ask(3)
+                halves_feed.start()
+        need_out = fetch.start(h.out_cross, wb.at[0])
+        need_out_self = fetch.start(h.out_self, wb.at[1])
+        wide.multiply(1)
+        wide.ask(4)
+        wide.move(1)
         for c in range(chunks):
             need_up[c].wait()
             for b in range(images):
@@ -1141,7 +1184,6 @@
                 need_up[c + 2] = up_chunk(c + 2)
         need_query = fetch.start(h.query_cross, wa.at[0])
         need_key = fetch.start(h.key_cross, wa.at[1])
-        halves_feed.start()
         gacc[...] = jnp.zeros_like(gacc)
 
         def back_rows(b, above, mask, source, gain, slot, keep, mine):
@@ -1174,48 +1216,60 @@
 
             columns_of(width, step)
 
-        def out_back(b, full):
-            d_att[of(b), :] = dot(full[of(b), :], wb[...], LAST).astype(LOW)
-
-        wide.tick(-1)
+        def out_back(b, full, j):
+            d_att[of(b), :] = dot(full[of(b), :], wb[j], LAST).astype(LOW)
+
+        wide.multiply(2)
+        wide.ask(5)
+        wide.move(2)
         for b in range(images):
             scatter.cross(b)
-        wide.tick(0)
+        wide.multiply(3)
+        wide.ask(6)
         need_cot.wait()
         need_late.wait()
         for b in range(images):
             back_rows(b, cot, marks, late, gain_feed, 2, late, gather_c.mine(b))
             gather_c.start(b)
-        wide.ask(2)
-        wide.ask(3)
+        wide.move(3)
         for b in range(images):
             gather_c.forward(b)
-        wide.tick(1)
+        halves_feed.forward()
+        wide.multiply(4)
+        wide.ask(7)
         need_out.wait()
         for b in range(images):
             scatter.finish(b)
             gather_c.finish(b)
-            out_back(b, full_c)
-        need_out = fetch.start(h.out_self, wb)
+            out_back(b, full_c, 0)
+        need_text = fetch.start(h.text_proj.at[pl.ds(0, inner)], wb.at[0])
+        wide.move(4)
         for need in need_ca:
             need.wait()
         heads_back(images, xq, xk, xv, d_att)
-        wide.tick(2)
         need_query.wait()
         for b in range(images):
             multiply(b, part, [xq], [0])
             scatter.start(b)
         need_value = fetch.start(h.value_cross, wa.at[0])
+        wide.multiply(5)
         for b in range(images):
             scatter.cross(b)
+        wide.multiply(6)
+        wide.move(5)
         need_mid.wait()
         for b in range(images):
             back_rows(b, late, None, mid, gain_cross, 1, mid, gather_s.mine(b))
             gather_s.start(b)
-        wide.tick(3)
         need_again = fetch.start(h.resid_late, late)
+        wide.multiply(7)
+        wide.multiply(8)
+        wide.ask(9)
+        wide.ask(10)
+        halves_cross.start()
         for b in range(images):
             gather_s.forward(b)
+        wide.move(6)
         for b in range(images):
             scatter.finish(b)
             gather_s.finish(b)
@@ -1229,16 +1283,16 @@
             multiply(b, text.part, [xk, xv], [1, 0], words)
             text.start(b)
         need_qkv = [fetch.start(h.query_self, wa.at[0]), fetch.start(h.key_self, wa.at[1])]
-        need_out.wait()
-        for b in range(images):
-            out_back(b, full_s)
-        need_text = fetch.start(h.text_proj.at[pl.ds(0, inner)], wb)
-        wide.tick(4)
+        need_out_self.wait()
+        for b in range(images):
+            out_back(b, full_s, 1)
+        need_second = fetch.start(h.text_proj.at[pl.ds(inner, inner)], wb.at[1])
         for b in range(images):
             text.cross(b)
         for need in need_sa:
             need.wait()
         heads_back(images, sq, sk, sv, d_att)
+        wide.move(7)
         for b in range(images):
             text.ready(b)
             mine = gather_x.mine(b)
@@ -1250,23 +1304,27 @@
             gather_x.start(b)
         for b in range(images):
             gather_x.forward(b)
-        wide.tick(5)
+        wide.multiply(9)
+        wide.ask(11)
         for b in range(images):
             text.finish(b)
             gather_x.finish(b)
-        for c in range(text_chunks):
-            need_text.wait()
-            word_grad[:, pl.ds(c * inner, inner)] = dot(full_x[...], wb[...], LAST).astype(LOW)
-            if c + 1 < text_chunks:
-                need_text = fetch.start(h.text_proj.at[pl.ds((c + 1) * inner, inner)], wb)
+        for c, need in enumerate((need_text, need_second)):
+            need.wait()
+            word_grad[:, pl.ds(c * inner, inner)] = dot(full_x[...], wb[c], LAST).astype(LOW)
         store.later(word_grad, words_out)
-        need_down = fetch.start(h.down_proj.at[pl.ds(0, inner)], wb)
+        need_down = {c: down_chunk(c) for c in range(2)}
+        wide.move(8)
         for need in need_qkv:
             need.wait()
         for b in range(images):
             multiply(b, part, [sq, sk], [0, 1])
         need_value = fetch.start(h.value_self, wa.at[0])
+        for c in range(chunks):
+            wide.leave(chunks + c)
         need_act = fetch.start(h.activ, big)
+        wide.multiply(10)
+        halves_cross.forward()
         need_value.wait()
         for b in range(images):
 
@@ -1275,41 +1333,54 @@
 
             columns_of(width, step)
             scatter.start(b)
-        wide.tick(6)
+        wide.multiply(11)
+        wide.move(9)
         for b in range(images):
             scatter.cross(b)
+        wide.multiply(12)
+        wide.move(10)
         need_tok.wait()
         for b in range(images):
             back_rows(b, mid, None, tok, gain_self, 0, None, low_rows.at[b])
         store.later(low_rows, tokens_out)
         for b in range(images):
             scatter.finish(b)
-        wide.tick(7)
+        wide.multiply(13)
+        wide.ask(15)
+        wide.move(11)
         for j, peer in enumerate((net.core, net.chip, wide.peer, near, far)):
             trip = send(gacc, gland.at[j], gsems, (j,), peer)
             trip.start()
             trip.wait()
             gacc[...] = gacc[...] + gland[j]
         store.later(gacc, gain_out)
-        wide.tick(8)
+        wide.multiply(14)
+        wide.ask(16)
+        wide.move(12)
         need_act.wait()
         for c in range(chunks):
-            need_down.wait()
+            need_down[c].wait()
             for b in range(images):
 
                 def step(cols, b=b, c=c):
-                    term = dot(big[of(b), pl.ds(c * inner, inner)], wb[:, cols])
+                    term = dot(big[of(b), pl.ds(c * inner, inner)], wb[c % 2, :, cols])
                     part[b, :, cols] = term if c == 0 else part[b, :, cols] + term
 
                 columns_of(width, step)
-            if c + 1 < chunks:
-                need_down = fetch.start(h.down_proj.at[pl.ds((c + 1) * inner, inner)], wb)
+            if c + 2 < chunks:
+                need_down[c + 2] = down_chunk(c + 2)
+            if c == 1:
+                wide.multiply(15)
+                wide.ask(17)
+                wide.move(13)
         for b in range(images):
             scatter.start(b)
-        wide.tick(9)
+        wide.multiply(16)
+        wide.move(14)
         for b in range(images):
             scatter.cross(b)
-        wide.tick(10)
+        wide.multiply(17)
+        wide.move(15)
         need_again.wait()
         for b in range(images):
             scatter.ready(b)
@@ -1320,10 +1391,11 @@
             each_slab(own, step)
             scatter.finish(b)
         store.later(tok, layer_out)
-        for k in range(11, count + pairs - 1):
-            wide.tick(k)
+        for k in range(16, count + pairs - 1):
+            wide.move(k)
         wide.drain()
         halves_feed.leave()
+        halves_cross.leave()
         store.close()
 
     V, DS = pltpu.VMEM, pltpu.SemaphoreType.DMA
@@ -1332,12 +1404,12 @@
     scratch = scatter_scratch(images, own, width)
     scratch += [V((rows, width), LOW), V((rows, width), LOW), V((word_rows, width), LOW)] + [gsem] * 4
     scratch += [
-        V((rows, ff), LOW), V((rows, inner), LOW), V((2, width, inner), LOW), V((inner, width), LOW),
+        V((rows, ff), LOW), V((rows, inner), LOW), V((2, width, inner), LOW), V((2, inner, width), LOW),
         V((rows, inner), LOW), V((word_rows, inner), LOW), V((word_rows, inner), LOW),
         V((rows, inner), LOW), V((rows, inner), LOW), V((rows, inner), LOW),
         V((images, own, width), LOW), V((images, own, width), F32), V((images, own, width), F32),
         V((images, own, width), LOW), V((images, own, width), LOW), V((word_rows, states), LOW),
-        DS((40,)), DS((8,)), DS((2, count)), DS((2, 1, pairs)), V((8, width), F32), V((5, 8, width), F32), DS((2, 5)),
+        DS((48,)), DS((8,)), DS((2, count)), DS((2, 2, pairs + 1)), V((8, width), F32), V((5, 8, width), F32), DS((2, 5)),
     ]
     scratch += [
         V((HELD, pairs, blk, inner), LOW), V((2, pairs, blk, inner), LOW), V((sums, pairs, blk, inner), LOW),
@@ -1353,9 +1425,10 @@
         out_shape=[
             sds((count, blk, inner), LOW), sds((word_rows, states), LOW), sds((images, own, width), LOW),
             sds((images, own, width), LOW), sds((8, width), F32), sds((count, rows, inner), LOW), sds((rows, half), LOW),
+            sds((rows, half), LOW),
         ],
         in_specs=[HB] * len(vars_in) + [VM] * 4,
-        out_specs=[HB] * 7,
+        out_specs=[HB] * 8,
         scratch_shapes=scratch,
         compiler_params=params(number, 62),
         name="backward_all",
@@ -1373,14 +1446,14 @@
         gains_out, refs = refs[:3], refs[3:]
         for j, row in enumerate(gains_out):
             row[...] = gains_ref[j, :]
-        held, flat_stage, turned_stage, isem, osem, wsem = refs
+        held, flat_stage, turned_stage, isem, osem, wsem, *kept = refs
         ins = [pltpu.make_async_copy(blocks_ref.at[i], held.at[i], isem.at[i]) for i in range(count)]
         for copy in ins:
             copy.start()
         done, plain, turns = [], 0, 0
-        for j in range(more):
-            done.append(pltpu.make_async_copy(whole_in[j], whole_out[j], wsem.at[j]))
-            done[-1].start()
+        came = [pltpu.make_async_copy(whole_in[j], kept[j], wsem.at[0, j]) for j in range(more)]
+        for copy in came:
+            copy.start()
         for i, (which, row, col, turned) in enumerate(places):
             ins[i].wait()
             if turned:
@@ -1396,6 +1469,10 @@
                 place = outs[which].at[pl.ds(row, blk), pl.ds(col, inner)]
             done.append(pltpu.make_async_copy(stage, place, osem.at[i]))
             done[-1].start()
+        for j in range(more):
+            came[j].wait()
+            done.append(pltpu.make_async_copy(kept[j], whole_out[j], wsem.at[1, j]))
+            done[-1].start()
         for copy in done:
             copy.wait()
 
@@ -1410,8 +1487,8 @@
         out_specs=[HB] * (len(shapes) + more) + [VM] * 3,
         scratch_shapes=[
             V((count, blk, inner), LOW), V((count - turns, blk, inner), F32), V((turns, inner, blk), F32),
-            DS((count,)), DS((count,)), DS((more,)),
-        ],
+            DS((count,)), DS((count,)), DS((2, more)),
+        ] + [V(array.shape, array.dtype) for array in whole],
         compiler_params=pltpu.CompilerParams(vmem_limit_bytes=62 * 1024 * 1024),
         name="spread",
     )(blocks, *whole, gains)
@@ -1436,7 +1513,7 @@
     ff, text = up_proj.shape[1] // inner, caption.shape[2] // inner
     places = [(10, c * inner, 0, True) for c in range(ff)]
     places += [(9, 0, c * inner, False) for c in range(ff)]
-    places += [(8, 0, 0, True), (5, 0, 0, False), (6, 0, 0, False), (7, 0, 0, False)]
+    places += [(8, 0, 0, True), (6, 0, 0, False), (7, 0, 0, False), (5, 0, 0, False)]
     places += [(0, c * inner, 0, True) for c in range(text)]
     places += [(4, 0, 0, True), (1, 0, 0, False), (2, 0, 0, False), (3, 0, 0, False)]
     shapes = [(text * inner, blk)] + [(blk, inner)] * 3 + [(inner, blk)] + [(blk, inner)] * 3 + [(inner, blk)]

time: 578 us -> 473 us (0.82)
  Pallas kernels: 567 us -> 462 us
    pallas_call x1, Pallas kernels: 396 us -> 343 us  [backward_all(): pl.pallas_call(kernel, out_shape=[sds((count, blk, inner), LOW), sds((wor...]
    pallas_call x1, Pallas kernels: 50.6 us -> 7.3 us  [spread(): pl.pallas_call(kernel, out_shape=[jax.ShapeDtypeStruct(shape, F32) for sh...]
    pallas_call x1, Pallas kernels: 120 us -> 112 us  [forward_all(): pl.pallas_call(kernel, out_shape=list(outs.values()), in_specs=[HB] * len...]
where the time goes in v4:
time: 473 us; the launch traced here: 464 us
  Pallas kernels  462 us (98%)
    pallas_call x1, Pallas kernels, backward_all(): pl.pallas_call(kernel, out_shape=[sds((count, blk, inner), LOW), sds((wor...  343 us
    pallas_call x1, Pallas kernels, forward_all(): pl.pallas_call(kernel, out_shape=list(outs.values()), in_specs=[HB] * len...  112 us

profile of v4, /device:TPU:0, one launch (start us, length us, event | category | flops | bytes accessed | tf_op | source)
XLA Modules:
  0.0 464.2 jit_solution(6045111856704975888)
XLA Ops:
  0.7 0.7 convert_bitcast_fusion
  1.3 0.7 copy.35.refs_13_.refs_35_
  2.1 111.5 %forward_all.1 = (bf16[512,2048]{1,0:T(8,128)(2,1)}, bf16[512,2048]{1,0:T(8,128)(2,1)}, bf16[512,2048]{1,0:T(8,128)(2,1)}, bf16[512,2048]{1,0:T(8,128)(2,1)}, bf...) custom-call(bf16[2,64,2048]{2,1,0:T(8,128)(2,1)} %refs_21_.1, ...), custom_call_target="tpu_custom_call" | custom-call | tf_op jit(solution)/shard_map/forward_all/pallas_call | solution.py:1047
  113.6 342.9 %backward_all.1 = (bf16[18,256,512]{2,1,0:T(8,128)(2,1)}, bf16[256,1024]{1,0:T(8,128)(2,1)}, bf16[2,64,2048]{2,1,0:T(8,128)(2,1)}, bf16[2,64,2048]{2,1,0:T(8,128...) custom-call(bf16[512,2048]{1,0:T(8,128)(2,1)} %get-tuple-element.60., ...), custom_call_target="tpu_custom_call" | custom-call | tf_op jit(solution)/shard_map/backward_all/pallas_call | solution.py:1423
  456.5 7.3 %spread.1 = (f32[1024,256]{1,0:T(8,128)}, f32[256,512]{1,0:T(8,128)}, f32[256,512]{1,0:T(8,128)}, f32[256,512]{1,0:T(8,128)}, f32[512,256]{1,0:T(8,128)}, /*inde...) custom-call(bf16[18,256,512]{2,1,0:T(8,128)(2,1)} %get-tuple-element, ...), custom_call_target="tpu_custom_call" | custom-call | tf_op jit(solution)/shard_map/spread/pallas_call | solution.py:1481

commit v5 on v4

--- a/solution.py
+++ b/solution.py
@@ -253,18 +253,16 @@
 
 class Wide:
     def __init__(self, pairs, units, refs):
-        (self.mine, self.theirs, self.fromy, self.right, self.left, self.stage,
-         self.aslot, self.bslot, self.ysem, self.rsem, self.lsem, self.asem, self.bsem,
-         self.osem, self.rfree, self.lfree) = refs
+        (self.mine, self.right, self.left, self.stage, self.aslot, self.bslot, self.rsem, self.lsem, self.asem,
+         self.bsem, self.osem, self.rfree, self.lfree) = refs
         self.pairs, self.units = pairs, units
-        self.asked, self.released, self.gone = set(), set(), set()
+        self.asked, self.gone = set(), set()
         me = lax.axis_index(WIDE)
         self.z, self.y = me // 2, me % 2
         self.has_right, self.has_left = self.z < pairs - 1, self.z > 0
         self.peer = {WIDE: self.z * 2 + 1 - self.y}
         self.next = {WIDE: jnp.minimum(self.z + 1, pairs - 1) * 2 + self.y}
         self.last = {WIDE: jnp.maximum(self.z - 1, 0) * 2 + self.y}
-        self.summed = [i for i, unit in enumerate(units) if not unit.trade]
         group = -1
         for i, unit in enumerate(units):
             if i == 0 or unit.rows is not units[i - 1].rows:
@@ -295,44 +293,29 @@
         copies = []
         if i == 0 or self.units[i - 1].group != unit.group:
             for k in range(self.pairs):
-                for part in (0, 1):
-                    if part == 0 or not unit.trade:
-                        at = (k * 2 + (self.y if part == 0 else 1 - self.y)) * self.blk
-                        src = unit.rows.at[:, pl.ds(pl.multiple_of(at, self.blk), self.blk)]
-                    else:
-                        src = unit.nb_rows.at[:, pl.ds(k * self.blk, self.blk)]
+                at = pl.multiple_of((k * 2 + self.y) * self.blk, self.blk)
+                sources = (unit.rows.at[:, pl.ds(at, self.blk)], unit.nb_rows.at[:, pl.ds(k * self.blk, self.blk)])
+                for part, src in enumerate(sources):
                     copies.append(
                         pltpu.make_async_copy(
                             src, self.aslot.at[s, part, k, pl.ds(0, rows)], self.asem.at[s, part, k]
                         )
                     )
         q = i % 2
-        copies.append(
-            pltpu.make_async_copy(
-                unit.columns, self.bslot.at[q, 0, pl.ds(0, rows)], self.bsem.at[q, 0]
-            )
-        )
-        if unit.trade:
+        for part, src in enumerate((unit.columns, unit.nb_columns)):
             copies.append(
-                pltpu.make_async_copy(
-                    unit.nb_columns, self.bslot.at[q, 1, pl.ds(0, rows)], self.bsem.at[q, 1]
-                )
+                pltpu.make_async_copy(src, self.bslot.at[q, part, pl.ds(0, rows)], self.bsem.at[q, part])
             )
         return copies
 
     def load(self, i):
         unit = self.units[i]
-        if unit.trade:
-            if not unit.early:
-                self.trade(i).wait_recv()
-            if unit.halves is not None and (i == 0 or self.units[i - 1].group != unit.group):
-                unit.halves.arrive()
+        if not unit.early:
+            self.trade(i).wait_recv()
+        if unit.halves is not None and (i == 0 or self.units[i - 1].group != unit.group):
+            unit.halves.arrive()
         for copy in self.loads(i):
             copy.start()
-
-    def y_copy(self, i, k):
-        n = self.summed.index(i)
-        return send(self.theirs.at[n % 2, k], self.fromy.at[n, k], self.ysem, (n, k), self.peer)
 
     def compute(self, i):
         unit = self.units[i]
@@ -341,37 +324,18 @@
             copy.wait()
         if i >= HELD:
             self.sent(i - HELD)
-        if not unit.trade:
-            n = self.summed.index(i)
-            if n >= 2:
-                for k in range(self.pairs):
-                    self.y_copy(self.summed[n - 2], k).wait_send()
-
-            def far(k, carry):
-                self.theirs[n % 2, k] = lax.dot_general(
-                    self.aslot[s, 1, k, :rows], self.bslot[q, 0, :rows], FIRST,
-                    preferred_element_type=F32,
-                ).astype(LOW)
-                return carry
-
-            lax.fori_loop(0, self.pairs, far, 0)
-            for k in range(self.pairs):
-                self.y_copy(i, k).start()
-
-        def near(k, carry):
-            total = lax.dot_general(
-                self.aslot[s, 0, k, :rows], self.bslot[q, 0, :rows], FIRST,
-                preferred_element_type=F32,
-            )
-            if unit.trade:
-                total = total + lax.dot_general(
-                    self.aslot[s, 1, k, :rows], self.bslot[q, 1, :rows], FIRST,
-                    preferred_element_type=F32,
+
+        def body(k, carry):
+            total = None
+            for part in (0, 1):
+                term = lax.dot_general(
+                    self.aslot[s, part, k, :rows], self.bslot[q, part, :rows], FIRST, preferred_element_type=F32
                 )
+                total = term if total is None else total + term
             self.mine[g, k] = total.astype(LOW)
             return carry
 
-        lax.fori_loop(0, self.pairs, near, 0)
+        lax.fori_loop(0, self.pairs, body, 0)
 
     def add(self, dst, src):
         def step(s):
@@ -379,12 +343,6 @@
 
         each_slab(self.blk, step, 64)
 
-    def y_add(self, i):
-        n = self.summed.index(i)
-        for k in range(self.pairs):
-            self.y_copy(i, k).wait_recv()
-            self.add(self.mine.at[i % HELD, k], self.fromy.at[n, k])
-
     def r_copy(self, i, t):
         d = jnp.clip(self.pairs - t + self.z, 0, self.pairs - 1)
         return send(self.mine.at[i % HELD, d], self.right.at[i % RING, t - 1], self.rsem, (i, t - 1), self.next)
@@ -407,12 +365,6 @@
                 pl.semaphore_wait(free, 1)
 
     def release(self, i):
-        if i in self.released:
-            return
-        self.released.add(i)
-        if not self.units[i].trade:
-            self.y_add(i)
-
         @pl.when(self.z == 0)
         def _():
             if i >= RING:
@@ -494,7 +446,7 @@
                 self.l_copy(i, t).wait_send()
 
     def ask(self, i):
-        if i < len(self.units) and self.units[i].trade and not self.units[i].early and i not in self.asked:
+        if i < len(self.units) and not self.units[i].early and i not in self.asked:
             self.asked.add(i)
             self.trade(i).start()
 
@@ -505,20 +457,17 @@
                 self.step(k - (t - 1), t)
         if 0 <= k - (pairs - 1) < count:
             self.final(k - (pairs - 1))
-        if k + 1 < count and not self.units[k + 1].trade:
-            self.release(k + 1)
 
     def leave(self, i):
-        if self.units[i].trade and not self.units[i].early and i not in self.gone:
+        if not self.units[i].early and i not in self.gone:
             self.gone.add(i)
             self.trade(i).wait_send()
 
-    def multiply(self, i):
-        self.load(i)
+    def multiply(self, i, loaded=False):
+        if not loaded:
+            self.load(i)
         self.compute(i)
-        if self.units[i].trade:
-            for j in range(i + 1):
-                self.release(j)
+        self.release(i)
 
     def drain(self):
         count = len(self.units)
@@ -526,9 +475,6 @@
             self.out_copy(i).wait()
         for i in range(max(0, count - HELD), count):
             self.sent(i)
-        for i in self.summed[-2:]:
-            for k in range(self.pairs):
-                self.y_copy(i, k).wait_send()
         for i in range(count):
             self.leave(i)
 
@@ -808,7 +754,8 @@
         resid_mid=sds((images, own, width), F32), resid_late=sds((images, own, width), F32),
         activ=sds((rows, ff), LOW), pre_act=sds((images, length, ff), F32),
         nb_self=sds((rows, half), LOW), nb_low=sds((rows, half), LOW),
-        nb_context=sds((word_rows, half), LOW), nb_first=sds((rows, inner), LOW),
+        nb_context=sds((word_rows, half), LOW), nb_first=sds((rows, inner), LOW), nb_caption=sds((word_rows, states), LOW),
+        nb_att_sa=sds((rows, inner), LOW), nb_att_ca=sds((rows, inner), LOW),
     )
 
     def kernel(*refs):
@@ -826,7 +773,8 @@
         fetch, store = Copies(fsem), Copies(osem)
         barrier = pltpu.get_barrier_semaphore()
         me = lax.axis_index(WIDE)
-        greet(barrier, {WIDE: me + 1 - 2 * (me % 2)})
+        pair = {WIDE: me + 1 - 2 * (me % 2)}
+        greet(barrier, pair)
         others = net.meet(barrier) + 1
 
         def whole(j, ref):
@@ -868,6 +816,8 @@
             each_slab(own, step)
             gather_s.start(b)
         need_cap.wait()
+        first = [send(cap, o.nb_caption, asem, (images,), pair)]
+        first[0].start()
         for need in need_proj:
             need.wait()
         for b in range(images):
@@ -937,6 +887,8 @@
             gather_x.start(b)
         halves_self = Halves(net, full_s, o.nb_self, pairs, hsem, 0)
         halves_self.start()
+        first.append(send(att_s, o.nb_att_sa, asem, (images + 1,), pair))
+        first[-1].start()
 
         def rows_out(b, source, target, gain, gather):
             scatter.ready(b)
@@ -989,6 +941,8 @@
                 halves_low = Halves(net, full_d, o.nb_low, pairs, hsem, 2)
                 halves_low.start()
                 store.later(full_d, o.d_image)
+        first.append(send(att_c, o.nb_att_ca, asem, (images + 2,), pair))
+        first[-1].start()
         store.later(full_c, o.image_cross)
         store.later(xq, o.query_ca)
         store.later(att_c, o.attended_ca)
@@ -999,9 +953,8 @@
         rows_out(1, mid, late, gain_feed, gather_f)
         store.later(late, o.resid_late)
         halves_low.forward()
-        first = [
-            send(act.at[of(b), pl.ds(0, inner)], o.nb_first.at[of(b)], asem, (b,), {WIDE: me + 1 - 2 * (me % 2)})
-            for b in range(images)
+        first += [
+            send(act.at[of(b), pl.ds(0, inner)], o.nb_first.at[of(b)], asem, (b,), pair) for b in range(images)
         ]
         gather_f.forward(0)
         for b in range(images):
@@ -1020,7 +973,7 @@
 
                 each_slab(length, step)
                 if c == 0:
-                    first[b].start()
+                    first[3 + b].start()
         store.later(act, o.activ)
         store.later(part, o.pre_act)
         store.later(full_f, o.image_feed)
@@ -1042,7 +995,7 @@
         V((rows, inner), LOW), V((word_rows, inner), LOW), V((word_rows, inner), LOW),
         V((rows, inner), LOW), V((rows, inner), LOW),
         V((images, own, width), F32), V((images, own, width), F32), V((rows, ff), LOW),
-        DS((40,)), DS((40,)), DS((2, 3, pairs + 1)), DS((2, images)),
+        DS((40,)), DS((40,)), DS((2, 3, pairs + 1)), DS((2, images + 3)),
     ]
     result = pl.pallas_call(
         kernel,
@@ -1077,8 +1030,8 @@
         h = types.SimpleNamespace(**dict(zip(vars_in, refs)))
         refs = refs[len(vars_in):]
         marks, gain_self, gain_cross, gain_feed = refs[:4]
-        grads_out, words_out, tokens_out, layer_out, gain_out, nb_cols, nb_feed, nb_cross = refs[4:12]
-        refs = refs[12:]
+        grads_out, words_out, tokens_out, layer_out, gain_out, nb_cols, nb_feed, nb_cross, nb_late, nb_mid, nb_words = refs[4:15]
+        refs = refs[15:]
         scatter_refs = refs[:5]
         (full_c, full_s, full_x, gsem_c, gsem_s, gsem_x, text_sem,
          big, d_att, wa, wb, xq, xk, xv, sq, sk, sv, cot, late, mid, tok, low_rows, word_grad,
@@ -1086,11 +1039,11 @@
         net = Narrow()
         units = []
 
-        def unit(trade, rows_ref, nb_rows, columns, size, halves=None, early=None):
+        def unit(rows_ref, nb_rows, columns, size, halves=None, early=None):
             i = len(units)
             there = nb_cols.at[i, pl.ds(0, size)] if early is None else early
             units.append(types.SimpleNamespace(
-                trade=trade, rows=rows_ref, nb_rows=nb_rows, columns=columns, count=size, halves=halves,
+                rows=rows_ref, nb_rows=nb_rows, columns=columns, count=size, halves=halves,
                 nb_columns=there, sems=nbsem, out=grads_out.at[i], early=early is not None,
             ))
 
@@ -1098,21 +1051,23 @@
             return ref.at[:, pl.ds(c * inner, inner)]
 
         halves_feed = Halves(net, h.image_feed, nb_feed, pairs, hsem, 0)
+        halves_cross = Halves(net, h.image_cross, nb_cross, pairs, hsem, 1)
+        halves_late = Halves(net, full_c, nb_late, pairs, hsem, 2)
+        halves_mid = Halves(net, full_s, nb_mid, pairs, hsem, 3)
+        halves_words = Halves(net, full_x, nb_words, pairs, hsem, 4)
         for c in range(chunks):
-            unit(True, h.d_image, h.nb_low, chunk(h.activ, c), rows, None, h.nb_first if c == 0 else None)
+            unit(h.d_image, h.nb_low, chunk(h.activ, c), rows, None, h.nb_first if c == 0 else None)
         for c in range(chunks):
-            unit(True, h.image_feed, nb_feed, chunk(big, c), rows, halves_feed)
-        unit(False, full_c, None, h.attended_ca, rows)
-        unit(True, h.context, h.nb_context, xk, word_rows)
-        unit(True, h.context, h.nb_context, xv, word_rows)
-        halves_cross = Halves(net, h.image_cross, nb_cross, pairs, hsem, 1)
-        unit(True, h.image_cross, nb_cross, xq, rows, halves_cross)
+            unit(h.image_feed, nb_feed, chunk(big, c), rows, halves_feed)
+        unit(full_c, nb_late, h.attended_ca, rows, halves_late, h.nb_att_ca)
+        unit(h.context, h.nb_context, xk, word_rows)
+        unit(h.context, h.nb_context, xv, word_rows)
+        unit(h.image_cross, nb_cross, xq, rows, halves_cross)
         for c in range(text_chunks):
-            unit(False, full_x, None, chunk(h.caption, c), word_rows)
-        unit(False, full_s, None, h.attended_sa, rows)
-        unit(True, h.image_self, h.nb_self, sq, rows)
-        unit(True, h.image_self, h.nb_self, sk, rows)
-        unit(True, h.image_self, h.nb_self, sv, rows)
+            unit(full_x, nb_words, chunk(h.caption, c), word_rows, halves_words, chunk(h.nb_caption, c))
+        unit(full_s, nb_mid, h.attended_sa, rows, halves_mid, h.nb_att_sa)
+        for column in (sq, sk, sv):
+            unit(h.image_self, h.nb_self, column, rows)
         wide = Wide(pairs, units, refs[35:])
         fetch, store = Copies(fsem), Copies(osem)
 
@@ -1128,6 +1083,7 @@
         def up_chunk(c):
             return fetch.start(chunk(h.up_proj, c), wa.at[c % 2])
 
+        wide.load(0)
         need_image = fetch.start(h.d_image, full_s)
 
         def down_chunk(c):
@@ -1145,7 +1101,7 @@
         pl.semaphore_wait(barrier, others)
         wide.ask(1)
         wide.ask(2)
-        wide.multiply(0)
+        wide.multiply(0, True)
         scatter = Scatter(net, *scatter_refs)
         part = scatter.part
         gather_c, gather_s = Gather(net, full_c, own, gsem_c), Gather(net, full_s, own, gsem_s)
@@ -1232,9 +1188,9 @@
             back_rows(b, cot, marks, late, gain_feed, 2, late, gather_c.mine(b))
             gather_c.start(b)
         wide.move(3)
+        halves_feed.forward()
         for b in range(images):
             gather_c.forward(b)
-        halves_feed.forward()
         wide.multiply(4)
         wide.ask(7)
         need_out.wait()
@@ -1242,20 +1198,25 @@
             scatter.finish(b)
             gather_c.finish(b)
             out_back(b, full_c, 0)
+        halves_late.start()
         need_text = fetch.start(h.text_proj.at[pl.ds(0, inner)], wb.at[0])
         wide.move(4)
+        wide.multiply(5)
         for need in need_ca:
             need.wait()
         heads_back(images, xq, xk, xv, d_att)
+        wide.ask(9)
+        wide.ask(10)
+        halves_cross.start()
         need_query.wait()
         for b in range(images):
             multiply(b, part, [xq], [0])
             scatter.start(b)
         need_value = fetch.start(h.value_cross, wa.at[0])
-        wide.multiply(5)
+        wide.multiply(6)
+        wide.ask(11)
         for b in range(images):
             scatter.cross(b)
-        wide.multiply(6)
         wide.move(5)
         need_mid.wait()
         for b in range(images):
@@ -1263,16 +1224,15 @@
             gather_s.start(b)
         need_again = fetch.start(h.resid_late, late)
         wide.multiply(7)
+        halves_late.forward()
+        wide.move(6)
+        for b in range(images):
+            gather_s.forward(b)
         wide.multiply(8)
-        wide.ask(9)
-        wide.ask(10)
-        halves_cross.start()
-        for b in range(images):
-            gather_s.forward(b)
-        wide.move(6)
         for b in range(images):
             scatter.finish(b)
             gather_s.finish(b)
+        halves_mid.start()
         text = Scatter(
             net, part.at[:, pl.ds(0, words)], scatter.landed.at[:, :, pl.ds(0, word_own)],
             scatter.outgoing.at[:, pl.ds(0, word_own)], scatter.arrived.at[:, pl.ds(0, word_own)], text_sem,
@@ -1287,12 +1247,13 @@
         for b in range(images):
             out_back(b, full_s, 1)
         need_second = fetch.start(h.text_proj.at[pl.ds(inner, inner)], wb.at[1])
+        wide.move(7)
         for b in range(images):
             text.cross(b)
+        wide.multiply(9)
         for need in need_sa:
             need.wait()
         heads_back(images, sq, sk, sv, d_att)
-        wide.move(7)
         for b in range(images):
             text.ready(b)
             mine = gather_x.mine(b)
@@ -1302,29 +1263,30 @@
 
             each_slab(word_own, step)
             gather_x.start(b)
+        wide.multiply(10)
+        halves_cross.forward()
+        wide.move(8)
         for b in range(images):
             gather_x.forward(b)
-        wide.multiply(9)
-        wide.ask(11)
         for b in range(images):
             text.finish(b)
             gather_x.finish(b)
+        halves_words.start()
         for c, need in enumerate((need_text, need_second)):
             need.wait()
             word_grad[:, pl.ds(c * inner, inner)] = dot(full_x[...], wb[c], LAST).astype(LOW)
         store.later(word_grad, words_out)
         need_down = {c: down_chunk(c) for c in range(2)}
-        wide.move(8)
         for need in need_qkv:
             need.wait()
         for b in range(images):
             multiply(b, part, [sq, sk], [0, 1])
         need_value = fetch.start(h.value_self, wa.at[0])
+        wide.multiply(11)
         for c in range(chunks):
             wide.leave(chunks + c)
         need_act = fetch.start(h.activ, big)
-        wide.multiply(10)
-        halves_cross.forward()
+        wide.move(9)
         need_value.wait()
         for b in range(images):
 
@@ -1333,11 +1295,10 @@
 
             columns_of(width, step)
             scatter.start(b)
-        wide.multiply(11)
-        wide.move(9)
+        halves_words.forward()
+        wide.multiply(12)
         for b in range(images):
             scatter.cross(b)
-        wide.multiply(12)
         wide.move(10)
         need_tok.wait()
         for b in range(images):
@@ -1345,42 +1306,60 @@
         store.later(low_rows, tokens_out)
         for b in range(images):
             scatter.finish(b)
+        wide.ask(15)
+        halves_mid.forward()
         wide.multiply(13)
-        wide.ask(15)
         wide.move(11)
-        for j, peer in enumerate((net.core, net.chip, wide.peer, near, far)):
-            trip = send(gacc, gland.at[j], gsems, (j,), peer)
-            trip.start()
-            trip.wait()
-            gacc[...] = gacc[...] + gland[j]
-        store.later(gacc, gain_out)
-        wide.multiply(14)
-        wide.ask(16)
-        wide.move(12)
-        need_act.wait()
-        for c in range(chunks):
+        trips = [
+            send(gacc, gland.at[j], gsems, (j,), peer)
+            for j, peer in enumerate((net.core, net.chip, wide.peer, near, far))
+        ]
+
+        def trip(j):
+            if j > 0:
+                trips[j - 1].wait()
+                gacc[...] = gacc[...] + gland[j - 1]
+            if j < len(trips):
+                trips[j].start()
+
+        def forward_chunk(c):
             need_down[c].wait()
             for b in range(images):
 
-                def step(cols, b=b, c=c):
+                def step(cols, b=b):
                     term = dot(big[of(b), pl.ds(c * inner, inner)], wb[c % 2, :, cols])
                     part[b, :, cols] = term if c == 0 else part[b, :, cols] + term
 
                 columns_of(width, step)
             if c + 2 < chunks:
                 need_down[c + 2] = down_chunk(c + 2)
-            if c == 1:
-                wide.multiply(15)
-                wide.ask(17)
-                wide.move(13)
-        for b in range(images):
-            scatter.start(b)
+
+        trip(0)
+        wide.multiply(14)
+        wide.ask(16)
+        trip(1)
+        wide.move(12)
+        trip(2)
+        wide.multiply(15)
+        wide.ask(17)
+        trip(3)
+        wide.move(13)
         wide.multiply(16)
+        need_act.wait()
+        forward_chunk(0)
         wide.move(14)
-        for b in range(images):
-            scatter.cross(b)
+        forward_chunk(1)
         wide.multiply(17)
         wide.move(15)
+        for c in range(2, chunks):
+            forward_chunk(c)
+        for b in range(images):
+            scatter.start(b)
+        wide.move(16)
+        for b in range(images):
+            scatter.cross(b)
+        trip(4)
+        wide.move(17)
         need_again.wait()
         for b in range(images):
             scatter.ready(b)
@@ -1391,16 +1370,17 @@
             each_slab(own, step)
             scatter.finish(b)
         store.later(tok, layer_out)
-        for k in range(16, count + pairs - 1):
+        for k in range(18, count + pairs - 1):
             wide.move(k)
+        trip(5)
+        store.later(gacc, gain_out)
         wide.drain()
-        halves_feed.leave()
-        halves_cross.leave()
+        for halves in (halves_feed, halves_cross, halves_late, halves_mid, halves_words):
+            halves.leave()
         store.close()
 
     V, DS = pltpu.VMEM, pltpu.SemaphoreType.DMA
     gsem = DS((2, images, 3))
-    sums = 2 + text_chunks
     scratch = scatter_scratch(images, own, width)
     scratch += [V((rows, width), LOW), V((rows, width), LOW), V((word_rows, width), LOW)] + [gsem] * 4
     scratch += [
@@ -1409,13 +1389,13 @@
         V((rows, inner), LOW), V((rows, inner), LOW), V((rows, inner), LOW),
         V((images, own, width), LOW), V((images, own, width), F32), V((images, own, width), F32),
         V((images, own, width), LOW), V((images, own, width), LOW), V((word_rows, states), LOW),
-        DS((48,)), DS((8,)), DS((2, count)), DS((2, 2, pairs + 1)), V((8, width), F32), V((5, 8, width), F32), DS((2, 5)),
+        DS((48,)), DS((8,)), DS((2, count)), DS((2, 5, pairs + 1)), V((8, width), F32), V((5, 8, width), F32), DS((2, 5)),
     ]
     scratch += [
-        V((HELD, pairs, blk, inner), LOW), V((2, pairs, blk, inner), LOW), V((sums, pairs, blk, inner), LOW),
+        V((HELD, pairs, blk, inner), LOW),
         V((RING, pairs - 1, blk, inner), LOW), V((RING, pairs - 1, blk, inner), LOW), V((2, blk, inner), LOW),
         V((2, 2, pairs, rows, blk), LOW), V((2, 2, rows, inner), LOW),
-        DS((2, sums, pairs)), DS((2, count, pairs - 1)), DS((2, count, pairs - 1)),
+        DS((2, count, pairs - 1)), DS((2, count, pairs - 1)),
         DS((2, 2, pairs)), DS((2, 2)), DS((2,)),
         pltpu.SemaphoreType.REGULAR, pltpu.SemaphoreType.REGULAR,
     ]
@@ -1425,10 +1405,10 @@
         out_shape=[
             sds((count, blk, inner), LOW), sds((word_rows, states), LOW), sds((images, own, width), LOW),
             sds((images, own, width), LOW), sds((8, width), F32), sds((count, rows, inner), LOW), sds((rows, half), LOW),
-            sds((rows, half), LOW),
+            sds((rows, half), LOW), sds((rows, half), LOW), sds((rows, half), LOW), sds((word_rows, half), LOW),
         ],
         in_specs=[HB] * len(vars_in) + [VM] * 4,
-        out_specs=[HB] * 8,
+        out_specs=[HB] * 11,
         scratch_shapes=scratch,
         compiler_params=params(number, 62),
         name="backward_all",

time: 473 us -> 456 us (0.964)
  Pallas kernels: 462 us -> 445 us
    pallas_call x1, Pallas kernels: 343 us -> 325 us  [backward_all(): pl.pallas_call(kernel, out_shape=[sds((count, blk, inner), LOW), sds((wor...]
where the time goes in v5:
time: 456 us; the launch traced here: 447 us
  Pallas kernels  445 us (98%)
    pallas_call x1, Pallas kernels, backward_all(): pl.pallas_call(kernel, out_shape=[sds((count, blk, inner), LOW), sds((wor...  325 us
    pallas_call x1, Pallas kernels, forward_all(): pl.pallas_call(kernel, out_shape=list(outs.values()), in_specs=[HB] * len...  113 us

profile of v5, /device:TPU:0, one launch (start us, length us, event | category | flops | bytes accessed | tf_op | source)
XLA Modules:
  0.0 447.4 jit_solution(15336194285187392639)
XLA Ops:
  0.7 0.7 convert_bitcast_fusion
  1.3 0.7 copy.35.refs_13_.refs_38_
  2.1 112.7 %forward_all.1 = (bf16[512,2048]{1,0:T(8,128)(2,1)}, bf16[512,2048]{1,0:T(8,128)(2,1)}, bf16[512,2048]{1,0:T(8,128)(2,1)}, bf16[512,2048]{1,0:T(8,128)(2,1)}, bf...) custom-call(bf16[2,64,2048]{2,1,0:T(8,128)(2,1)} %refs_24_.1, ...), custom_call_target="tpu_custom_call" | custom-call | tf_op jit(solution)/shard_map/forward_all/pallas_call | solution.py:1000
  114.8 324.8 %backward_all.1 = (bf16[18,256,512]{2,1,0:T(8,128)(2,1)}, bf16[256,1024]{1,0:T(8,128)(2,1)}, bf16[2,64,2048]{2,1,0:T(8,128)(2,1)}, bf16[2,64,2048]{2,1,0:T(8,128...) custom-call(bf16[512,2048]{1,0:T(8,128)(2,1)} %get-tuple-element.63., ...), custom_call_target="tpu_custom_call" | custom-call | tf_op jit(solution)/shard_map/backward_all/pallas_call | solution.py:1403
  439.6 7.3 %spread.1 = (f32[1024,256]{1,0:T(8,128)}, f32[256,512]{1,0:T(8,128)}, f32[256,512]{1,0:T(8,128)}, f32[256,512]{1,0:T(8,128)}, f32[512,256]{1,0:T(8,128)}, /*inde...) custom-call(bf16[18,256,512]{2,1,0:T(8,128)(2,1)} %get-tuple-element, ...), custom_call_target="tpu_custom_call" | custom-call | tf_op jit(solution)/shard_map/spread/pallas_call | solution.py:1461
